TPU v7x, 32 devices: a whole 2x2x4 slice. The times are simulated.
32 devices in a mesh: rows: 8 (over z, y), seq: 4 (over x, core).
Axes of the slice: x: 2, y: 2, z: 4, core: 2. Of those that a mesh axis runs over, the one named last changes fastest.
Arguments:
- inputs: bfloat16 [32, 1024, 768], P('rows', 'seq'), may hold values from -6 to 6
- segment_ids: int32 [32, 1024], P('rows'), may hold values from 0 to 3, as said below
- gain_one: float32 [768], replicated, may hold values from 0.1 to 1.9
- w_query: bfloat16 [768, 768], replicated, may hold values from -0.4375 to 0.4375
- w_key: bfloat16 [768, 768], replicated, may hold values from -0.21875 to 0.21875
- w_value: bfloat16 [768, 768], replicated, may hold values from -0.21875 to 0.21875
- w_out: bfloat16 [768, 768], replicated, may hold values from -0.875 to 0.875
- mix_logits: bfloat16 [12, 12], replicated, may hold values from -1.75 to 1.75
- mix_weights: bfloat16 [12, 12], replicated, may hold values from -1.75 to 1.75
- gain_two: float32 [768], replicated, may hold values from 0.1 to 1.9
- w_hidden: bfloat16 [768, 3072], replicated, may hold values from -0.21875 to 0.21875
- w_back: bfloat16 [3072, 768], replicated, may hold values from -0.15625 to 0.15625
- cotangent: bfloat16 [32, 1024, 768], P('rows', 'seq'), may hold values from -6 to 6
Outputs:
- block_out: bfloat16 [32, 1024, 768], P('rows', 'seq')
- grad_inputs: bfloat16 [32, 1024, 768], P('rows', 'seq')
- grad_gain_one: float32 [768], replicated
- grad_w_query: float32 [768, 768], replicated
- grad_w_key: float32 [768, 768], replicated
- grad_w_value: float32 [768, 768], replicated
- grad_w_out: float32 [768, 768], replicated
- grad_mix_logits: float32 [12, 12], replicated
- grad_mix_weights: float32 [12, 12], replicated
- grad_gain_two: float32 [768], replicated
- grad_w_hidden: float32 [768, 3072], replicated
- grad_w_back: float32 [3072, 768], replicated
Inputs may be any that keep to these rules, and one draw needn't show every extreme that they name: `segment_ids`: in each row the ids never fall and name four documents 0, 1, 2, 3, each nonempty; document 2 starts before token 256, and document 3 starts at token 3 * (256) or later.
All inputs are finite; a program needn't handle non-finite values.
Results may differ from a plain program's by a relative error of at most 0.017.
The roundings to bfloat16 on the way count: a program that leaves them out, or rounds other values in their place, can miss the bound.
Values may be sent and summed in bfloat16 or wider, within the bound.
No kernel may reach another device: no remote copies, remote signals or barrier semaphores. Data moves between devices by JAX's collectives and lax.ppermute only.
A program may use at most 320 MiB of HBM per device.

v0:
```python
from functools import partial

from jax import lax
import jax
import jax.numpy as jnp
from jax.experimental import pallas as pl
from jax.experimental.pallas import tpu as pltpu
from jax.sharding import PartitionSpec as P

D, H, DH, LEN, TILE = 768, 12, 64, 1024, 256
TILES = LEN // TILE
F32, BF16 = jnp.float32, jnp.bfloat16
FORWARD_HEADS, BACKWARD_HEADS = 4, 2
VMEM_LIMIT = 60 * 1024 * 1024
MATMUL_FLOPS = 2 * H * 10 * TILE * TILE * D


def span(i):
    return slice(i * TILE, (i + 1) * TILE)


def head_rows(h):
    return slice(h * DH, (h + 1) * DH)


def mm(a, b):
    return jnp.dot(a, b, preferred_element_type=F32)


def whole(shape):
    return pl.BlockSpec(shape, lambda i: (0,) * len(shape), pipeline_mode=pl.Buffered(1))


def some_heads(count, shape):
    return pl.BlockSpec((count,) + shape, lambda i: (i,) + (0,) * len(shape))


SMEM = pl.BlockSpec(memory_space=pltpu.SMEM)


def params():
    return pltpu.CompilerParams(dimension_semantics=("arbitrary",), vmem_limit_bytes=VMEM_LIMIT)


def shape(s, t=BF16):
    return jax.ShapeDtypeStruct(s, t)


def attend_kernel(mix_l, mix_w, id_row, id_col, q_t, k, v_t, soft, out, bias, scaled, acc):
    step = pl.program_id(0)

    @pl.when(step == 0)
    def start():
        acc[...] = jnp.zeros_like(acc)
        for t in range(TILES):
            for u in range(t + 1):
                allowed = id_col[span(u), :] == id_row[:, span(t)]
                if u == t:
                    key = lax.broadcasted_iota(jnp.int32, (TILE, TILE), 0)
                    query = lax.broadcasted_iota(jnp.int32, (TILE, TILE), 1)
                    allowed = allowed & (key <= query)
                bias[span(u), span(t)] = jnp.where(allowed, 0.0, -1e30)

    for i in range(FORWARD_HEADS):
        j = step * FORWARD_HEADS + i
        for h in range(H):
            scaled[i, head_rows(h), :] = (q_t[head_rows(h), :].astype(F32) * mix_l[h, j]).astype(BF16)
        for t in reversed(range(TILES)):
            n = (t + 1) * TILE
            logits = mm(k[:n, :], scaled[i, :, span(t)]) + bias[:n, span(t)]
            e = jnp.exp(logits - jnp.max(logits, axis=0, keepdims=True))
            p = (e * (1.0 / jnp.sum(e, axis=0, keepdims=True))).astype(BF16)
            soft[i, :n, span(t)] = p
            part = mm(v_t[:, :n], p)
            for h in range(H):
                acc[head_rows(h), span(t)] += part[head_rows(h), :] * mix_w[j, h]

    @pl.when(step == H // FORWARD_HEADS - 1)
    def finish():
        for t in range(TILES):
            out[span(t), :] = acc[:, span(t)].T.astype(BF16)


def attend(mix_l, mix_w, ids, q_t, k, v_t):
    heads = FORWARD_HEADS
    return pl.pallas_call(
        attend_kernel,
        grid=(H // heads,),
        in_specs=[SMEM, SMEM, whole((1, LEN)), whole((LEN, 1)), whole((D, LEN)), whole((LEN, D)), whole((D, LEN))],
        out_specs=[some_heads(heads, (LEN, LEN)), whole((LEN, D))],
        out_shape=[shape((H, LEN, LEN)), shape((LEN, D))],
        scratch_shapes=[
            pltpu.VMEM((LEN, LEN), F32), pltpu.VMEM((heads, D, LEN), BF16), pltpu.VMEM((D, LEN), F32)
        ],
        compiler_params=params(),
        cost_estimate=pl.CostEstimate(flops=MATMUL_FLOPS // 4, bytes_accessed=LEN * LEN, transcendentals=0),
        name="attend",
    )(mix_l, mix_w, ids.reshape(1, LEN), ids.reshape(LEN, 1), q_t, k, v_t)


def head_row(weight_of):
    head = lax.broadcasted_iota(jnp.int32, (1, D), 1) // DH
    row = jnp.full((1, D), weight_of(0), F32)
    for h in range(1, H):
        row = jnp.where(head == h, weight_of(h), row)
    return row


def value_grads_kernel(mix_w, soft, v, g, *rest):
    out, mix_grad, acc = rest[-3:]
    step = pl.program_id(0)

    @pl.when(step == 0)
    def start():
        acc[...] = jnp.zeros_like(acc)

    for i in range(BACKWARD_HEADS):
        total = jnp.zeros((1, D), F32)
        mix_row = head_row(lambda h: mix_w[step * BACKWARD_HEADS + i, h])
        for u in range(TILES):
            part = mm(soft[i, span(u), u * TILE :], g[u * TILE :, :])
            acc[span(u), :] += part * mix_row
            total = total + jnp.sum(part * v[span(u), :].astype(F32), axis=0, keepdims=True)
        mix_grad[i] = total

    @pl.when(step == H // BACKWARD_HEADS - 1)
    def finish():
        out[...] = acc[...].astype(BF16)


def query_grads_kernel(heads, mix_w, mix_l, soft, v, g_t, k_t, q_t, *rest):
    before, (out, grad_logits, mix_grad, acc, scaled) = rest[0], rest[-5:]
    step = pl.program_id(0)
    first_head = heads[0] + step * BACKWARD_HEADS

    @pl.when(step == 0)
    def start():
        acc[...] = before[...] if heads[0] else jnp.zeros_like(acc)

    for i in range(BACKWARD_HEADS):
        j = first_head + i
        for h in range(H):
            scaled[i, head_rows(h), :] = (g_t[head_rows(h), :].astype(F32) * mix_w[j, h]).astype(BF16)
    order = [(i, t) for i in range(BACKWARD_HEADS) for t in reversed(range(TILES))]

    def grad_soft(i, t):
        return mm(v[: (t + 1) * TILE, :], scaled[i, :, span(t)])

    coming = grad_soft(*order[0])
    total = jnp.zeros((D, 128), F32)
    for at, (i, t) in enumerate(order):
        n = (t + 1) * TILE
        p = soft[i, :n, span(t)].astype(F32)
        weighted = p * coming
        low = (weighted - p * jnp.sum(weighted, axis=0, keepdims=True)).astype(BF16)
        grad_logits[i, :n, span(t)] = low
        if at + 1 < len(order):
            coming = grad_soft(*order[at + 1])
        part = mm(k_t[:, :n], low)
        for h in range(H):
            acc[head_rows(h), span(t)] += part[head_rows(h), :] * mix_l[h, first_head + i]
        product = part * q_t[:, span(t)].astype(F32)
        total = total + product[:, :128] + product[:, 128:]
        if t == 0:
            mix_grad[i] = jnp.sum(total.T, axis=0, keepdims=True)
            total = jnp.zeros((D, 128), F32)

    @pl.when(step == pl.num_programs(0) - 1)
    def finish():
        if heads[1] < H:
            out[...] = acc[...]
        else:
            for t in range(TILES):
                out[span(t), :] = acc[:, span(t)].T.astype(BF16)


def key_grads_kernel(mix_l, grad_logits, q, *rest):
    out, acc = rest[-2:]
    step = pl.program_id(0)

    @pl.when(step == 0)
    def start():
        acc[...] = jnp.zeros_like(acc)

    for i in range(BACKWARD_HEADS):
        mix_row = head_row(lambda h: mix_l[h, step * BACKWARD_HEADS + i])
        for u in range(TILES):
            acc[span(u), :] += mm(grad_logits[i, span(u), u * TILE :], q[u * TILE :, :]) * mix_row

    @pl.when(step == H // BACKWARD_HEADS - 1)
    def finish():
        out[...] = acc[...].astype(BF16)


def back_call(kernel, heads, in_specs, out_specs, out_shape, scratch, matmuls, name):
    def run(*operands):
        *used, first = operands
        return pl.pallas_call(
            kernel,
            grid=(heads // BACKWARD_HEADS,),
            in_specs=in_specs + [pl.BlockSpec(memory_space=pl.ANY)] * len(first),
            out_specs=out_specs,
            out_shape=out_shape,
            scratch_shapes=scratch,
            compiler_params=params(),
            cost_estimate=pl.CostEstimate(
                flops=matmuls * MATMUL_FLOPS * heads // H // 8, bytes_accessed=LEN * LEN, transcendentals=0
            ),
            name=name,
        )(*used, *first)

    return run


ROW, COLUMN = whole((LEN, D)), whole((D, LEN))
PER_HEAD, PER_HEAD_ROW = some_heads(BACKWARD_HEADS, (LEN, LEN)), some_heads(BACKWARD_HEADS, (1, D))


def value_grads(mix_w, soft, v, g, first):
    grads, mix_grad = back_call(
        value_grads_kernel,
        H,
        [SMEM, PER_HEAD, ROW, ROW],
        [ROW, PER_HEAD_ROW],
        [shape((LEN, D)), shape((H, 1, D), F32)],
        [pltpu.VMEM((LEN, D), F32)],
        1,
        "value_grads",
    )(mix_w, soft, v, g, first)
    return grads, mix_grad


def query_grads(mix_w, mix_l, soft, v, g_t, k_t, q_t, first, heads=(0, H), before=()):
    low, high = heads
    count, last = high - low, high == H
    per_head = pl.BlockSpec((BACKWARD_HEADS, LEN, LEN), lambda i: (i + low // BACKWARD_HEADS, 0, 0))
    grads, grad_logits, mix_grad = back_call(
        partial(query_grads_kernel, heads),
        count,
        [SMEM, SMEM, per_head, ROW, COLUMN, COLUMN, COLUMN] + [COLUMN] * len(before),
        [ROW if last else COLUMN, PER_HEAD, PER_HEAD_ROW],
        [shape((LEN, D)) if last else shape((D, LEN), F32), shape((count, LEN, LEN)), shape((count, 1, D), F32)],
        [pltpu.VMEM((D, LEN), F32), pltpu.VMEM((BACKWARD_HEADS, D, LEN), BF16)],
        2,
        "query_grads",
    )(mix_w, mix_l, soft, v, g_t, k_t, q_t, *before, first)
    return grads, grad_logits, mix_grad


def key_grads(mix_l, grad_logits, q, first):
    return back_call(
        key_grads_kernel, H, [SMEM, PER_HEAD, ROW], ROW, shape((LEN, D)), [pltpu.VMEM((LEN, D), F32)], 1,
        "key_grads",
    )(mix_l, grad_logits, q, first)


epsilon = 1e-06
GELU_SCALE = 0.7978845608028654
GELU_CUBIC = 0.044715
FEED_COLUMNS = 1024
COST_SHARE = 4
HALF = D // 2
ANY = pl.BlockSpec(memory_space=pl.ANY)
VMEM = pl.BlockSpec(memory_space=pltpu.VMEM)


def against(left, right):
    return lax.dot_general(left, right, (((1,), (1,)), ((), ())), preferred_element_type=F32)


def across(left, right):
    return lax.dot_general(left, right, (((0,), (0,)), ((), ())), preferred_element_type=F32)


def inverse_rms(values):
    return lax.rsqrt(jnp.mean(values * values, axis=-1, keepdims=True) + epsilon)


def cost(matrices):
    return pl.CostEstimate(flops=int(matrices * LEN * D * D) // COST_SHARE, bytes_accessed=LEN * D, transcendentals=0)


def fixed(s):
    return pl.BlockSpec(s, lambda i, at: (0,) * len(s), pipeline_mode=pl.Buffered(1))


def tokens(rows, shift=0):
    return pl.BlockSpec((rows, D), lambda i, at: (at[0] ^ (i + shift), 0))


def tokens_t(columns, shift=0):
    return pl.BlockSpec((D, columns), lambda i, at: (0, at[0] ^ (i + shift)))


def step_call(kernel, at, steps, in_specs, operands, out_specs, out_shape, matrices, name, scratch=(), aliases=None):
    return pl.pallas_call(
        kernel,
        grid_spec=pltpu.PrefetchScalarGridSpec(
            num_scalar_prefetch=1, grid=(steps,), in_specs=in_specs, out_specs=out_specs, scratch_shapes=list(scratch)),
        out_shape=out_shape,
        input_output_aliases=aliases or {},
        compiler_params=params(),
        cost_estimate=cost(matrices),
        name=name,
    )(at, *operands)


def chosen(refs, step):
    values = refs[0][...]
    for i, ref in enumerate(refs[1:]):
        values = jnp.where(step == i + 1, ref[...], values)
    return values


def write_parts(outs, step, values):
    for i, out in enumerate(outs[:-1]):

        @pl.when(step == i)
        def write():
            out[...] = values

    far = outs[-1].shape[0]
    for i in range(far):

        @pl.when(step == len(outs) - 1 + i)
        def write_far():
            outs[-1][i] = values


def part_outs(parts, rows):
    near = parts // 2
    specs = [fixed((rows, D))] * near + [fixed((parts - near, rows, D))]
    return specs, [shape((rows, D))] * near + [shape((parts - near, rows, D))]


def project_kernel(steps, waits, shares, at, *refs):
    parts, (gain, w_query, w_key, w_value) = refs[:steps], refs[steps : steps + 4]
    rest = refs[steps + 4 + waits :]
    cotangent, rest = (rest[0], rest[1:]) if shares else (None, rest)
    row, normed_t, q, q_t, k, k_t, v, v_t = rest[:8]
    step = pl.program_id(0)
    low = chosen(parts, step)
    row[...] = low
    values = low.astype(F32)
    normed = (values * inverse_rms(values) * gain[...]).astype(BF16)
    normed_t[...] = normed.T
    for weight, out, out_t in ((w_query, q, q_t), (w_key, k, k_t), (w_value, v, v_t)):
        part = mm(normed, weight[...]).astype(BF16)
        out[...] = part
        out_t[...] = part.T
    if shares:

        @pl.when(step == 0)
        def lay_out():
            for i, out in enumerate(rest[8:]):
                out[...] = cotangent[at[0] ^ i]


def project(at, parts, shift, gain, w_query, w_key, w_value, before=(), cotangent=None):
    count, rows = len(parts), parts[0].shape[0]
    square, ways = fixed((D, D)), 0 if cotangent is None else cotangent.shape[0]
    row, column = (tokens(rows, shift), shape((LEN, D))), (tokens_t(rows, shift), shape((D, LEN)))
    outs = [row, column, row, column, row, column, row, column] + [(fixed((rows, D)), shape((rows, D)))] * ways
    start = 1 + count + 4
    return step_call(
        partial(project_kernel, count, len(before), ways > 0), at, count,
        [fixed((rows, D))] * count + [fixed((1, D)), square, square, square] + [ANY] * len(before)
        + [fixed((ways, rows, D))] * (ways > 0),
        (*parts, gain, w_query, w_key, w_value, *before) + ((cotangent,) if ways else ()),
        [o[0] for o in outs], [o[1] for o in outs], 3 * count / 4, "project",
        aliases={start + i: i for i in range(len(before))})


def feed_kernel(parts, at, x, attended, *refs):
    cots, (w_out, w_hidden, w_back, gain), rest = refs[:parts], refs[parts : parts + 4], refs[parts + 4 :]
    outs, (cot_row, normed_two, activated, grad_hidden, grad_middle, grad_attn, g, g_t) = rest[:-8], rest[-8:]
    step = pl.program_id(0)
    scale = gain[...]
    cotangent = chosen(cots, step)
    cot_row[...] = cotangent
    middle = x[...].astype(F32) + mm(attended[...], w_out[...])
    inverse = inverse_rms(middle)
    n2 = (middle * inverse * scale).astype(BF16)
    normed_two[...] = n2
    total = middle
    grad_n2 = jnp.zeros_like(middle)
    width = FEED_COLUMNS
    for c in range(w_hidden.shape[1] // width):
        cols = slice(c * width, (c + 1) * width)
        hidden = mm(n2, w_hidden[:, cols])
        grad_act = against(cotangent, w_back[cols, :])
        squared = hidden * hidden
        tanh = jnp.tanh(GELU_SCALE * hidden * (1.0 + GELU_CUBIC * squared))
        half = 0.5 + 0.5 * tanh
        act = (hidden * half).astype(BF16)
        activated[:, cols] = act
        slope = half + (0.5 * GELU_SCALE) * hidden * (1.0 - tanh * tanh) * (1.0 + 3.0 * GELU_CUBIC * squared)
        grad = (grad_act * slope).astype(BF16)
        grad_hidden[:, cols] = grad
        total = total + mm(act, w_back[cols, :])
        grad_n2 = grad_n2 + against(grad, w_hidden[:, cols])
    low = total.astype(BF16)
    write_parts(outs, step, low)
    weighted = grad_n2 * scale
    mean = jnp.mean(weighted * middle, axis=-1, keepdims=True)
    grad_mid = cotangent.astype(F32) + inverse * weighted - middle * (inverse * inverse * inverse * mean)
    grad_middle[...] = grad_mid
    grad_low = grad_mid.astype(BF16)
    grad_attn[...] = grad_low
    grad = against(grad_low, w_out[...]).astype(BF16)
    g[...] = grad
    g_t[...] = grad.T


def feed(at, x, attended, cots, w_out, w_hidden, w_back, gain):
    ff, parts, rows = w_hidden.shape[1], len(cots), cots[0].shape[0]
    tile = (tokens(rows), shape((LEN, D)))
    wide = (pl.BlockSpec((rows, ff), lambda i, at: (at[0] ^ i, 0)), shape((LEN, ff)))
    outs = list(zip(*part_outs(parts, rows))) + [
        tile, tile, wide, wide, (tokens(rows), shape((LEN, D), F32)), tile, tile, (tokens_t(rows), shape((D, LEN)))]
    found = step_call(
        partial(feed_kernel, parts), at, parts,
        [tokens(rows), tokens(rows)] + [fixed((rows, D))] * parts
        + [fixed((D, D)), fixed((D, ff)), fixed((ff, D)), fixed((1, D))],
        (x, attended, *cots, w_out, w_hidden, w_back, gain), [o[0] for o in outs], [o[1] for o in outs],
        2 + 4 * ff // D, "feed")
    return found[:-8], found[-8:]


def input_kernel(parts, at, grad_q, grad_k, grad_v, x, grad_middle, w_query, w_key, w_value, gain, first, *outs):
    upstream = against(grad_q[...], w_query[...]) + against(grad_k[...], w_key[...]) + against(grad_v[...], w_value[...])
    values = x[...].astype(F32)
    inverse = inverse_rms(values)
    weighted = upstream * gain[...]
    mean = jnp.mean(weighted * values, axis=-1, keepdims=True)
    low = (grad_middle[...] + inverse * weighted - values * (inverse * inverse * inverse * mean)).astype(BF16)
    write_parts(outs, pl.program_id(0), low)


def input_grads(at, parts, grad_q, grad_k, grad_v, x, grad_middle, w_query, w_key, w_value, gain, first):
    rows, square = LEN // parts, fixed((D, D))
    return step_call(
        partial(input_kernel, parts), at, parts, [tokens(rows)] * 5 + [square, square, square, fixed((1, D)), ANY],
        (grad_q, grad_k, grad_v, x, grad_middle, w_query, w_key, w_value, gain, first),
        *part_outs(parts, rows), 3, "input_grads")


def both_halves(kept, sent, product, left_kept, left_sent, right):
    kept[0, :HALF] = product(left_kept[...], right[...]).astype(BF16)
    sent[0, :HALF] = product(left_sent[...], right[...]).astype(BF16)


def wide_kernel(backs, core, act_kept, act_sent, cot, n2_kept, n2_sent, grad_hidden, kept, sent):
    step = pl.program_id(0)
    pl.when(step < backs)(partial(both_halves, kept, sent, across, act_kept, act_sent, cot))
    pl.when(step >= backs)(partial(both_halves, kept, sent, across, n2_kept, n2_sent, grad_hidden))


def thin_kernel(hiddens, core, n2_kept, n2_sent, grad_hidden, att_kept, att_sent, grad_attn, *refs):
    step, (kept, sent) = pl.program_id(0), refs[-2:]
    pl.when(step < hiddens)(partial(both_halves, kept, sent, across, n2_kept, n2_sent, grad_hidden))
    pl.when(step >= hiddens)(partial(both_halves, kept, sent, across, att_kept, att_sent, grad_attn))


def columns_half(other, at=lambda i: 0):
    return pl.BlockSpec((LEN, HALF), lambda i, core: (0, 2 * at(i) + (core[0] ^ other)))


def rows_half(other):
    return pl.BlockSpec((HALF, LEN), lambda i, core: (core[0] ^ other, 0))


def wide_and_thin(blocks):
    count = 2 * blocks + 1
    return 2 * count // 3, count - 2 * count // 3


def wide_weight_grads(core, activated, cot, normed_two, grad_hidden):
    blocks = activated.shape[1] // D
    count, _ = wide_and_thin(blocks)
    row, half = fixed((LEN, D)), pl.BlockSpec((1, HALF, D), lambda i, core: (i, 0, 0))

    def back(i):
        return jnp.minimum(i, blocks - 1)

    return step_call(
        partial(wide_kernel, blocks), core, count,
        [columns_half(0, back), columns_half(1, back), row, columns_half(0), columns_half(1),
         pl.BlockSpec((LEN, D), lambda i, core: (0, jnp.maximum(i - blocks, 0)))],
        (activated, activated, cot, normed_two, normed_two, grad_hidden),
        [half, half], [shape((count, HALF, D))] * 2, count, "wide_weight_grads")


def thin_weight_grads(core, normed_two, grad_hidden, attended, grad_attn, first):
    blocks = grad_hidden.shape[1] // D
    count, left = wide_and_thin(blocks)
    row, half = fixed((LEN, D)), pl.BlockSpec((1, HALF, D), lambda i, core: (i, 0, 0))
    return step_call(
        partial(thin_kernel, left - 1), core, left,
        [columns_half(0), columns_half(1),
         pl.BlockSpec((LEN, D), lambda i, core: (0, jnp.minimum(i + count - blocks, blocks - 1))),
         columns_half(0), columns_half(1), row] + [ANY] * len(first),
        (normed_two, normed_two, grad_hidden, attended, attended, grad_attn, *first),
        [half, half], [shape((left, HALF, D))] * 2, left, "thin_weight_grads")


SMALL_ROWS = 8


def small_sums(by_logits, by_weights):
    rows = jnp.concatenate([by_logits[:, 0, :], by_weights[:, 0, :]])
    head = lax.broadcasted_iota(jnp.int32, (D, 128), 0) // DH
    select = (head == lax.broadcasted_iota(jnp.int32, (D, 128), 1)).astype(F32)
    sums = jnp.dot(rows, select, precision=lax.Precision.HIGHEST, preferred_element_type=F32)
    groups = [sums[r : r + SMALL_ROWS, :] for r in range(0, 2 * H, SMALL_ROWS)]
    return jnp.concatenate(groups + [jnp.zeros((SMALL_ROWS, D - 128 * len(groups)), F32)], axis=1)


def project_weights_kernel(count, waits, core, nt_kept, nt_sent, *refs):
    grads, small, (kept, sent) = refs[:count], refs[count : -2 - waits], refs[-2:]
    for i, each in enumerate(grads):
        pl.when(pl.program_id(0) == i)(partial(both_halves, kept, sent, mm, nt_kept, nt_sent, each))
    if small:
        rows = jnp.concatenate([small_sums(*small), jnp.zeros((SMALL_ROWS, D), F32)]).astype(BF16)
        kept[0, HALF:] = rows
        sent[0, HALF:] = rows


def project_weight_grads(core, normed_t, grads, small=(), first=()):
    count, rows = len(grads), HALF + 2 * SMALL_ROWS * (len(small) > 0)
    half = pl.BlockSpec((1, rows, D), lambda i, core: (i, 0, 0))
    return step_call(
        partial(project_weights_kernel, count, len(first)), core, count,
        [rows_half(0), rows_half(1)] + [fixed((LEN, D))] * count + [fixed((H, 1, D))] * len(small) + [ANY] * len(first),
        (normed_t, normed_t, *grads, *small, *first), [half, half], [shape((count, rows, D))] * 2, count, "project_weight_grads")


def split_kernel(waits, mine, kept, came, *refs):
    outs, total = refs[waits:-1], refs[-1]
    total[...] = kept[...].astype(F32) + came[...].astype(F32)
    for c, out in enumerate(outs):
        rows = out.shape[1]
        out[...] = total[:, pl.ds(pl.multiple_of((mine[0] ^ c) * rows, 8), rows), :].astype(BF16)


def split(mine, kept, came, ways, name, first=()):
    count, rows, _ = kept.shape
    block = pl.BlockSpec((1, rows, D), lambda m, mine: (m, 0, 0))
    return step_call(
        partial(split_kernel, len(first)), mine, count, [block, block] + [ANY] * len(first), (kept, came, *first),
        [pl.BlockSpec((1, rows // ways, D), lambda m, mine: (m, 0, 0))] * ways,
        [shape((count, rows // ways, D))] * ways, 0, name, [pltpu.VMEM((1, rows, D), F32)])


def lay_out_kernel(waits, mine, kept, came, *refs):
    out = refs[waits]
    ways, _, rows, _ = out.shape
    for m in range(kept.shape[0]):
        total = kept[m].astype(F32) + came[m].astype(F32)
        for c in range(ways):
            out[c, m] = total[c * rows : (c + 1) * rows, :].astype(BF16)


def lay_out(mine, kept, came, ways, per_step, name, first=()):
    count, rows, _ = kept.shape
    block = pl.BlockSpec((per_step, rows, D), lambda m, mine: (m, 0, 0))
    return step_call(
        partial(lay_out_kernel, len(first)), mine, count // per_step, [block, block] + [ANY] * len(first),
        (kept, came, *first),
        pl.BlockSpec((ways, per_step, rows // ways, D), lambda m, mine: (0, m, 0, 0)),
        shape((ways, count, rows // ways, D)), 0, name)


def plain_call(kernel, operands, mine, out_shape, name, scratch=(), first=(), through=()):
    outs = pl.pallas_call(
        kernel,
        in_specs=[SMEM] + [VMEM] * len(operands) + [ANY] * (len(first) + len(through)),
        out_specs=[VMEM] * len(out_shape) + [ANY] * len(through),
        out_shape=list(out_shape) + [shape(t.shape, t.dtype) for t in through],
        input_output_aliases={1 + len(operands) + len(first) + i: len(out_shape) + i for i in range(len(through))},
        scratch_shapes=list(scratch),
        compiler_params=pltpu.CompilerParams(vmem_limit_bytes=VMEM_LIMIT),
        name=name,
    )(mine, *operands, *first, *through)
    return outs[: len(out_shape)], outs[len(out_shape) :]


def added(refs):
    return sum(ref[...].astype(F32) for ref in refs)


def sum_first(ref):
    return sum(ref[i].astype(F32) for i in range(ref.shape[0]))


def reshare_kernel(line, waits, mine, wide, *refs):
    thin, outs, total = refs[:line], refs[line + waits : -1], refs[-1]
    total[...] = sum_first(wide)
    for c in range(line):
        rows = outs[c].shape[1]
        outs[c][...] = total[:, pl.ds(pl.multiple_of((mine[1] ^ c) * rows, 8), rows), :].astype(BF16)
    out = outs[line]
    thin_sum, rows = added(thin), out.shape[2]
    for c in range(out.shape[0]):
        out[c] = thin_sum[:, c * rows : (c + 1) * rows, :].astype(BF16)


def reshare(mine, wide, thin, first):
    plane, count, rows, _ = wide.shape
    line, (left, thin_rows, _) = len(thin), thin[0].shape
    outs, _ = plain_call(
        partial(reshare_kernel, line, len(first)), [wide, *thin], mine,
        [shape((count, rows // line, D))] * line + [shape((plane, left, thin_rows // plane, D))], "reshare",
        [pltpu.VMEM((count, rows, D), F32)], first)
    return outs[:line], outs[line]


def piece_kernel(line, waits, mine, thin, *refs):
    wide, out = refs[:line], refs[line + waits]
    count = wide[0].shape[0]
    out[:count] = added(wide).astype(BF16)
    out[count:] = sum_first(thin).astype(BF16)


def piece_of(mine, wide, thin, first, through):
    (count, rows, _), left = wide[0].shape, thin.shape[1]
    (out,), through = plain_call(
        partial(piece_kernel, len(wide), len(first) + len(through)), [thin, *wide], mine,
        [shape((count + left, rows, D))], "piece", (), first, through)
    return out, through


def split_small_kernel(mine, kept, came, *refs):
    outs, total, share = refs[:-2], refs[-2], refs[-1]
    total[...] = kept[0].astype(F32) + came[0].astype(F32)
    rows = share.shape[0] - SMALL_ROWS
    share[rows:] = total[HALF : HALF + SMALL_ROWS, :]
    for c, out in enumerate(outs):
        share[:rows] = total[pl.ds(pl.multiple_of((mine[0] ^ c) * rows, 8), rows), :]
        out[...] = share[...].astype(BF16)


def split_small(mine, kept, came, ways, name):
    rows = HALF // ways + SMALL_ROWS
    outs, _ = plain_call(
        split_small_kernel, [kept, came], mine, [shape((rows, D))] * ways, name,
        [pltpu.VMEM(kept.shape[1:], F32), pltpu.VMEM((rows, D), F32)])
    return outs


def project_reshare_kernel(ways, waits, mine, *refs):
    line, through = waits
    pairs, ones, outs = refs[:ways], refs[ways : 2 * ways], refs[2 * ways + through : 2 * ways + through + line]
    pair, one, share = refs[-3:]
    pair[...] = added(pairs)
    one[...] = added(ones)
    rows = pair.shape[1] // len(outs)
    share[3 * rows :] = one[pair.shape[1] :, :]
    for c, out in enumerate(outs):
        start = pl.multiple_of((mine[1] ^ c) * rows, 8)
        share[:rows] = pair[0, pl.ds(start, rows), :]
        share[rows : 2 * rows] = pair[1, pl.ds(start, rows), :]
        share[2 * rows : 3 * rows] = one[pl.ds(start, rows), :]
        out[...] = share[...].astype(BF16)


def project_reshare(mine, pairs, ones, ways, through):
    rows = 3 * pairs[0].shape[1] // ways + SMALL_ROWS
    return plain_call(
        partial(project_reshare_kernel, len(pairs), (ways, len(through))), [*pairs, *ones], mine,
        [shape((rows, D))] * ways, "project_reshare",
        [pltpu.VMEM(pairs[0].shape, F32), pltpu.VMEM(ones[0].shape, F32), pltpu.VMEM((rows, D), F32)], (), through)


def project_piece_kernel(mine, *refs):
    parts, (out, small, total) = refs[:-3], refs[-3:]
    total[...] = added(parts)
    rows = out.shape[1]
    for m in range(3):
        out[m] = total[m * rows : (m + 1) * rows, :].astype(BF16)
    small[...] = total[3 * rows :, :]


def project_piece(mine, parts):
    rows = parts[0].shape[0]
    (out, small), _ = plain_call(
        project_piece_kernel, list(parts), mine,
        [shape((3, (rows - SMALL_ROWS) // 3, D)), shape((SMALL_ROWS, D), F32)], "project_piece",
        [pltpu.VMEM((rows, D), F32)])
    return out, small


def stack_kernel(count, waits, mine, *refs):
    out, at = refs[count + waits], 0
    for ref in refs[:count]:
        out[at : at + ref.shape[0]] = ref[...]
        at += ref.shape[0]


def stack(mine, parts, name, first=()):
    rows = sum(p.shape[0] for p in parts)
    (out,), _ = plain_call(
        partial(stack_kernel, len(parts), len(first)), list(parts), mine, [shape((rows,) + parts[0].shape[1:])], name,
        (), first)
    return out


def tokens_kernel(waits, at, *refs):
    near, near_came, far, forwarded, out = *refs[:4], refs[4 + waits]
    for i, ref in enumerate((near, near_came, far.at[0], forwarded)):
        out[at[0] ^ i] = ref[...]


def tokens_of(at, came, name, first=()):
    (out,), _ = plain_call(
        partial(tokens_kernel, len(first)), list(came), at, [shape((4,) + came[0].shape)], name, (), first)
    return out


def weigh(out, weight):
    product = out[...] * weight[...].astype(F32)
    return sum(product[:, c : c + 128] for c in range(0, D, 128))


def as_row(weighed):
    return jnp.sum(weighed[...].T, axis=0, keepdims=True)


def spread_kernel(sizes, place, own, other, w_query, w_key, w_value, gain, *refs):
    outs, by_gain, weighed = refs[-5:-2], refs[-2], refs[-1]
    matrix = pl.program_id(0)
    plane, line = sizes
    rows = own.shape[2]

    @pl.when(matrix == 0)
    def zero():
        weighed[...] = jnp.zeros_like(weighed)

    for i, (out, weight) in enumerate(zip(outs, (w_query, w_key, w_value))):

        @pl.when(matrix == i)
        def here():
            for c, pieces in enumerate((own, other)):
                for p in range(plane):
                    for n in range(line):
                        at = (place[0] ^ c) * plane * line + (place[1] ^ p) * line + (place[2] ^ n)
                        out[pl.ds(pl.multiple_of(at * rows, 8), rows), :] = pieces[p * line + n, 0].astype(F32)
            weighed[...] += weigh(out, weight)

    @pl.when(matrix == 2)
    def finish():
        by_gain[...] = as_row(weighed) / gain[...]


def matrix_outs(down, over):
    specs, shapes, begin, places = [], [], 0, []
    for d, o in zip(down, over):
        count = d * o

        def place_of(m, *at, begin=begin, count=count, o=o):
            within = jnp.clip(m - begin, 0, count - 1)
            return (within // o, within % o)

        places.append(place_of)
        specs.append(pl.BlockSpec((D, D), place_of))
        shapes.append(shape((d * D, o * D), F32))
        begin += count
    return specs, shapes, begin, places


def spread(place, sizes, own, other, w_query, w_key, w_value, gain, first):
    out_specs, out_shape, count, _ = matrix_outs((1, 1, 1), (1, 1, 1))
    devices, matrices, rows, _ = own.shape
    block = pl.BlockSpec((devices, 1, rows, D), lambda m, place: (0, m, 0, 0))
    square = fixed((D, D))
    return step_call(
        partial(spread_kernel, sizes), place, count, [block, block, square, square, square, fixed((1, D))] + [ANY] * len(first),
        (own, other, w_query, w_key, w_value, gain, *first),
        out_specs + [fixed((1, D))], out_shape + [shape((1, D), F32)], 0, "spread", [pltpu.VMEM((D, 128), F32)])


def fill_kernel(counts, wide_count, starts, pieces, w_hidden, gain, *refs):
    outs, by_gain, weighed = refs[:3], refs[3], refs[4]
    matrix, begin, rows = pl.program_id(0), 0, pieces.shape[2]

    @pl.when(matrix == 0)
    def zero():
        weighed[...] = jnp.zeros_like(weighed)

    for index, (out, count) in enumerate(zip(outs, counts)):
        for table, low, high in ((0, begin, min(begin + count, wide_count)), (1, max(begin, wide_count), begin + count)):
            if low < high:

                @pl.when((matrix >= low) & (matrix < high))
                def here():
                    for device, start in enumerate(starts[table]):
                        out[start : start + rows, :] = pieces[device, 0].astype(F32)
                    if index == 1:
                        weighed[...] += weigh(out, w_hidden)

        begin += count

    @pl.when(matrix == begin - 1)
    def finish():
        by_gain[...] = as_row(weighed) / gain[...]


def fill(pieces, starts, w_hidden, gain):
    blocks = w_hidden.shape[1] // D
    down, over = (blocks, 1, 1), (1, blocks, 1)
    out_specs, out_shape, count, places = matrix_outs(down, over)
    devices, matrices, rows, _ = pieces.shape
    line = whole((1, D))
    return pl.pallas_call(
        partial(fill_kernel, tuple(d * o for d, o in zip(down, over)), wide_and_thin(blocks)[0], starts),
        grid=(count,),
        in_specs=[pl.BlockSpec((devices, 1, rows, D), lambda m: (0, m, 0, 0)), pl.BlockSpec((D, D), places[1]), line],
        out_specs=out_specs + [line],
        out_shape=out_shape + [shape((1, D), F32)],
        scratch_shapes=[pltpu.VMEM((D, 128), F32)],
        compiler_params=params(),
        name="fill",
    )(pieces, w_hidden, gain)


BOTH = ("rows", "seq")


def swap(values, mask):
    n = lax.axis_size("rows") * lax.axis_size("seq")
    return lax.ppermute(values, BOTH, [(s, s ^ mask) for s in range(n)])


def device_bits():
    n = lax.axis_size("rows") * lax.axis_size("seq")
    return [1 << b for b in range(n.bit_length() - 1)]


def masks(dims):
    return [(c, sum(bit for i, bit in enumerate(dims) if c >> i & 1)) for c in range(1 << len(dims))]


def place(dims):
    me = lax.axis_index(BOTH)
    return sum(((me // bit) % 2) << i for i, bit in enumerate(dims))


def exchange(parts, dims):
    return [swap(part, mask) if mask else part for part, (c, mask) in zip(parts, masks(dims))]


def chip_groups():
    chips = device_bits()[1:]
    plane, line, rows = chips[:2], [], HALF >> 2
    for bit in chips[2:]:
        if rows >> (len(line) + 1) << (len(line) + 1) == rows and (rows >> (len(line) + 1)) % 8 == 0:
            line.append(bit)
    return plane, line, chips[2 + len(line) :]


def finish_sum(total, dims):
    for bit in dims:
        total = (total.astype(F32) + swap(total, bit).astype(F32)).astype(total.dtype)
    return total


def row_starts(first, second):
    starts = []
    for device in range(1 << len(device_bits())):
        row, size = 0, D
        for dims in ([1], first, second):
            size >>= len(dims)
            row += size * sum(((device // bit) % 2) << i for i, bit in enumerate(dims))
        starts.append(row)
    return tuple(starts)


def trade(values, dims):
    n = lax.axis_size("rows") * lax.axis_size("seq")
    groups, found = [], set()
    for device in range(n):
        if device not in found:
            group = [device ^ mask for c, mask in masks(dims)]
            found.update(group)
            groups.append(group)
    return lax.all_to_all(values, BOTH, split_axis=0, concat_axis=0, tiled=True, axis_index_groups=groups)


def widen(mine, values, dims, name, first=()):
    return stack(mine, exchange([values] * (1 << len(dims)), dims), name, first)


def send_tokens(parts):
    mine, near, far = parts
    return mine, swap(near, 1), swap(far, 2)


def hand_on(came):
    return (*came, swap(came[2][1], 1))


def per_device(
    inputs,
    segment_ids,
    gain_one,
    w_query,
    w_key,
    w_value,
    w_out,
    mix_logits,
    mix_weights,
    gain_two,
    w_hidden,
    w_back,
    cotangent,
):
    plane, line, others = chip_groups()
    where = jnp.stack([place([1]), place(plane), place(line)])
    core, spots = where[:1], where[1:]
    sizes = (1 << len(plane), 1 << len(line))
    parts, seq = lax.axis_size("seq"), lax.axis_index("seq")
    row_bits, at = device_bits()[: parts.bit_length() - 1], seq.reshape(1)
    ids = lax.dynamic_slice_in_dim(segment_ids, seq, 1, 0)
    gain_one, gain_two = gain_one.reshape(1, D), gain_two.reshape(1, D)
    scale = DH ** -0.5
    mix_l = mix_logits.astype(F32) * scale
    mix_w = mix_weights.astype(F32)

    came = exchange([lax.dynamic_index_in_dim(inputs, seq ^ i, 0, keepdims=False) for i in range(parts)], row_bits)
    near = parts // 2
    begun = project(at, came[:near], 0, gain_one, w_query, w_key, w_value)
    done = project(at, came[near:], near, gain_one, w_query, w_key, w_value, begun, cotangent)
    (x, normed_t, q, q_t, k, k_t, v, v_t), cots = done[:8], exchange(done[8:], row_bits)
    soft, attended = attend(mix_l, mix_w, ids, q_t, k, v_t)
    out, (cot, normed_two, activated, grad_hidden, grad_middle, grad_attn, g, g_t) = feed(
        at, x, attended, cots, w_out, w_hidden, w_back, gain_two
    )
    out = send_tokens(out)
    wide_kept, wide_sent = wide_weight_grads(core, activated, cot, normed_two, grad_hidden)
    thin_kept, thin_sent = thin_weight_grads(core, normed_two, grad_hidden, attended, grad_attn, [wide_kept, *out[1:]])
    wide = lay_out(core, wide_kept, swap(wide_sent, 1), sizes[0], 2, "lay_out_wide", [thin_kept])
    thin = split(spots[1:], thin_kept, swap(thin_sent, 1), sizes[1], "split_thin", [wide])
    grad_q, grad_logits, by_logits = query_grads(mix_w, mix_l, soft, v, g_t, k_t, q_t, [wide, thin[0]])
    wide, thin = reshare(spots, trade(wide, plane), exchange(thin, line), [grad_q])
    grad_k = key_grads(mix_l, grad_logits, q, [wide[0]])
    pair_kept, pair_sent = project_weight_grads(core, normed_t, [grad_q, grad_k])
    out = hand_on(out)
    piece, _ = piece_of(spots, exchange(wide, line), trade(thin, plane), [grad_k], [])
    pieces = lax.all_gather(finish_sum(piece, others), BOTH, axis=0)
    pair_kept, pair_sent = project_weight_grads(core, normed_t, [grad_q, grad_k], (), [piece])
    pair = split(spots[:1], pair_kept, swap(pair_sent, 1), sizes[0], "split_pair")
    grad_v, by_weights = value_grads(mix_w, soft, v, g, [piece, pair[0]])
    pair = exchange(pair, plane)
    one_kept, one_sent = project_weight_grads(core, normed_t, [grad_v], [by_logits, by_weights], pair[1:])
    one = split_small(spots[:1], one_kept, swap(one_sent, 1), sizes[0], "split_one")
    grad_in = input_grads(
        at, parts, grad_q, grad_k, grad_v, x, grad_middle, w_query, w_key, w_value, gain_one, one[0])
    shares, grad_in = project_reshare(spots, pair, exchange(one, plane), sizes[1], grad_in)
    own, small = project_piece(spots, exchange(shares, line))
    own, small = finish_sum(own, others)[None], finish_sum(small, others)
    block_out = tokens_of(at, out, "block_out")
    grad_in = send_tokens(grad_in)
    own = widen(spots, own, line, "stack_line", [block_out, *grad_in[1:]])
    grad_w_back, grad_w_hidden, grad_w_out, grad_gain_two = fill(
        pieces, (row_starts(plane, line), row_starts(line, plane)), w_hidden, gain_two)
    grad_inputs = tokens_of(at, hand_on(grad_in), "grad_inputs", [grad_w_out])
    own = widen(spots, own, plane, "stack_plane", [grad_w_out])
    grad_w_query, grad_w_key, grad_w_value, grad_gain_one = spread(
        where, sizes, own, swap(own, 1), w_query, w_key, w_value, gain_one, [grad_w_out])
    small = small[:, : 3 * 128].reshape(SMALL_ROWS, 3, 128).transpose(1, 0, 2).reshape(2, H, 128)[:, :, :H]
    return (
        block_out,
        grad_inputs,
        grad_gain_one.reshape(D),
        grad_w_query,
        grad_w_key,
        grad_w_value,
        grad_w_out,
        small[0].T * scale,
        small[1],
        grad_gain_two.reshape(D),
        grad_w_hidden,
        grad_w_back,
    )


def solution(mesh):
    sharded, copied = P("rows", "seq", None), P()
    in_specs = (sharded, P("rows", None)) + (copied,) * 10 + (sharded,)
    out_specs = (sharded, sharded) + (copied,) * 10
    return jax.shard_map(
        per_device, mesh=mesh, in_specs=in_specs, out_specs=out_specs, check_vma=False
    )
```

profile of v0, /device:TPU:0, one launch (start us, length us, event | category | flops | bytes accessed | tf_op | source)
XLA Modules:
  0.0 424.1 jit_solution(16413140578516638720)
XLA Ops:
  7.3 2.2 dynamic-slice_bitcast_fusion
  9.9 2.5 collective-permute-start
  13.8 1.0 copy.39.id_col
  16.7 5.9 %project.2 = (bf16[1024,768]{1,0:T(8,128)(2,1)}, bf16[768,1024]{1,0:T(8,128)(2,1)}, bf16[1024,768]{1,0:T(8,128)(2,1)}, bf16[768,1024]{1,0:T(8,128)(2,1)}, bf16[1...) custom-call(s32[1]{0:T(128)} %bitcast.at, ...), custom_call_target="tpu_custom_call" | custom-call | flops 226492416 | bytes 786432 | tf_op jit(solution)/shard_map/project/pallas_call | solution.py:296
  22.6 7.8 %collective-permute-done.1.refs_1_ = bf16[256,768]{1,0:T(8,128)(2,1)S(1)} collective-permute-done((bf16[256,768]{1,0:T(8,128)(2,1)S(1)}, bf16[256,768]{1,0:T(8,128)(2,1)S(1)}, u32[]{:S(2)}, u32[]{:S(2)}) %collective-permute-start.1) | collective-permute-done | bytes 393248 | tf_op jit(solution)/shard_map/ppermute | solution.py:831
  31.2 7.7 %project.3 = (bf16[1024,768]{1,0:T(8,128)(2,1)}, bf16[768,1024]{1,0:T(8,128)(2,1)}, bf16[1024,768]{1,0:T(8,128)(2,1)}, bf16[768,1024]{1,0:T(8,128)(2,1)}, bf16[1...) custom-call(s32[1]{0:T(128)} %bitcast.at, ...), custom_call_target="tpu_custom_call", output_to_operand_aliasing={{0}: (7, {}), {1}: (8, {}), {2}: (9, {}), {3}: (10, {}), {4... | custom-call | flops 226492416 | bytes 786432 | tf_op jit(solution)/shard_map/project/pallas_call | solution.py:296
  39.1 1.6 collective-permute-start.4
  41.5 41.4 %attend.1 = (bf16[12,1024,1024]{2,1,0:T(8,128)(2,1)}, bf16[1024,768]{1,0:T(8,128)(2,1)}) custom-call(f32[12,12]{1,0:T(8,128)} %convert_multiply_fusion.mix_l, f32[12,12]{1,0:T(8,128)} %convert_element_type.7.mix_w, s32[1,1024]{1,0:T(1,128)} %constant_dynamic-slice_fusion.id_row, s32[1024,1]{1,0:T(8,128)} %copy.39.id_col, ...), custom_call_target="tpu_custom_call" | custom-call | flops 3019898880 | bytes 1048576 | tf_op jit(solution)/shard_map/attend/pallas_call | solution.py:86
  83.9 36.7 %feed.1 = (bf16[256,768]{1,0:T(8,128)(2,1)}, bf16[256,768]{1,0:T(8,128)(2,1)}, bf16[2,256,768]{2,1,0:T(8,128)(2,1)}, bf16[1024,768]{1,0:T(8,128)(2,1)}, bf16[102...) custom-call(s32[1]{0:T(128)} %bitcast.at, ...), custom_call_target="tpu_custom_call" | custom-call | flops 2717908992 | bytes 786432 | tf_op jit(solution)/shard_map/feed/pallas_call | solution.py:296
  120.6 13.7 %wide_weight_grads.1 = (bf16[6,384,768]{2,1,0:T(8,128)(2,1)}, bf16[6,384,768]{2,1,0:T(8,128)(2,1)}) custom-call(s32[1]{0:T(128)} %bitcast.9.core.mine, bf16[1024,3072]{1,0:T(8,128)(2,1)} %get-tuple-element.120.act_kept.act_sent, bf16[1024,3072]{1,0:T(8,128)(2,1)} %get-tuple-element.120.act_kept.act_sent, bf16[1024,768]{1,0:T(8,128)(2,1)} %get-tuple-element.121.cot, ...), custom_call_target="tpu_custom_call" | custom-call | flops 905969664 | bytes 786432 | tf_op jit(solution)/shard_map/wide_weight_grads/pallas_call | solution.py:296
  134.6 1.7 collective-permute-start.7
  136.3 4.8 %collective-permute-done.6.refs_1_ = bf16[256,768]{1,0:T(8,128)(2,1)S(1)} collective-permute-done((bf16[256,768]{1,0:T(8,128)(2,1)S(1)}, bf16[256,768]{1,0:T(8,128)(2,1)S(1)}, u32[]{:S(2)}, u32[]{:S(2)}) %collective-permute-start.6) | collective-permute-done | bytes 393248 | tf_op jit(solution)/shard_map/ppermute | solution.py:831
  141.1 13.2 %collective-permute-done.7.refs_2_ = bf16[2,256,768]{2,1,0:T(8,128)(2,1)S(1)} collective-permute-done((bf16[2,256,768]{2,1,0:T(8,128)(2,1)S(1)}, bf16[2,256,768]{2,1,0:T(8,128)(2,1)S(1)}, u32[]{:S(2)}, u32[]{:S(2)}) %collective-permute-start.7) | collective-permute-done | bytes 786464 | tf_op jit(solution)/shard_map/ppermute | solution.py:831
  155.1 8.2 %thin_weight_grads.1 = (bf16[3,384,768]{2,1,0:T(8,128)(2,1)}, bf16[3,384,768]{2,1,0:T(8,128)(2,1)}) custom-call(s32[1]{0:T(128)} %bitcast.9.core.mine, bf16[1024,768]{1,0:T(8,128)(2,1)} %get-tuple-element.122.n2_kept.n2_sent, bf16[1024,768]{1,0:T(8,128)(2,1)} %get-tuple-element.122.n2_kept.n2_sent, bf16[1024,3072]{1,0:T(8,128)(2,1)} %get-tuple-element.123.grad_hidden, ...), custom_call_target="tpu_custom_call" | custom-call | flops 452984832 | bytes 786432 | tf_op jit(solution)/shard_map/thin_weight_grads/pallas_call | solution.py:296
  163.3 5.8 %lay_out_wide.1.refs_0_.rest_0_ = bf16[4,6,96,768]{3,2,1,0:T(8,128)(2,1)} custom-call(s32[1]{0:T(128)} %bitcast.9.core.mine, bf16[6,384,768]{2,1,0:T(8,128)(2,1)} %get-tuple-element.124.refs_0_.kept, bf16[6,384,768]{2,1,0:T(8,128)(2,1)} %collective-permute-done.9.came, bf16[3,384,768]{2,1,0:T(8,128)(2,1)} %get-tuple-element.127.refs_0_.kept), custom_call_target="tpu_custom_call" | custom-call | bytes 786432 | tf_op jit(solution)/shard_map/lay_out_wide/pallas_call | solution.py:296
  169.1 3.9 all-to-all-start
  173.2 4.0 collective-permute-done.10.came
  177.2 4.2 split_thin.1
  181.3 1.6 collective-permute-start.11
  182.9 2.6 collective-permute-start.12
  186.3 39.4 %query_grads.1 = (bf16[1024,768]{1,0:T(8,128)(2,1)}, bf16[12,1024,1024]{2,1,0:T(8,128)(2,1)}, f32[12,1,768]{2,1,0:T(1,128)}) custom-call(f32[12,12]{1,0:T(8,128)} %convert_element_type.7.mix_w, f32[12,12]{1,0:T(8,128)} %convert_multiply_fusion.mix_l, bf16[12,1024,1024]{2,1,0:T(8,128)(2,1)} %get-tuple-element.116.soft, ...), custom_call_target="tpu_custom_call" | custom-call | flops 3019898880 | bytes 1048576 | tf_op jit(solution)/shard_map/query_grads/pallas_call | solution.py:198
  225.8 1.8 copy-done.2
  227.5 4.5 %reshare.1 = (bf16[6,24,768]{2,1,0:T(8,128)(2,1)}, bf16[6,24,768]{2,1,0:T(8,128)(2,1)}, bf16[6,24,768]{2,1,0:T(8,128)(2,1)}, bf16[6,24,768]{2,1,0:T(8,128)(2,1)}, bf16[4,3,24,768]{3,2,1,0:T(8,128)(2,1)}) custom-call(s32[2]{0:T(128)} %pad_add_fusion.mine, bf16[4,6,96,768]{3,2,1,0:T(8,128)(2,1)} %copy-done.2, ...), custom_call_target="tpu_custom_call" | custom-call | tf_op jit(solution)/shard_map/reshare/pallas_call | solution.py:575
  232.0 4.2 all-to-all-start.1
  236.9 3.5 collective-permute-start.15
  240.6 17.8 %key_grads.1.refs_4_.refs_1_.grad_k = bf16[1024,768]{1,0:T(8,128)(2,1)} custom-call(f32[12,12]{1,0:T(8,128)} %convert_multiply_fusion.mix_l, bf16[12,1024,1024]{2,1,0:T(8,128)(2,1)} %get-tuple-element.131.grad_logits, bf16[1024,768]{1,0:T(8,128)(2,1)} %get-tuple-element.132.q, bf16[6,24,768]{2,1,0:T(8,128)(2,1)} %get-tuple-element.136.rest_0_.refs_0_), custom_call_target="tpu_custom_call" | custom-call | flops 1509949440 | bytes 1048576 | tf_op jit(solution)/shard_map/key_grads/pallas_call | solution.py:198
  260.0 2.3 piece.1.refs_2_.rest_0_
  262.3 6.2 %project_weight_grads.2 = (bf16[2,384,768]{2,1,0:T(8,128)(2,1)}, bf16[2,384,768]{2,1,0:T(8,128)(2,1)}) custom-call(s32[1]{0:T(128)} %bitcast.9.core.mine, bf16[768,1024]{1,0:T(8,128)(2,1)} %get-tuple-element.115.nt_kept.nt_sent, bf16[768,1024]{1,0:T(8,128)(2,1)} %get-tuple-element.115.nt_kept.nt_sent, ...), custom_call_target="tpu_custom_call" | custom-call | flops 301989888 | bytes 786432 | tf_op jit(solution)/shard_map/project_weight_grads/pallas_call | solution.py:296
  268.5 3.1 collective-permute-done.17.came
  271.6 1.0 copy-done.14
  272.6 2.7 split_pair.1
  275.3 2.0 collective-permute-start.18
  277.3 1.5 collective-permute-start.19
  278.9 19.4 %value_grads.1 = (bf16[1024,768]{1,0:T(8,128)(2,1)}, f32[12,1,768]{2,1,0:T(1,128)}) custom-call(f32[12,12]{1,0:T(8,128)} %convert_element_type.7.mix_w, bf16[12,1024,1024]{2,1,0:T(8,128)(2,1)} %get-tuple-element.116.soft, bf16[1024,768]{1,0:T(8,128)(2,1)} %get-tuple-element.117.v, bf16[1024,768]{1,0:T(8,128)(2,1)} %get-tuple-element.147.g, ...), custom_call_target="tpu_custom_call" | custom-call | flops 1509949440 | bytes 1048576 | tf_op jit(solution)/shard_map/value_grads/pallas_call | solution.py:198
  299.2 4.5 %project_weight_grads.3 = (bf16[1,400,768]{2,1,0:T(8,128)(2,1)}, bf16[1,400,768]{2,1,0:T(8,128)(2,1)}) custom-call(s32[1]{0:T(128)} %bitcast.9.core.mine, bf16[768,1024]{1,0:T(8,128)(2,1)} %get-tuple-element.115.nt_kept.nt_sent, bf16[768,1024]{1,0:T(8,128)(2,1)} %get-tuple-element.115.nt_kept.nt_sent, bf16[1024,768]{1,0:T(8,128)(2,1)} %get-tuple-element.148.refs_0_.grad_v, ...), custom_call_target="tpu_custom_call" | custom-call | flops 150994944 | bytes 786432 | tf_op jit(solution)/shard_map/project_weight_grads/pallas_call | solution.py:296
  303.7 2.2 collective-permute-done.21.came
  306.8 2.3 split_one.1
  309.1 2.0 collective-permute-start.22
  311.1 1.5 collective-permute-start.23
  312.6 10.2 %input_grads.1 = (bf16[256,768]{1,0:T(8,128)(2,1)}, bf16[256,768]{1,0:T(8,128)(2,1)}, bf16[2,256,768]{2,1,0:T(8,128)(2,1)}) custom-call(s32[1]{0:T(128)} %bitcast.at, bf16[1024,768]{1,0:T(8,128)(2,1)} %get-tuple-element.130.refs_4_.refs_0_.grad_q, bf16[1024,768]{1,0:T(8,128)(2,1)} %key_grads.1.refs_4_.refs_1_.grad_k, ...), custom_call_target="tpu_custom_call" | custom-call | flops 452984832 | bytes 786432 | tf_op jit(solution)/shard_map/input_grads/pallas_call | solution.py:296
  323.7 2.6 project_reshare.1
  326.4 2.4 collective-permute-start.26
  329.6 4.2 collective-permute-start.29
  333.8 6.3 %collective-permute-done.28.refs_1_ = bf16[80,768]{1,0:T(8,128)(2,1)S(1)} collective-permute-done((bf16[80,768]{1,0:T(8,128)(2,1)}, bf16[80,768]{1,0:T(8,128)(2,1)S(1)}, u32[]{:S(2)}, u32[]{:S(2)}) %collective-permute-start.28) | collective-permute-done | bytes 122912 | tf_op jit(solution)/shard_map/ppermute | solution.py:831
  340.1 1.6 collective-permute-start.30
  341.8 5.8 %collective-permute-done.30.refs_3_ = bf16[80,768]{1,0:T(8,128)(2,1)S(1)} collective-permute-done((bf16[80,768]{1,0:T(8,128)(2,1)}, bf16[80,768]{1,0:T(8,128)(2,1)S(1)}, u32[]{:S(2)}, u32[]{:S(2)}) %collective-permute-start.30) | collective-permute-done | bytes 122912 | tf_op jit(solution)/shard_map/ppermute | solution.py:831
  348.2 1.9 project_piece.1
  350.1 2.6 collective-permute-start.31
  352.7 2.4 collective-permute-start.33
  355.0 2.7 block_out.1.refs_4_
  357.8 5.4 %collective-permute-done.31.refs_1_ = bf16[1,3,24,768]{3,2,1,0:T(8,128)(2,1)S(1)} collective-permute-done((bf16[1,3,24,768]{3,2,1,0:T(8,128)(2,1)}, bf16[1,3,24,768]{3,2,1,0:T(8,128)(2,1)S(1)}, u32[]{:S(2)}, u32[]{:S(2)}) %collective-permute-start.31) | collective-permute-done | bytes 110624 | tf_op jit(solution)/shard_map/ppermute | solution.py:831
  364.0 4.6 %collective-permute-done.33.refs_3_ = bf16[1,3,24,768]{3,2,1,0:T(8,128)(2,1)S(1)} collective-permute-done((bf16[1,3,24,768]{3,2,1,0:T(8,128)(2,1)}, bf16[1,3,24,768]{3,2,1,0:T(8,128)(2,1)S(1)}, u32[]{:S(2)}, u32[]{:S(2)}) %collective-permute-start.33) | collective-permute-done | bytes 110624 | tf_op jit(solution)/shard_map/ppermute | solution.py:831
  369.4 0.9 copy-done.5
  370.2 1.9 stack_line.1.refs_0_
  372.1 1.5 collective-permute-start.34
  373.6 1.5 collective-permute-start.35
  375.6 16.7 %fill.1 = (f32[3072,768]{1,0:T(8,128)}, f32[768,3072]{1,0:T(8,128)}, f32[768,768]{1,0:T(8,128)}, f32[1,768]{1,0:T(1,128)}) custom-call(bf16[32,9,24,768]{3,2,1,0:T(8,128)(2,1)} %bitcast.30, bf16[768,3072]{1,0:T(8,128)(2,1)} %w_hidden.1, f32[1,768]{1,0:T(1,128)} %reshape.53.refs_7_.gain), custom_call_target="tpu_custom_call" | custom-call | tf_op jit(solution)/shard_map/fill/pallas_call | solution.py:814
  392.3 2.2 collective-permute-done.35.refs_2_
  395.5 2.8 stack_plane.1.own
  401.4 1.1 collective-permute-done.27.refs_3_
  403.3 2.7 grad_inputs.1
  406.0 1.2 copy-done.8
  407.2 8.5 %spread.1 = (f32[768,768]{1,0:T(8,128)}, f32[768,768]{1,0:T(8,128)}, f32[768,768]{1,0:T(8,128)}, f32[1,768]{1,0:T(1,128)}) custom-call(s32[3]{0:T(128)} %pad_add_fusion.1.place, bf16[16,3,24,768]{3,2,1,0:T(8,128)(2,1)} %stack_plane.1.own, bf16[16,3,24,768]{3,2,1,0:T(8,128)(2,1)} %copy-done.8, bf16[768,768]{1,0:T(8,128)(2,1)} %w_query.3, ...), custom_call_target="tpu_custom_call" | custom-call | bytes 786432 | tf_op jit(solution)/shard_map/spread/pallas_call | solution.py:296
  415.7 1.3 reduce
  (157 shorter events, 21.9 us)
Async XLA Ops:
  7.2 6.6 %copy-start = (s32[4,1024]{1,0:T(4,128)S(1)}, s32[4,1024]{1,0:T(4,128)}, u32[]{:S(2)}) copy-start(s32[4,1024]{1,0:T(4,128)} %param.14) | copy-start | bytes 49156
  7.2 5.4 %copy-start.42 = (f32[768]{0:T(1024)S(1)}, f32[768]{0:T(1024)}, u32[]{:S(2)}) copy-start(f32[768]{0:T(1024)} %param.15) | copy-start | bytes 9220
  7.2 5.9 %copy-start.40 = (bf16[12,12]{1,0:T(8,128)(2,1)S(1)}, bf16[12,12]{1,0:T(8,128)(2,1)}, u32[]{:S(2)}) copy-start(bf16[12,12]{1,0:T(8,128)(2,1)} %param.21) | copy-start | bytes 868
  7.2 7.6 %copy-start.43 = (f32[768]{0:T(1024)S(1)}, f32[768]{0:T(1024)}, u32[]{:S(2)}) copy-start(f32[768]{0:T(1024)} %param.22) | copy-start | bytes 9220
  7.2 8.1 %copy-start.41 = (bf16[12,12]{1,0:T(8,128)(2,1)S(1)}, bf16[12,12]{1,0:T(8,128)(2,1)}, u32[]{:S(2)}) copy-start(bf16[12,12]{1,0:T(8,128)(2,1)} %param.20) | copy-start | bytes 868
  9.5 6.5 %collective-permute-start.2 = (bf16[256,768]{1,0:T(8,128)(2,1)S(1)}, bf16[256,768]{1,0:T(8,128)(2,1)S(1)}, u32[]{:S(2)}, u32[]{:S(2)}) collective-permute-start(bf16[256,768]{1,0:T(8,128)(2,1)S(1)} %get-tuple-element.214), channel_id=1, source_target_pairs={{0,1},{1,0},{2,3},{3,2},{4,5},{5,4},{6,7},{7,6},{8,9},{9,8},{10,11... | collective-permute-start | bytes 1179656 | tf_op jit(solution)/shard_map/ppermute | solution.py:831
  9.9 12.7 %collective-permute-start = (bf16[256,768]{1,0:T(8,128)(2,1)S(1)}, bf16[256,768]{1,0:T(8,128)(2,1)S(1)}, u32[]{:S(2)}, u32[]{:S(2)}) collective-permute-start(bf16[256,768]{1,0:T(8,128)(2,1)S(1)} %get-tuple-element.216), channel_id=1, source_target_pairs={{0,2},{1,3},{2,0},{3,1},{4,6},{5,7},{6,4},{7,5},{8,10},{9,11},{10,... | collective-permute-start | bytes 1179656 | tf_op jit(solution)/shard_map/ppermute | solution.py:831
  12.4 18.0 %collective-permute-start.1 = (bf16[256,768]{1,0:T(8,128)(2,1)S(1)}, bf16[256,768]{1,0:T(8,128)(2,1)S(1)}, u32[]{:S(2)}, u32[]{:S(2)}) collective-permute-start(bf16[256,768]{1,0:T(8,128)(2,1)S(1)} %get-tuple-element.215), channel_id=1, source_target_pairs={{0,3},{1,2},{2,1},{3,0},{4,7},{5,6},{6,5},{7,4},{8,11},{9,10},{10,... | collective-permute-start | bytes 1179656 | tf_op jit(solution)/shard_map/ppermute | solution.py:831
  22.6 7.8 %copy-start.22 = (bf16[256,768]{1,0:T(8,128)(2,1)}, bf16[256,768]{1,0:T(8,128)(2,1)S(1)}, u32[]{:S(2)}) copy-start(bf16[256,768]{1,0:T(8,128)(2,1)S(1)} %collective-permute-done.refs_0_) | copy-start | bytes 1179652
  38.9 43.9 %collective-permute-start.3 = (bf16[256,768]{1,0:T(8,128)(2,1)}, bf16[256,768]{1,0:T(8,128)(2,1)S(1)}, u32[]{:S(2)}, u32[]{:S(2)}) collective-permute-start(bf16[256,768]{1,0:T(8,128)(2,1)} %get-tuple-element.109), channel_id=1, source_target_pairs={{0,1},{1,0},{2,3},{3,2},{4,5},{5,4},{6,7},{7,6},{8,9},{9,8},{10,11... | collective-permute-start | bytes 1179656 | tf_op jit(solution)/shard_map/ppermute | solution.py:831
  39.1 43.7 %collective-permute-start.4 = (bf16[256,768]{1,0:T(8,128)(2,1)}, bf16[256,768]{1,0:T(8,128)(2,1)S(1)}, u32[]{:S(2)}, u32[]{:S(2)}) collective-permute-start(bf16[256,768]{1,0:T(8,128)(2,1)} %get-tuple-element.110), channel_id=1, source_target_pairs={{0,2},{1,3},{2,0},{3,1},{4,6},{5,7},{6,4},{7,5},{8,10},{9,11},{10,... | collective-permute-start | bytes 1179656 | tf_op jit(solution)/shard_map/ppermute | solution.py:831
  40.8 42.1 %collective-permute-start.5 = (bf16[256,768]{1,0:T(8,128)(2,1)}, bf16[256,768]{1,0:T(8,128)(2,1)S(1)}, u32[]{:S(2)}, u32[]{:S(2)}) collective-permute-start(bf16[256,768]{1,0:T(8,128)(2,1)} %get-tuple-element.111), channel_id=1, source_target_pairs={{0,3},{1,2},{2,1},{3,0},{4,7},{5,6},{6,5},{7,4},{8,11},{9,10},{10,... | collective-permute-start | bytes 1179656 | tf_op jit(solution)/shard_map/ppermute | solution.py:831
  120.6 14.1 %copy-start.45 = (bf16[2,256,768]{2,1,0:T(8,128)(2,1)S(1)}, bf16[2,256,768]{2,1,0:T(8,128)(2,1)}, u32[]{:S(2)}) copy-start(bf16[2,256,768]{2,1,0:T(8,128)(2,1)} %get-tuple-element.114) | copy-start | bytes 2359300
  120.6 15.7 %copy-start.46 = (bf16[256,768]{1,0:T(8,128)(2,1)S(1)}, bf16[256,768]{1,0:T(8,128)(2,1)}, u32[]{:S(2)}) copy-start(bf16[256,768]{1,0:T(8,128)(2,1)} %get-tuple-element.113) | copy-start | bytes 1179652
  134.3 29.0 %collective-permute-start.9 = (bf16[6,384,768]{2,1,0:T(8,128)(2,1)}, bf16[6,384,768]{2,1,0:T(8,128)(2,1)}, u32[]{:S(2)}, u32[]{:S(2)}) collective-permute-start(bf16[6,384,768]{2,1,0:T(8,128)(2,1)} %get-tuple-element.125), channel_id=1, source_target_pairs={{0,1},{1,0},{2,3},{3,2},{4,5},{5,4},{6,7},{7,6},{8,9},{9,8},{10,11... | collective-permute-start | bytes 10616840 | tf_op jit(solution)/shard_map/ppermute | solution.py:831
  134.6 19.6 %collective-permute-start.7 = (bf16[2,256,768]{2,1,0:T(8,128)(2,1)S(1)}, bf16[2,256,768]{2,1,0:T(8,128)(2,1)S(1)}, u32[]{:S(2)}, u32[]{:S(2)}) collective-permute-start(bf16[2,256,768]{2,1,0:T(8,128)(2,1)S(1)} %copy-done.45), channel_id=1, source_target_pairs={{0,2},{1,3},{2,0},{3,1},{4,6},{5,7},{6,4},{7,5},{8,10},{9,11},{10,... | collective-permute-start | bytes 2359304 | tf_op jit(solution)/shard_map/ppermute | solution.py:831
  136.3 4.8 %collective-permute-start.6 = (bf16[256,768]{1,0:T(8,128)(2,1)S(1)}, bf16[256,768]{1,0:T(8,128)(2,1)S(1)}, u32[]{:S(2)}, u32[]{:S(2)}) collective-permute-start(bf16[256,768]{1,0:T(8,128)(2,1)S(1)} %copy-done.46), channel_id=1, source_target_pairs={{0,1},{1,0},{2,3},{3,2},{4,5},{5,4},{6,7},{7,6},{8,9},{9,8},{10,11... | collective-permute-start | bytes 1179656 | tf_op jit(solution)/shard_map/ppermute | solution.py:831
  141.1 13.2 %copy-start.10 = (bf16[256,768]{1,0:T(8,128)(2,1)}, bf16[256,768]{1,0:T(8,128)(2,1)S(1)}, u32[]{:S(2)}) copy-start(bf16[256,768]{1,0:T(8,128)(2,1)S(1)} %collective-permute-done.6.refs_1_) | copy-start | bytes 1179652
  169.1 56.6 %all-to-all-start = ((bf16[4,6,96,768]{3,2,1,0:T(8,128)(2,1)}), bf16[4,6,96,768]{3,2,1,0:T(8,128)(2,1)S(1)}, u32[]{:S(2)}, u32[]{:S(2)}) async-start(bf16[4,6,96,768]{3,2,1,0:T(8,128)(2,1)} %lay_out_wide.1.refs_0_.rest_0_), calls=%async_computation | async-start | bytes 7077888 | tf_op jit(solution)/shard_map/all_to_all | solution.py:886
  173.1 4.1 collective-permute-start.10
  181.3 44.4 %collective-permute-start.11 = (bf16[3,96,768]{2,1,0:T(8,128)(2,1)}, bf16[3,96,768]{2,1,0:T(8,128)(2,1)}, u32[]{:S(2)}, u32[]{:S(2)}) collective-permute-start(bf16[3,96,768]{2,1,0:T(8,128)(2,1)} %get-tuple-element.133), channel_id=1, source_target_pairs={{0,8},{1,9},{2,10},{3,11},{4,12},{5,13},{6,14},{7,15},{8,0},{9,1},... | collective-permute-start | bytes 1327112 | tf_op jit(solution)/shard_map/ppermute | solution.py:831
  182.9 42.8 %collective-permute-start.12 = (bf16[3,96,768]{2,1,0:T(8,128)(2,1)}, bf16[3,96,768]{2,1,0:T(8,128)(2,1)}, u32[]{:S(2)}, u32[]{:S(2)}) collective-permute-start(bf16[3,96,768]{2,1,0:T(8,128)(2,1)} %get-tuple-element.134), channel_id=1, source_target_pairs={{0,16},{1,17},{2,18},{3,19},{4,20},{5,21},{6,22},{7,23},{8,24},{9,... | collective-permute-start | bytes 1327112 | tf_op jit(solution)/shard_map/ppermute | solution.py:831
  185.5 40.2 %collective-permute-start.13 = (bf16[3,96,768]{2,1,0:T(8,128)(2,1)}, bf16[3,96,768]{2,1,0:T(8,128)(2,1)}, u32[]{:S(2)}, u32[]{:S(2)}) collective-permute-start(bf16[3,96,768]{2,1,0:T(8,128)(2,1)} %get-tuple-element.135), channel_id=1, source_target_pairs={{0,24},{1,25},{2,26},{3,27},{4,28},{5,29},{6,30},{7,31},{8,16},{9,... | collective-permute-start | bytes 1327112 | tf_op jit(solution)/shard_map/ppermute | solution.py:831
  225.8 1.8 copy-start.2
  232.0 26.4 %all-to-all-start.1 = ((bf16[4,3,24,768]{3,2,1,0:T(8,128)(2,1)}), bf16[4,3,24,768]{3,2,1,0:T(8,128)(2,1)S(1)}, u32[]{:S(2)}, u32[]{:S(2)}) async-start(bf16[4,3,24,768]{3,2,1,0:T(8,128)(2,1)} %get-tuple-element.137), calls=%async_computation.1 | async-start | bytes 884736 | tf_op jit(solution)/shard_map/all_to_all | solution.py:886
  236.2 139.4 %all-gather.3.cloned.1.call-start = ((), (), s32[]{:S(2)}) async-start(), calls=%async_computation.2 | async-start | bytes 10948608 | tf_op jit(solution)/shard_map/all_gather | solution.py:949
  236.2 22.2 %collective-permute-start.14 = (bf16[6,24,768]{2,1,0:T(8,128)(2,1)}, bf16[6,24,768]{2,1,0:T(8,128)(2,1)S(1)}, u32[]{:S(2)}, u32[]{:S(2)}) collective-permute-start(bf16[6,24,768]{2,1,0:T(8,128)(2,1)} %get-tuple-element.138), channel_id=1, source_target_pairs={{0,8},{1,9},{2,10},{3,11},{4,12},{5,13},{6,14},{7,15},{8,0},{9,1},... | collective-permute-start | bytes 663560 | tf_op jit(solution)/shard_map/ppermute | solution.py:831
  236.9 21.5 %collective-permute-start.15 = (bf16[6,24,768]{2,1,0:T(8,128)(2,1)}, bf16[6,24,768]{2,1,0:T(8,128)(2,1)S(1)}, u32[]{:S(2)}, u32[]{:S(2)}) collective-permute-start(bf16[6,24,768]{2,1,0:T(8,128)(2,1)} %get-tuple-element.139), channel_id=1, source_target_pairs={{0,16},{1,17},{2,18},{3,19},{4,20},{5,21},{6,22},{7,23},{8,24},{9,... | collective-permute-start | bytes 663560 | tf_op jit(solution)/shard_map/ppermute | solution.py:831
  240.4 18.1 %collective-permute-start.16 = (bf16[6,24,768]{2,1,0:T(8,128)(2,1)}, bf16[6,24,768]{2,1,0:T(8,128)(2,1)S(1)}, u32[]{:S(2)}, u32[]{:S(2)}) collective-permute-start(bf16[6,24,768]{2,1,0:T(8,128)(2,1)} %get-tuple-element.140), channel_id=1, source_target_pairs={{0,24},{1,25},{2,26},{3,27},{4,28},{5,29},{6,30},{7,31},{8,16},{9,... | collective-permute-start | bytes 663560 | tf_op jit(solution)/shard_map/ppermute | solution.py:831
  268.5 3.1 collective-permute-start.17
  271.6 1.0 copy-start.14
  275.3 23.0 %collective-permute-start.18 = (bf16[2,96,768]{2,1,0:T(8,128)(2,1)}, bf16[2,96,768]{2,1,0:T(8,128)(2,1)S(1)}, u32[]{:S(2)}, u32[]{:S(2)}) collective-permute-start(bf16[2,96,768]{2,1,0:T(8,128)(2,1)} %get-tuple-element.144), channel_id=1, source_target_pairs={{0,2},{1,3},{2,0},{3,1},{4,6},{5,7},{6,4},{7,5},{8,10},{9,11},{10,... | collective-permute-start | bytes 884744 | tf_op jit(solution)/shard_map/ppermute | solution.py:831
  277.3 21.0 %collective-permute-start.19 = (bf16[2,96,768]{2,1,0:T(8,128)(2,1)}, bf16[2,96,768]{2,1,0:T(8,128)(2,1)S(1)}, u32[]{:S(2)}, u32[]{:S(2)}) collective-permute-start(bf16[2,96,768]{2,1,0:T(8,128)(2,1)} %get-tuple-element.145), channel_id=1, source_target_pairs={{0,4},{1,5},{2,6},{3,7},{4,0},{5,1},{6,2},{7,3},{8,12},{9,13},{10,... | collective-permute-start | bytes 884744 | tf_op jit(solution)/shard_map/ppermute | solution.py:831
  278.8 19.5 %collective-permute-start.20 = (bf16[2,96,768]{2,1,0:T(8,128)(2,1)}, bf16[2,96,768]{2,1,0:T(8,128)(2,1)S(1)}, u32[]{:S(2)}, u32[]{:S(2)}) collective-permute-start(bf16[2,96,768]{2,1,0:T(8,128)(2,1)} %get-tuple-element.146), channel_id=1, source_target_pairs={{0,6},{1,7},{2,4},{3,5},{4,2},{5,3},{6,0},{7,1},{8,14},{9,15},{10,... | collective-permute-start | bytes 884744 | tf_op jit(solution)/shard_map/ppermute | solution.py:831
  303.7 2.2 collective-permute-start.21
  309.1 13.7 %collective-permute-start.22 = (bf16[104,768]{1,0:T(8,128)(2,1)}, bf16[104,768]{1,0:T(8,128)(2,1)S(1)}, u32[]{:S(2)}, u32[]{:S(2)}) collective-permute-start(bf16[104,768]{1,0:T(8,128)(2,1)} %get-tuple-element.154), channel_id=1, source_target_pairs={{0,2},{1,3},{2,0},{3,1},{4,6},{5,7},{6,4},{7,5},{8,10},{9,11},{10,... | collective-permute-start | bytes 479240 | tf_op jit(solution)/shard_map/ppermute | solution.py:831
  311.1 11.8 %collective-permute-start.23 = (bf16[104,768]{1,0:T(8,128)(2,1)}, bf16[104,768]{1,0:T(8,128)(2,1)S(1)}, u32[]{:S(2)}, u32[]{:S(2)}) collective-permute-start(bf16[104,768]{1,0:T(8,128)(2,1)} %get-tuple-element.155), channel_id=1, source_target_pairs={{0,4},{1,5},{2,6},{3,7},{4,0},{5,1},{6,2},{7,3},{8,12},{9,13},{10,... | collective-permute-start | bytes 479240 | tf_op jit(solution)/shard_map/ppermute | solution.py:831
  312.5 10.5 %collective-permute-start.24 = (bf16[104,768]{1,0:T(8,128)(2,1)}, bf16[104,768]{1,0:T(8,128)(2,1)S(1)}, u32[]{:S(2)}, u32[]{:S(2)}) collective-permute-start(bf16[104,768]{1,0:T(8,128)(2,1)} %get-tuple-element.156), channel_id=1, source_target_pairs={{0,6},{1,7},{2,4},{3,5},{4,2},{5,3},{6,0},{7,1},{8,14},{9,15},{10,... | collective-permute-start | bytes 479240 | tf_op jit(solution)/shard_map/ppermute | solution.py:831
  323.7 5.0 %copy-start.4 = (bf16[2,256,768]{2,1,0:T(8,128)(2,1)S(1)}, bf16[2,256,768]{2,1,0:T(8,128)(2,1)}, u32[]{:S(2)}) copy-start(bf16[2,256,768]{2,1,0:T(8,128)(2,1)} %copy-done.3) | copy-start | bytes 2359300
  326.4 42.2 %collective-permute-start.26 = (bf16[2,256,768]{2,1,0:T(8,128)(2,1)}, bf16[2,256,768]{2,1,0:T(8,128)(2,1)S(1)}, u32[]{:S(2)}, u32[]{:S(2)}) collective-permute-start(bf16[2,256,768]{2,1,0:T(8,128)(2,1)} %get-tuple-element.163), channel_id=1, source_target_pairs={{0,2},{1,3},{2,0},{3,1},{4,6},{5,7},{6,4},{7,5},{8,10},{9,11},{10,... | collective-permute-start | bytes 2359304 | tf_op jit(solution)/shard_map/ppermute | solution.py:831
  328.8 23.9 %collective-permute-start.8 = (bf16[256,768]{1,0:T(8,128)(2,1)S(1)}, bf16[256,768]{1,0:T(8,128)(2,1)S(1)}, u32[]{:S(2)}, u32[]{:S(2)}) collective-permute-start(bf16[256,768]{1,0:T(8,128)(2,1)S(1)} %slice_bitcast_fusion.1), channel_id=1, source_target_pairs={{0,1},{1,0},{2,3},{3,2},{4,5},{5,4},{6,7},{7,6},{8,9},{9,8},{10,11... | collective-permute-start | bytes 1179656 | tf_op jit(solution)/shard_map/ppermute | solution.py:831
  328.9 39.7 %collective-permute-start.25 = (bf16[256,768]{1,0:T(8,128)(2,1)}, bf16[256,768]{1,0:T(8,128)(2,1)S(1)}, u32[]{:S(2)}, u32[]{:S(2)}) collective-permute-start(bf16[256,768]{1,0:T(8,128)(2,1)} %get-tuple-element.162), channel_id=1, source_target_pairs={{0,1},{1,0},{2,3},{3,2},{4,5},{5,4},{6,7},{7,6},{8,9},{9,8},{10,11... | collective-permute-start | bytes 1179656 | tf_op jit(solution)/shard_map/ppermute | solution.py:831
  329.4 10.7 %collective-permute-start.28 = (bf16[80,768]{1,0:T(8,128)(2,1)}, bf16[80,768]{1,0:T(8,128)(2,1)S(1)}, u32[]{:S(2)}, u32[]{:S(2)}) collective-permute-start(bf16[80,768]{1,0:T(8,128)(2,1)} %get-tuple-element.166), channel_id=1, source_target_pairs={{0,8},{1,9},{2,10},{3,11},{4,12},{5,13},{6,14},{7,15},{8,0},{9,1},... | collective-permute-start | bytes 368648 | tf_op jit(solution)/shard_map/ppermute | solution.py:831
  329.6 12.1 %collective-permute-start.29 = (bf16[80,768]{1,0:T(8,128)(2,1)}, bf16[80,768]{1,0:T(8,128)(2,1)S(1)}, u32[]{:S(2)}, u32[]{:S(2)}) collective-permute-start(bf16[80,768]{1,0:T(8,128)(2,1)} %get-tuple-element.167), channel_id=1, source_target_pairs={{0,16},{1,17},{2,18},{3,19},{4,20},{5,21},{6,22},{7,23},{8,24},{9,... | collective-permute-start | bytes 368648 | tf_op jit(solution)/shard_map/ppermute | solution.py:831
  340.1 7.4 %copy-start.33 = (bf16[80,768]{1,0:T(8,128)(2,1)}, bf16[80,768]{1,0:T(8,128)(2,1)S(1)}, u32[]{:S(2)}) copy-start(bf16[80,768]{1,0:T(8,128)(2,1)S(1)} %collective-permute-done.28.refs_1_) | copy-start | bytes 368644
  340.1 7.4 %collective-permute-start.30 = (bf16[80,768]{1,0:T(8,128)(2,1)}, bf16[80,768]{1,0:T(8,128)(2,1)S(1)}, u32[]{:S(2)}, u32[]{:S(2)}) collective-permute-start(bf16[80,768]{1,0:T(8,128)(2,1)} %get-tuple-element.168), channel_id=1, source_target_pairs={{0,24},{1,25},{2,26},{3,27},{4,28},{5,29},{6,30},{7,31},{8,16},{9,... | collective-permute-start | bytes 368648 | tf_op jit(solution)/shard_map/ppermute | solution.py:831
  341.7 5.8 %copy-start.34 = (bf16[80,768]{1,0:T(8,128)(2,1)}, bf16[80,768]{1,0:T(8,128)(2,1)S(1)}, u32[]{:S(2)}) copy-start(bf16[80,768]{1,0:T(8,128)(2,1)S(1)} %collective-permute-done.29.refs_2_) | copy-start | bytes 368644
  350.1 13.1 %collective-permute-start.31 = (bf16[1,3,24,768]{3,2,1,0:T(8,128)(2,1)}, bf16[1,3,24,768]{3,2,1,0:T(8,128)(2,1)S(1)}, u32[]{:S(2)}, u32[]{:S(2)}) collective-permute-start(bf16[1,3,24,768]{3,2,1,0:T(8,128)(2,1)} %bitcast.31), channel_id=1, source_target_pairs={{0,8},{1,9},{2,10},{3,11},{4,12},{5,13},{6,14},{7,15},{8,0},{9,1},... | collective-permute-start | bytes 331784 | tf_op jit(solution)/shard_map/ppermute | solution.py:831
  352.7 11.3 %collective-permute-start.32 = (bf16[1,3,24,768]{3,2,1,0:T(8,128)(2,1)}, bf16[1,3,24,768]{3,2,1,0:T(8,128)(2,1)S(1)}, u32[]{:S(2)}, u32[]{:S(2)}) collective-permute-start(bf16[1,3,24,768]{3,2,1,0:T(8,128)(2,1)} %bitcast.32), channel_id=1, source_target_pairs={{0,16},{1,17},{2,18},{3,19},{4,20},{5,21},{6,22},{7,23},{8,24},{9,... | collective-permute-start | bytes 331784 | tf_op jit(solution)/shard_map/ppermute | solution.py:831
  352.7 2.4 copy-start.21
  352.7 15.9 %collective-permute-start.33 = (bf16[1,3,24,768]{3,2,1,0:T(8,128)(2,1)}, bf16[1,3,24,768]{3,2,1,0:T(8,128)(2,1)S(1)}, u32[]{:S(2)}, u32[]{:S(2)}) collective-permute-start(bf16[1,3,24,768]{3,2,1,0:T(8,128)(2,1)} %bitcast.33), channel_id=1, source_target_pairs={{0,24},{1,25},{2,26},{3,27},{4,28},{5,29},{6,30},{7,31},{8,16},{9,... | collective-permute-start | bytes 331784 | tf_op jit(solution)/shard_map/ppermute | solution.py:831
  363.2 5.4 %copy-start.36 = (bf16[1,3,24,768]{3,2,1,0:T(8,128)(2,1)}, bf16[1,3,24,768]{3,2,1,0:T(8,128)(2,1)S(1)}, u32[]{:S(2)}) copy-start(bf16[1,3,24,768]{3,2,1,0:T(8,128)(2,1)S(1)} %collective-permute-done.31.refs_1_) | copy-start | bytes 331780
  364.0 4.6 %copy-start.37 = (bf16[1,3,24,768]{3,2,1,0:T(8,128)(2,1)}, bf16[1,3,24,768]{3,2,1,0:T(8,128)(2,1)S(1)}, u32[]{:S(2)}) copy-start(bf16[1,3,24,768]{3,2,1,0:T(8,128)(2,1)S(1)} %collective-permute-done.32.refs_2_) | copy-start | bytes 331780
  372.1 20.2 %collective-permute-start.34 = (bf16[4,3,24,768]{3,2,1,0:T(8,128)(2,1)}, bf16[4,3,24,768]{3,2,1,0:T(8,128)(2,1)S(1)}, u32[]{:S(2)}, u32[]{:S(2)}) collective-permute-start(bf16[4,3,24,768]{3,2,1,0:T(8,128)(2,1)} %stack_line.1.refs_0_), channel_id=1, source_target_pairs={{0,2},{1,3},{2,0},{3,1},{4,6},{5,7},{6,4},{7,5},{8,10},{9,11},{10,... | collective-permute-start | bytes 1327112 | tf_op jit(solution)/shard_map/ppermute | solution.py:831
  373.6 20.9 %collective-permute-start.35 = (bf16[4,3,24,768]{3,2,1,0:T(8,128)(2,1)}, bf16[4,3,24,768]{3,2,1,0:T(8,128)(2,1)S(1)}, u32[]{:S(2)}, u32[]{:S(2)}) collective-permute-start(bf16[4,3,24,768]{3,2,1,0:T(8,128)(2,1)} %stack_line.1.refs_0_), channel_id=1, source_target_pairs={{0,4},{1,5},{2,6},{3,7},{4,0},{5,1},{6,2},{7,3},{8,12},{9,13},{10,... | collective-permute-start | bytes 1327112 | tf_op jit(solution)/shard_map/ppermute | solution.py:831
  375.2 19.4 %collective-permute-start.36 = (bf16[4,3,24,768]{3,2,1,0:T(8,128)(2,1)}, bf16[4,3,24,768]{3,2,1,0:T(8,128)(2,1)S(1)}, u32[]{:S(2)}, u32[]{:S(2)}) collective-permute-start(bf16[4,3,24,768]{3,2,1,0:T(8,128)(2,1)} %stack_line.1.refs_0_), channel_id=1, source_target_pairs={{0,6},{1,7},{2,4},{3,5},{4,2},{5,3},{6,0},{7,1},{8,14},{9,15},{10,... | collective-permute-start | bytes 1327112 | tf_op jit(solution)/shard_map/ppermute | solution.py:831
  392.3 2.3 copy-start.16
  395.5 3.4 copy-start.6
  395.5 4.0 copy-start.39
  395.5 5.3 %copy-start.44 = (f32[1,768]{1,0:T(1,128)S(1)}, f32[1,768]{1,0:T(1,128)}, u32[]{:S(2)}) copy-start(f32[1,768]{1,0:T(1,128)} %get-tuple-element.175) | copy-start | bytes 9220
  398.3 7.7 %collective-permute-start.37 = (bf16[16,3,24,768]{3,2,1,0:T(8,128)(2,1)}, bf16[16,3,24,768]{3,2,1,0:T(8,128)(2,1)S(1)}, u32[]{:S(2)}, u32[]{:S(2)}) collective-permute-start(bf16[16,3,24,768]{3,2,1,0:T(8,128)(2,1)} %stack_plane.1.own), channel_id=1, source_target_pairs={{0,1},{1,0},{2,3},{3,2},{4,5},{5,4},{6,7},{7,6},{8,9},{9,8},{10,11... | collective-permute-start | bytes 5308424 | tf_op jit(solution)/shard_map/ppermute | solution.py:831
  398.9 3.6 collective-permute-start.27
  406.0 1.2 copy-start.8
  407.2 9.8 %copy-start.1 = (s32[4,1024]{1,0:T(4,128)S(1)}, s32[4,1024]{1,0:T(4,128)}, u32[]{:S(2)}) copy-start(s32[4,1024]{1,0:T(4,128)} %param.14) | copy-start | bytes 49156
  (24 other events, 18.6 us)
Sparse Core Ops, SparseCore 0:
  262.4 103.4 all-gather.2
where the time goes:
time: 428 us; the launch traced here: 424 us
  Pallas kernels  273 us (64%)
  waiting for transfers between devices  61.5 us (14%)
  starting transfers between devices  49.1 us (11%)
  local copies, waits for them, and re-layouts  21.1 us (5%)
  between operations  14.8 us (3%)
  other arithmetic  4.88 us (1%)
    pallas_call x12, Pallas kernels, step_call(): pl.pallas_call(kernel, grid_spec=pltpu.PrefetchScalarGridSpec(num_scalar_...  114 us
    pallas_call x3, Pallas kernels, run(): pl.pallas_call(kernel, grid=(heads // BACKWARD_HEADS,), in_specs=in_specs...  76.7 us
    ppermute x38, waiting for transfers between devices, swap(): return lax.ppermute(values, BOTH, [(s, s ^ mask) for s in range(n)])  61.5 us
    pallas_call x1, Pallas kernels, attend(): pl.pallas_call(attend_kernel, grid=(H // heads,), in_specs=[SMEM, SMEM, w...  41.4 us
    ppermute x38, starting transfers between devices, swap(): return lax.ppermute(values, BOTH, [(s, s ^ mask) for s in range(n)])  41 us
    pallas_call x9, Pallas kernels, plain_call(): pl.pallas_call(kernel, in_specs=[SMEM] + [VMEM] * len(operands) + [ANY] *...  23.7 us
    pallas_call x1, Pallas kernels, fill(): pl.pallas_call(partial(fill_kernel, tuple((d * o for d, o in zip(down, ov...  16.7 us
    unnamed x95, local copies, waits for them, and re-layouts  16 us
  transfers between devices with their start and end apart: 41, of which 14 were waited for; matrix products, arithmetic and copies ran while one was open for 2% of the time, Pallas kernels for 45%

commit v1 on v0

--- a/solution.py
+++ b/solution.py
@@ -552,23 +552,43 @@
         [shape((count, rows // ways, D))] * ways, 0, name, [pltpu.VMEM((1, rows, D), F32)])
 
 
-def lay_out_kernel(waits, mine, kept, came, *refs):
-    out = refs[waits]
-    ways, _, rows, _ = out.shape
-    for m in range(kept.shape[0]):
-        total = kept[m].astype(F32) + came[m].astype(F32)
-        for c in range(ways):
-            out[c, m] = total[c * rows : (c + 1) * rows, :].astype(BF16)
-
-
-def lay_out(mine, kept, came, ways, per_step, name, first=()):
-    count, rows, _ = kept.shape
-    block = pl.BlockSpec((per_step, rows, D), lambda m, mine: (m, 0, 0))
-    return step_call(
-        partial(lay_out_kernel, len(first)), mine, count // per_step, [block, block] + [ANY] * len(first),
-        (kept, came, *first),
-        pl.BlockSpec((ways, per_step, rows // ways, D), lambda m, mine: (0, m, 0, 0)),
-        shape((ways, count, rows // ways, D)), 0, name)
+def shares_kernel(wide_steps, mine, wide_kept, wide_came, thin_kept, thin_came, wide, *refs):
+    thin, total, step = refs[:-1], refs[-1], pl.program_id(0)
+
+    @pl.when(step < wide_steps)
+    def of_wide():
+        rows = wide.shape[2]
+        for m in range(wide_kept.shape[0]):
+            sums = wide_kept[m].astype(F32) + wide_came[m].astype(F32)
+            for c in range(wide.shape[0]):
+                wide[c, m] = sums[c * rows : (c + 1) * rows, :].astype(BF16)
+
+    @pl.when(step >= wide_steps)
+    def of_thin():
+        total[...] = thin_kept[...].astype(F32) + thin_came[...].astype(F32)
+        for c, out in enumerate(thin):
+            rows = out.shape[1]
+            out[...] = total[:, pl.ds(pl.multiple_of((mine[0] ^ c) * rows, 8), rows), :].astype(BF16)
+
+
+def shares_of(mine, wide_kept, wide_came, thin_kept, thin_came, plane, line, first):
+    count, left = wide_kept.shape[0], thin_kept.shape[0]
+    per_step = 2
+    steps = count // per_step
+
+    def of_wide(m, mine):
+        return jnp.minimum(m, steps - 1)
+
+    half = pl.BlockSpec((per_step, HALF, D), lambda m, mine: (of_wide(m, mine), 0, 0))
+    thin_half = fixed((left, HALF, D))
+    outs = step_call(
+        lambda mine, a, b, c, d, *refs: shares_kernel(steps, mine, a, b, c, d, *refs[len(first) :]), mine, steps + 1,
+        [half, half, thin_half, thin_half] + [ANY] * len(first), (wide_kept, wide_came, thin_kept, thin_came, *first),
+        [pl.BlockSpec((plane, per_step, HALF // plane, D), lambda m, mine: (0, of_wide(m, mine), 0, 0))]
+        + [fixed((left, HALF // line, D))] * line,
+        [shape((plane, count, HALF // plane, D))] + [shape((left, HALF // line, D))] * line, 0, "shares",
+        [pltpu.VMEM((left, HALF, D), F32)])
+    return outs[0], outs[1:]
 
 
 def plain_call(kernel, operands, mine, out_shape, name, scratch=(), first=(), through=()):
@@ -594,7 +614,7 @@
 
 
 def reshare_kernel(line, waits, mine, wide, *refs):
-    thin, outs, total = refs[:line], refs[line + waits : -1], refs[-1]
+    thin, outs, total = refs[:line], refs[line + waits :], refs[-1]
     total[...] = sum_first(wide)
     for c in range(line):
         rows = outs[c].shape[1]
@@ -605,14 +625,14 @@
         out[c] = thin_sum[:, c * rows : (c + 1) * rows, :].astype(BF16)
 
 
-def reshare(mine, wide, thin, first):
+def reshare(mine, wide, thin, first, through):
     plane, count, rows, _ = wide.shape
     line, (left, thin_rows, _) = len(thin), thin[0].shape
-    outs, _ = plain_call(
-        partial(reshare_kernel, line, len(first)), [wide, *thin], mine,
+    outs, through = plain_call(
+        partial(reshare_kernel, line, len(first) + len(through)), [wide, *thin], mine,
         [shape((count, rows // line, D))] * line + [shape((plane, left, thin_rows // plane, D))], "reshare",
-        [pltpu.VMEM((count, rows, D), F32)], first)
-    return outs[:line], outs[line]
+        [pltpu.VMEM((count, rows, D), F32)], first, through)
+    return outs[:line], outs[line], through
 
 
 def piece_kernel(line, waits, mine, thin, *refs):
@@ -890,13 +910,13 @@
     return stack(mine, exchange([values] * (1 << len(dims)), dims), name, first)
 
 
-def send_tokens(parts):
+def send_far(parts):
+    return (*parts[:2], swap(parts[2], 2))
+
+
+def hand_on(parts):
     mine, near, far = parts
-    return mine, swap(near, 1), swap(far, 2)
-
-
-def hand_on(came):
-    return (*came, swap(came[2][1], 1))
+    return mine, swap(near, 1), far, swap(far[1], 1)
 
 
 def per_device(
@@ -917,6 +937,9 @@
     plane, line, others = chip_groups()
     where = jnp.stack([place([1]), place(plane), place(line)])
     core, spots = where[:1], where[1:]
+    mixed = plane + line
+    pair_plane, pair_line = mixed[1:3], mixed[:1] + mixed[3:]
+    pair_spots = jnp.stack([place(pair_plane), place(pair_line)])
     sizes = (1 << len(plane), 1 << len(line))
     parts, seq = lax.axis_size("seq"), lax.axis_index("seq")
     row_bits, at = device_bits()[: parts.bit_length() - 1], seq.reshape(1)
@@ -928,45 +951,45 @@
 
     came = exchange([lax.dynamic_index_in_dim(inputs, seq ^ i, 0, keepdims=False) for i in range(parts)], row_bits)
     near = parts // 2
-    begun = project(at, came[:near], 0, gain_one, w_query, w_key, w_value)
-    done = project(at, came[near:], near, gain_one, w_query, w_key, w_value, begun, cotangent)
-    (x, normed_t, q, q_t, k, k_t, v, v_t), cots = done[:8], exchange(done[8:], row_bits)
+    begun = project(at, came[:near], 0, gain_one, w_query, w_key, w_value, (), cotangent)
+    cots = exchange(begun[8:], row_bits)
+    x, normed_t, q, q_t, k, k_t, v, v_t = project(
+        at, came[near:], near, gain_one, w_query, w_key, w_value, begun[:8])
     soft, attended = attend(mix_l, mix_w, ids, q_t, k, v_t)
     out, (cot, normed_two, activated, grad_hidden, grad_middle, grad_attn, g, g_t) = feed(
         at, x, attended, cots, w_out, w_hidden, w_back, gain_two
     )
-    out = send_tokens(out)
     wide_kept, wide_sent = wide_weight_grads(core, activated, cot, normed_two, grad_hidden)
-    thin_kept, thin_sent = thin_weight_grads(core, normed_two, grad_hidden, attended, grad_attn, [wide_kept, *out[1:]])
-    wide = lay_out(core, wide_kept, swap(wide_sent, 1), sizes[0], 2, "lay_out_wide", [thin_kept])
-    thin = split(spots[1:], thin_kept, swap(thin_sent, 1), sizes[1], "split_thin", [wide])
+    thin_kept, thin_sent = thin_weight_grads(core, normed_two, grad_hidden, attended, grad_attn, [wide_kept])
+    wide, thin = shares_of(
+        spots[1:], wide_kept, swap(wide_sent, 1), thin_kept, swap(thin_sent, 1), sizes[0], sizes[1], [thin_kept])
     grad_q, grad_logits, by_logits = query_grads(mix_w, mix_l, soft, v, g_t, k_t, q_t, [wide, thin[0]])
-    wide, thin = reshare(spots, trade(wide, plane), exchange(thin, line), [grad_q])
+    wide, thin, far = reshare(spots, trade(wide, plane), exchange(thin, line), [grad_q], out[2:])
+    out = send_far((*out[:2], *far))
     grad_k = key_grads(mix_l, grad_logits, q, [wide[0]])
-    pair_kept, pair_sent = project_weight_grads(core, normed_t, [grad_q, grad_k])
-    out = hand_on(out)
-    piece, _ = piece_of(spots, exchange(wide, line), trade(thin, plane), [grad_k], [])
+    piece, far = piece_of(spots, exchange(wide, line), trade(thin, plane), [grad_k], out[2:])
+    out = hand_on((*out[:2], *far))
     pieces = lax.all_gather(finish_sum(piece, others), BOTH, axis=0)
     pair_kept, pair_sent = project_weight_grads(core, normed_t, [grad_q, grad_k], (), [piece])
-    pair = split(spots[:1], pair_kept, swap(pair_sent, 1), sizes[0], "split_pair")
+    pair = split(pair_spots[:1], pair_kept, swap(pair_sent, 1), sizes[0], "split_pair")
     grad_v, by_weights = value_grads(mix_w, soft, v, g, [piece, pair[0]])
-    pair = exchange(pair, plane)
-    one_kept, one_sent = project_weight_grads(core, normed_t, [grad_v], [by_logits, by_weights], pair[1:])
-    one = split_small(spots[:1], one_kept, swap(one_sent, 1), sizes[0], "split_one")
+    pair = exchange(pair, pair_plane)
+    one_kept, one_sent = project_weight_grads(core, normed_t, [grad_v], [by_logits, by_weights], [*pair[1:], out[1], out[3]])
+    one = split_small(pair_spots[:1], one_kept, swap(one_sent, 1), sizes[0], "split_one")
     grad_in = input_grads(
         at, parts, grad_q, grad_k, grad_v, x, grad_middle, w_query, w_key, w_value, gain_one, one[0])
-    shares, grad_in = project_reshare(spots, pair, exchange(one, plane), sizes[1], grad_in)
-    own, small = project_piece(spots, exchange(shares, line))
+    shares, grad_in = project_reshare(pair_spots, pair, exchange(one, pair_plane), sizes[1], grad_in)
+    own, small = project_piece(pair_spots, exchange(shares, pair_line))
     own, small = finish_sum(own, others)[None], finish_sum(small, others)
     block_out = tokens_of(at, out, "block_out")
-    grad_in = send_tokens(grad_in)
-    own = widen(spots, own, line, "stack_line", [block_out, *grad_in[1:]])
+    grad_in = send_far(grad_in)
+    own = widen(spots, own, pair_line, "stack_line", [block_out, grad_in[2]])
     grad_w_back, grad_w_hidden, grad_w_out, grad_gain_two = fill(
         pieces, (row_starts(plane, line), row_starts(line, plane)), w_hidden, gain_two)
     grad_inputs = tokens_of(at, hand_on(grad_in), "grad_inputs", [grad_w_out])
-    own = widen(spots, own, plane, "stack_plane", [grad_w_out])
+    own = widen(spots, own, pair_plane, "stack_plane", [grad_w_out])
     grad_w_query, grad_w_key, grad_w_value, grad_gain_one = spread(
-        where, sizes, own, swap(own, 1), w_query, w_key, w_value, gain_one, [grad_w_out])
+        jnp.stack([core[0], *pair_spots]), sizes, own, swap(own, 1), w_query, w_key, w_value, gain_one, [grad_w_out])
     small = small[:, : 3 * 128].reshape(SMALL_ROWS, 3, 128).transpose(1, 0, 2).reshape(2, H, 128)[:, :, :H]
     return (
         block_out,

time: 428 us -> 413 us (0.965)
  waiting for transfers between devices: 61.5 us -> 48.1 us
    ppermute x38, waiting for transfers between devices: 61.5 us -> 48 us  [swap(): return lax.ppermute(values, BOTH, [(s, s ^ mask) for s in range(n)])]
    pallas_call x12 -> x11, Pallas kernels: 114 us -> 113 us  [step_call(): pl.pallas_call(kernel, grid_spec=pltpu.PrefetchScalarGridSpec(num_scalar_...]
  transfers between devices with their start and end apart: 41 -> 41, of which waited for: 14 -> 12; matrix products, arithmetic and copies ran while one was open for 2% -> 2% of each run, Pallas kernels for 45% -> 48%
where the time goes in v1:
time: 413 us; the launch traced here: 409 us
  Pallas kernels  271 us (66%)
  waiting for transfers between devices  48.1 us (12%)
  starting transfers between devices  47.7 us (12%)
  local copies, waits for them, and re-layouts  21.9 us (5%)
  between operations  14.8 us (4%)
  other arithmetic  5.48 us (1%)
    pallas_call x11, Pallas kernels, step_call(): pl.pallas_call(kernel, grid_spec=pltpu.PrefetchScalarGridSpec(num_scalar_...  113 us
    pallas_call x3, Pallas kernels, run(): pl.pallas_call(kernel, grid=(heads // BACKWARD_HEADS,), in_specs=in_specs...  76.7 us
    ppermute x38, waiting for transfers between devices, swap(): return lax.ppermute(values, BOTH, [(s, s ^ mask) for s in range(n)])  48 us
    pallas_call x1, Pallas kernels, attend(): pl.pallas_call(attend_kernel, grid=(H // heads,), in_specs=[SMEM, SMEM, w...  41.3 us
    ppermute x38, starting transfers between devices, swap(): return lax.ppermute(values, BOTH, [(s, s ^ mask) for s in range(n)])  39.8 us
    pallas_call x9, Pallas kernels, plain_call(): pl.pallas_call(kernel, in_specs=[SMEM] + [VMEM] * len(operands) + [ANY] *...  23.6 us
    unnamed x95, local copies, waits for them, and re-layouts  16.8 us
    pallas_call x1, Pallas kernels, fill(): pl.pallas_call(partial(fill_kernel, tuple((d * o for d, o in zip(down, ov...  16.7 us
  transfers between devices with their start and end apart: 41, of which 12 were waited for; matrix products, arithmetic and copies ran while one was open for 2% of the time, Pallas kernels for 48%

profile of v1, /device:TPU:0, one launch (start us, length us, event | category | flops | bytes accessed | tf_op | source)
XLA Modules:
  0.0 408.9 jit_solution(8532274303331673139)
XLA Ops:
  7.3 2.2 dynamic-slice_bitcast_fusion
  9.9 2.5 collective-permute-start
  13.2 1.0 copy.41.id_col
  16.8 7.7 %project.2 = (bf16[1024,768]{1,0:T(8,128)(2,1)}, bf16[768,1024]{1,0:T(8,128)(2,1)}, bf16[1024,768]{1,0:T(8,128)(2,1)}, bf16[768,1024]{1,0:T(8,128)(2,1)}, bf16[1...) custom-call(s32[1]{0:T(128)} %bitcast.at, ...), custom_call_target="tpu_custom_call" | custom-call | flops 226492416 | bytes 786432 | tf_op jit(solution)/shard_map/project/pallas_call | solution.py:296
  24.7 1.9 collective-permute-start.4
  27.2 3.3 collective-permute-done.1.refs_1_
  31.2 6.1 %project.3 = (bf16[1024,768]{1,0:T(8,128)(2,1)}, bf16[768,1024]{1,0:T(8,128)(2,1)}, bf16[1024,768]{1,0:T(8,128)(2,1)}, bf16[768,1024]{1,0:T(8,128)(2,1)}, bf16[1...) custom-call(s32[1]{0:T(128)} %bitcast.at, ...), custom_call_target="tpu_custom_call", output_to_operand_aliasing={{0}: (7, {}), {1}: (8, {}), {2}: (9, {}), {3}: (10, {}), {4... | custom-call | flops 226492416 | bytes 786432 | tf_op jit(solution)/shard_map/project/pallas_call | solution.py:296
  37.3 41.3 %attend.1 = (bf16[12,1024,1024]{2,1,0:T(8,128)(2,1)}, bf16[1024,768]{1,0:T(8,128)(2,1)}) custom-call(f32[12,12]{1,0:T(8,128)} %convert_multiply_fusion.mix_l, f32[12,12]{1,0:T(8,128)} %convert_element_type.7.mix_w, s32[1,1024]{1,0:T(1,128)} %constant_dynamic-slice_fusion.id_row, s32[1024,1]{1,0:T(8,128)} %copy.41.id_col, ...), custom_call_target="tpu_custom_call" | custom-call | flops 3019898880 | bytes 1048576 | tf_op jit(solution)/shard_map/attend/pallas_call | solution.py:86
  79.7 36.7 %feed.1 = (bf16[256,768]{1,0:T(8,128)(2,1)}, bf16[256,768]{1,0:T(8,128)(2,1)}, bf16[2,256,768]{2,1,0:T(8,128)(2,1)}, bf16[1024,768]{1,0:T(8,128)(2,1)}, bf16[102...) custom-call(s32[1]{0:T(128)} %bitcast.at, ...), custom_call_target="tpu_custom_call" | custom-call | flops 2717908992 | bytes 786432 | tf_op jit(solution)/shard_map/feed/pallas_call | solution.py:296
  116.4 13.6 %wide_weight_grads.1 = (bf16[6,384,768]{2,1,0:T(8,128)(2,1)}, bf16[6,384,768]{2,1,0:T(8,128)(2,1)}) custom-call(s32[1]{0:T(128)} %bitcast.8.core, bf16[1024,3072]{1,0:T(8,128)(2,1)} %get-tuple-element.118.act_kept.act_sent, bf16[1024,3072]{1,0:T(8,128)(2,1)} %get-tuple-element.118.act_kept.act_sent, bf16[1024,768]{1,0:T(8,128)(2,1)} %get-tuple-element.119.cot, ...), custom_call_target="tpu_custom_call" | custom-call | flops 905969664 | bytes 786432 | tf_op jit(solution)/shard_map/wide_weight_grads/pallas_call | solution.py:296
  130.2 8.2 %thin_weight_grads.1 = (bf16[3,384,768]{2,1,0:T(8,128)(2,1)}, bf16[3,384,768]{2,1,0:T(8,128)(2,1)}) custom-call(s32[1]{0:T(128)} %bitcast.8.core, bf16[1024,768]{1,0:T(8,128)(2,1)} %get-tuple-element.120.n2_kept.n2_sent, bf16[1024,768]{1,0:T(8,128)(2,1)} %get-tuple-element.120.n2_kept.n2_sent, bf16[1024,3072]{1,0:T(8,128)(2,1)} %get-tuple-element.121.grad_hidden, ...), custom_call_target="tpu_custom_call" | custom-call | flops 452984832 | bytes 786432 | tf_op jit(solution)/shard_map/thin_weight_grads/pallas_call | solution.py:296
  138.7 3.7 collective-permute-done.8.d
  142.4 1.8 copy-done.7
  144.2 8.3 %shares.1 = (bf16[4,6,96,768]{3,2,1,0:T(8,128)(2,1)}, bf16[3,96,768]{2,1,0:T(8,128)(2,1)}, bf16[3,96,768]{2,1,0:T(8,128)(2,1)}, bf16[3,96,768]{2,1,0:T(8,128)(2,1)}, bf16[3,96,768]{2,1,0:T(8,128)(2,1)}) custom-call(s32[1]{0:T(128)} %bitcast.7.mine, bf16[6,384,768]{2,1,0:T(8,128)(2,1)} %get-tuple-element.122.refs_0_.a, bf16[6,384,768]{2,1,0:T(8,128)(2,1)} %copy-done.7, ...), custom_call_target="tpu_custom_call" | custom-call | bytes 786432 | tf_op jit(solution)/shard_map/shares/pallas_call | solution.py:296
  152.5 4.4 %all-to-all-start = ((bf16[4,6,96,768]{3,2,1,0:T(8,128)(2,1)}), bf16[4,6,96,768]{3,2,1,0:T(8,128)(2,1)S(1)}, u32[]{:S(2)}, u32[]{:S(2)}) async-start(bf16[4,6,96,768]{3,2,1,0:T(8,128)(2,1)} %get-tuple-element.127.rest_0_), calls=%async_computation | async-start | bytes 7077888 | tf_op jit(solution)/shard_map/all_to_all | solution.py:906
  156.8 2.7 collective-permute-start.10
  159.5 1.3 collective-permute-start.11
  161.7 39.4 %query_grads.1 = (bf16[1024,768]{1,0:T(8,128)(2,1)}, bf16[12,1024,1024]{2,1,0:T(8,128)(2,1)}, f32[12,1,768]{2,1,0:T(1,128)}) custom-call(f32[12,12]{1,0:T(8,128)} %convert_element_type.7.mix_w, f32[12,12]{1,0:T(8,128)} %convert_multiply_fusion.mix_l, bf16[12,1024,1024]{2,1,0:T(8,128)(2,1)} %get-tuple-element.132.soft, ...), custom_call_target="tpu_custom_call" | custom-call | flops 3019898880 | bytes 1048576 | tf_op jit(solution)/shard_map/query_grads/pallas_call | solution.py:198
  201.1 1.8 copy-done.2
  202.9 4.5 %reshare.1 = (bf16[6,24,768]{2,1,0:T(8,128)(2,1)}, bf16[6,24,768]{2,1,0:T(8,128)(2,1)}, bf16[6,24,768]{2,1,0:T(8,128)(2,1)}, bf16[6,24,768]{2,1,0:T(8,128)(2,1)}...) custom-call(s32[2]{0:T(128)} %pad_add_fusion.mine, ...), custom_call_target="tpu_custom_call", output_to_operand_aliasing={{5}: (7, {})} | custom-call | tf_op jit(solution)/shard_map/reshare/pallas_call | solution.py:595
  207.4 2.0 collective-permute-start.15
  209.4 3.5 all-to-all-start.1
  212.9 1.9 collective-permute-start.12
  214.8 1.7 collective-permute-start.13
  216.5 0.9 collective-permute-start.14
  217.4 17.8 %key_grads.1.refs_4_.refs_1_.grad_k = bf16[1024,768]{1,0:T(8,128)(2,1)} custom-call(f32[12,12]{1,0:T(8,128)} %convert_multiply_fusion.mix_l, bf16[12,1024,1024]{2,1,0:T(8,128)(2,1)} %get-tuple-element.143.grad_logits, bf16[1024,768]{1,0:T(8,128)(2,1)} %get-tuple-element.144.q, bf16[6,24,768]{2,1,0:T(8,128)(2,1)} %get-tuple-element.139.rest_0_.refs_0_), custom_call_target="tpu_custom_call" | custom-call | flops 1509949440 | bytes 1048576 | tf_op jit(solution)/shard_map/key_grads/pallas_call | solution.py:198
  236.2 0.9 copy-done.5
  237.1 2.3 piece.1
  239.4 6.3 %project_weight_grads.2 = (bf16[2,384,768]{2,1,0:T(8,128)(2,1)}, bf16[2,384,768]{2,1,0:T(8,128)(2,1)}) custom-call(s32[1]{0:T(128)} %bitcast.8.core, bf16[768,1024]{1,0:T(8,128)(2,1)} %get-tuple-element.147.nt_kept.nt_sent, bf16[768,1024]{1,0:T(8,128)(2,1)} %get-tuple-element.147.nt_kept.nt_sent, ...), custom_call_target="tpu_custom_call" | custom-call | flops 301989888 | bytes 786432 | tf_op jit(solution)/shard_map/project_weight_grads/pallas_call | solution.py:296
  246.4 3.3 collective-permute-done.17.came
  249.7 1.0 copy-done.15
  250.7 2.6 split_pair.1
  253.3 1.9 collective-permute-start.18
  255.2 0.9 collective-permute-start.19
  256.8 19.5 %value_grads.1 = (bf16[1024,768]{1,0:T(8,128)(2,1)}, f32[12,1,768]{2,1,0:T(1,128)}) custom-call(f32[12,12]{1,0:T(8,128)} %convert_element_type.7.mix_w, bf16[12,1024,1024]{2,1,0:T(8,128)(2,1)} %get-tuple-element.132.soft, bf16[1024,768]{1,0:T(8,128)(2,1)} %get-tuple-element.133.v, bf16[1024,768]{1,0:T(8,128)(2,1)} %get-tuple-element.155.g, ...), custom_call_target="tpu_custom_call" | custom-call | flops 1509949440 | bytes 1048576 | tf_op jit(solution)/shard_map/value_grads/pallas_call | solution.py:198
  276.4 2.9 collective-permute-done.20.refs_5_.refs_3_
  280.0 4.5 %project_weight_grads.3 = (bf16[1,400,768]{2,1,0:T(8,128)(2,1)}, bf16[1,400,768]{2,1,0:T(8,128)(2,1)}) custom-call(s32[1]{0:T(128)} %bitcast.8.core, bf16[768,1024]{1,0:T(8,128)(2,1)} %get-tuple-element.147.nt_kept.nt_sent, bf16[768,1024]{1,0:T(8,128)(2,1)} %get-tuple-element.147.nt_kept.nt_sent, bf16[1024,768]{1,0:T(8,128)(2,1)} %get-tuple-element.156.refs_0_.grad_v, ...), custom_call_target="tpu_custom_call" | custom-call | flops 150994944 | bytes 786432 | tf_op jit(solution)/shard_map/project_weight_grads/pallas_call | solution.py:296
  284.5 2.2 collective-permute-done.21.came
  287.6 2.3 split_one.1
  290.1 3.3 collective-permute-start.24
  294.0 10.1 %input_grads.1 = (bf16[256,768]{1,0:T(8,128)(2,1)}, bf16[256,768]{1,0:T(8,128)(2,1)}, bf16[2,256,768]{2,1,0:T(8,128)(2,1)}) custom-call(s32[1]{0:T(128)} %bitcast.at, bf16[1024,768]{1,0:T(8,128)(2,1)} %get-tuple-element.136.refs_4_.refs_0_.grad_q, bf16[1024,768]{1,0:T(8,128)(2,1)} %key_grads.1.refs_4_.refs_1_.grad_k, ...), custom_call_target="tpu_custom_call" | custom-call | flops 452984832 | bytes 786432 | tf_op jit(solution)/shard_map/input_grads/pallas_call | solution.py:296
  304.1 10.5 %collective-permute-done.24.refs_7_ = bf16[104,768]{1,0:T(8,128)(2,1)S(1)} collective-permute-done((bf16[104,768]{1,0:T(8,128)(2,1)}, bf16[104,768]{1,0:T(8,128)(2,1)S(1)}, u32[]{:S(2)}, u32[]{:S(2)}) %collective-permute-start.24) | collective-permute-done | bytes 159776 | tf_op jit(solution)/shard_map/ppermute | solution.py:851
  315.3 2.6 project_reshare.1
  317.9 2.2 collective-permute-start.26
  320.2 4.3 %collective-permute-start.30 = (bf16[80,768]{1,0:T(8,128)(2,1)}, bf16[80,768]{1,0:T(8,128)(2,1)S(1)}, u32[]{:S(2)}, u32[]{:S(2)}) collective-permute-start(bf16[80,768]{1,0:T(8,128)(2,1)} %get-tuple-element.176), channel_id=1, source_target_pairs={{0,18},{1,19},{2,16},{3,17},{4,22},{5,23},{6,20},{7,21},{8,26},{9,... | collective-permute-start | bytes 368648 | tf_op jit(solution)/shard_map/ppermute | solution.py:851
  324.6 13.7 %collective-permute-done.28.refs_1_ = bf16[80,768]{1,0:T(8,128)(2,1)S(1)} collective-permute-done((bf16[80,768]{1,0:T(8,128)(2,1)}, bf16[80,768]{1,0:T(8,128)(2,1)S(1)}, u32[]{:S(2)}, u32[]{:S(2)}) %collective-permute-start.28) | collective-permute-done | bytes 122912 | tf_op jit(solution)/shard_map/ppermute | solution.py:851
  338.3 1.3 collective-permute-done.30.refs_3_
  340.2 1.8 project_piece.1
  342.0 1.1 collective-permute-start.31
  343.1 3.3 collective-permute-start.33
  346.4 2.7 block_out.1.refs_4_
  349.5 2.4 collective-permute-done.33.refs_3_
  352.6 0.9 copy-done.3
  353.4 1.9 stack_line.1.refs_0_
  355.3 2.8 collective-permute-start.34
  358.1 1.5 collective-permute-start.36
  359.5 16.7 %fill.1 = (f32[3072,768]{1,0:T(8,128)}, f32[768,3072]{1,0:T(8,128)}, f32[768,768]{1,0:T(8,128)}, f32[1,768]{1,0:T(1,128)}) custom-call(bf16[32,9,24,768]{3,2,1,0:T(8,128)(2,1)} %bitcast.32, bf16[768,3072]{1,0:T(8,128)(2,1)} %w_hidden.1, f32[1,768]{1,0:T(1,128)} %reshape.53.refs_7_.gain), custom_call_target="tpu_custom_call" | custom-call | tf_op jit(solution)/shard_map/fill/pallas_call | solution.py:834
  376.3 2.3 collective-permute-done.36.refs_3_
  379.3 2.8 stack_plane.1.own
  385.3 1.9 collective-permute-done.25.refs_1_
  388.1 2.7 grad_inputs.1
  390.8 1.2 copy-done.9
  392.0 8.5 %spread.1 = (f32[768,768]{1,0:T(8,128)}, f32[768,768]{1,0:T(8,128)}, f32[768,768]{1,0:T(8,128)}, f32[1,768]{1,0:T(1,128)}) custom-call(s32[3]{0:T(128)} %pad_add_fusion.2.place, bf16[16,3,24,768]{3,2,1,0:T(8,128)(2,1)} %stack_plane.1.own, bf16[16,3,24,768]{3,2,1,0:T(8,128)(2,1)} %copy-done.9, bf16[768,768]{1,0:T(8,128)(2,1)} %w_query.3, ...), custom_call_target="tpu_custom_call" | custom-call | bytes 786432 | tf_op jit(solution)/shard_map/spread/pallas_call | solution.py:296
  400.5 1.3 reduce
  (157 shorter events, 19.5 us)
Async XLA Ops:
  7.2 5.4 %copy-start = (s32[4,1024]{1,0:T(4,128)S(1)}, s32[4,1024]{1,0:T(4,128)}, u32[]{:S(2)}) copy-start(s32[4,1024]{1,0:T(4,128)} %param.14) | copy-start | bytes 49156
  7.2 5.4 %copy-start.43 = (f32[768]{0:T(1024)S(1)}, f32[768]{0:T(1024)}, u32[]{:S(2)}) copy-start(f32[768]{0:T(1024)} %param.15) | copy-start | bytes 9220
  7.2 7.0 %copy-start.41 = (bf16[12,12]{1,0:T(8,128)(2,1)S(1)}, bf16[12,12]{1,0:T(8,128)(2,1)}, u32[]{:S(2)}) copy-start(bf16[12,12]{1,0:T(8,128)(2,1)} %param.21) | copy-start | bytes 868
  7.2 7.6 %copy-start.44 = (f32[768]{0:T(1024)S(1)}, f32[768]{0:T(1024)}, u32[]{:S(2)}) copy-start(f32[768]{0:T(1024)} %param.22) | copy-start | bytes 9220
  7.2 8.2 %copy-start.42 = (bf16[12,12]{1,0:T(8,128)(2,1)S(1)}, bf16[12,12]{1,0:T(8,128)(2,1)}, u32[]{:S(2)}) copy-start(bf16[12,12]{1,0:T(8,128)(2,1)} %param.20) | copy-start | bytes 868
  9.5 6.5 %collective-permute-start.2 = (bf16[256,768]{1,0:T(8,128)(2,1)S(1)}, bf16[256,768]{1,0:T(8,128)(2,1)S(1)}, u32[]{:S(2)}, u32[]{:S(2)}) collective-permute-start(bf16[256,768]{1,0:T(8,128)(2,1)S(1)} %get-tuple-element.222), channel_id=1, source_target_pairs={{0,1},{1,0},{2,3},{3,2},{4,5},{5,4},{6,7},{7,6},{8,9},{9,8},{10,11... | collective-permute-start | bytes 1179656 | tf_op jit(solution)/shard_map/ppermute | solution.py:851
  9.9 17.2 %collective-permute-start = (bf16[256,768]{1,0:T(8,128)(2,1)S(1)}, bf16[256,768]{1,0:T(8,128)(2,1)S(1)}, u32[]{:S(2)}, u32[]{:S(2)}) collective-permute-start(bf16[256,768]{1,0:T(8,128)(2,1)S(1)} %get-tuple-element.224), channel_id=1, source_target_pairs={{0,2},{1,3},{2,0},{3,1},{4,6},{5,7},{6,4},{7,5},{8,10},{9,11},{10,... | collective-permute-start | bytes 1179656 | tf_op jit(solution)/shard_map/ppermute | solution.py:851
  12.4 18.0 %collective-permute-start.1 = (bf16[256,768]{1,0:T(8,128)(2,1)S(1)}, bf16[256,768]{1,0:T(8,128)(2,1)S(1)}, u32[]{:S(2)}, u32[]{:S(2)}) collective-permute-start(bf16[256,768]{1,0:T(8,128)(2,1)S(1)} %get-tuple-element.223), channel_id=1, source_target_pairs={{0,3},{1,2},{2,1},{3,0},{4,7},{5,6},{6,5},{7,4},{8,11},{9,10},{10,... | collective-permute-start | bytes 1179656 | tf_op jit(solution)/shard_map/ppermute | solution.py:851
  24.5 54.1 %collective-permute-start.3 = (bf16[256,768]{1,0:T(8,128)(2,1)}, bf16[256,768]{1,0:T(8,128)(2,1)S(1)}, u32[]{:S(2)}, u32[]{:S(2)}) collective-permute-start(bf16[256,768]{1,0:T(8,128)(2,1)} %get-tuple-element.113), channel_id=1, source_target_pairs={{0,1},{1,0},{2,3},{3,2},{4,5},{5,4},{6,7},{7,6},{8,9},{9,8},{10,11... | collective-permute-start | bytes 1179656 | tf_op jit(solution)/shard_map/ppermute | solution.py:851
  24.7 54.0 %collective-permute-start.4 = (bf16[256,768]{1,0:T(8,128)(2,1)}, bf16[256,768]{1,0:T(8,128)(2,1)S(1)}, u32[]{:S(2)}, u32[]{:S(2)}) collective-permute-start(bf16[256,768]{1,0:T(8,128)(2,1)} %get-tuple-element.114), channel_id=1, source_target_pairs={{0,2},{1,3},{2,0},{3,1},{4,6},{5,7},{6,4},{7,5},{8,10},{9,11},{10,... | collective-permute-start | bytes 1179656 | tf_op jit(solution)/shard_map/ppermute | solution.py:851
  26.6 52.1 %collective-permute-start.5 = (bf16[256,768]{1,0:T(8,128)(2,1)}, bf16[256,768]{1,0:T(8,128)(2,1)S(1)}, u32[]{:S(2)}, u32[]{:S(2)}) collective-permute-start(bf16[256,768]{1,0:T(8,128)(2,1)} %get-tuple-element.115), channel_id=1, source_target_pairs={{0,3},{1,2},{2,1},{3,0},{4,7},{5,6},{6,5},{7,4},{8,11},{9,10},{10,... | collective-permute-start | bytes 1179656 | tf_op jit(solution)/shard_map/ppermute | solution.py:851
  27.2 3.3 copy-start.23
  130.0 12.4 %collective-permute-start.7 = (bf16[6,384,768]{2,1,0:T(8,128)(2,1)}, bf16[6,384,768]{2,1,0:T(8,128)(2,1)S(1)}, u32[]{:S(2)}, u32[]{:S(2)}) collective-permute-start(bf16[6,384,768]{2,1,0:T(8,128)(2,1)} %get-tuple-element.123), channel_id=1, source_target_pairs={{0,1},{1,0},{2,3},{3,2},{4,5},{5,4},{6,7},{7,6},{8,9},{9,8},{10,11... | collective-permute-start | bytes 10616840 | tf_op jit(solution)/shard_map/ppermute | solution.py:851
  138.4 4.0 collective-permute-start.8
  152.5 48.6 %all-to-all-start = ((bf16[4,6,96,768]{3,2,1,0:T(8,128)(2,1)}), bf16[4,6,96,768]{3,2,1,0:T(8,128)(2,1)S(1)}, u32[]{:S(2)}, u32[]{:S(2)}) async-start(bf16[4,6,96,768]{3,2,1,0:T(8,128)(2,1)} %get-tuple-element.127.rest_0_), calls=%async_computation | async-start | bytes 7077888 | tf_op jit(solution)/shard_map/all_to_all | solution.py:906
  156.8 44.3 %collective-permute-start.10 = (bf16[3,96,768]{2,1,0:T(8,128)(2,1)}, bf16[3,96,768]{2,1,0:T(8,128)(2,1)}, u32[]{:S(2)}, u32[]{:S(2)}) collective-permute-start(bf16[3,96,768]{2,1,0:T(8,128)(2,1)} %get-tuple-element.130), channel_id=1, source_target_pairs={{0,16},{1,17},{2,18},{3,19},{4,20},{5,21},{6,22},{7,23},{8,24},{9,... | collective-permute-start | bytes 1327112 | tf_op jit(solution)/shard_map/ppermute | solution.py:851
  159.5 41.6 %collective-permute-start.11 = (bf16[3,96,768]{2,1,0:T(8,128)(2,1)}, bf16[3,96,768]{2,1,0:T(8,128)(2,1)}, u32[]{:S(2)}, u32[]{:S(2)}) collective-permute-start(bf16[3,96,768]{2,1,0:T(8,128)(2,1)} %get-tuple-element.131), channel_id=1, source_target_pairs={{0,24},{1,25},{2,26},{3,27},{4,28},{5,29},{6,30},{7,31},{8,16},{9,... | collective-permute-start | bytes 1327112 | tf_op jit(solution)/shard_map/ppermute | solution.py:851
  160.8 40.3 %collective-permute-start.9 = (bf16[3,96,768]{2,1,0:T(8,128)(2,1)}, bf16[3,96,768]{2,1,0:T(8,128)(2,1)}, u32[]{:S(2)}, u32[]{:S(2)}) collective-permute-start(bf16[3,96,768]{2,1,0:T(8,128)(2,1)} %get-tuple-element.129), channel_id=1, source_target_pairs={{0,8},{1,9},{2,10},{3,11},{4,12},{5,13},{6,14},{7,15},{8,0},{9,1},... | collective-permute-start | bytes 1327112 | tf_op jit(solution)/shard_map/ppermute | solution.py:851
  201.1 1.8 copy-start.2
  207.4 27.9 %collective-permute-start.15 = (bf16[2,256,768]{2,1,0:T(8,128)(2,1)}, bf16[2,256,768]{2,1,0:T(8,128)(2,1)S(1)}, u32[]{:S(2)}, u32[]{:S(2)}) collective-permute-start(bf16[2,256,768]{2,1,0:T(8,128)(2,1)} %get-tuple-element.145), channel_id=1, source_target_pairs={{0,2},{1,3},{2,0},{3,1},{4,6},{5,7},{6,4},{7,5},{8,10},{9,11},{10,... | collective-permute-start | bytes 2359304 | tf_op jit(solution)/shard_map/ppermute | solution.py:851
  209.4 25.8 %all-to-all-start.1 = ((bf16[4,3,24,768]{3,2,1,0:T(8,128)(2,1)}), bf16[4,3,24,768]{3,2,1,0:T(8,128)(2,1)S(1)}, u32[]{:S(2)}, u32[]{:S(2)}) async-start(bf16[4,3,24,768]{3,2,1,0:T(8,128)(2,1)} %get-tuple-element.138), calls=%async_computation.1 | async-start | bytes 884736 | tf_op jit(solution)/shard_map/all_to_all | solution.py:906
  212.9 146.6 %all-gather.3.cloned.1.call-start = ((), (), s32[]{:S(2)}) async-start(), calls=%async_computation.2 | async-start | bytes 10948608 | tf_op jit(solution)/shard_map/all_gather | solution.py:972
  212.9 22.3 %collective-permute-start.12 = (bf16[6,24,768]{2,1,0:T(8,128)(2,1)}, bf16[6,24,768]{2,1,0:T(8,128)(2,1)S(1)}, u32[]{:S(2)}, u32[]{:S(2)}) collective-permute-start(bf16[6,24,768]{2,1,0:T(8,128)(2,1)} %get-tuple-element.140), channel_id=1, source_target_pairs={{0,8},{1,9},{2,10},{3,11},{4,12},{5,13},{6,14},{7,15},{8,0},{9,1},... | collective-permute-start | bytes 663560 | tf_op jit(solution)/shard_map/ppermute | solution.py:851
  214.8 20.4 %collective-permute-start.13 = (bf16[6,24,768]{2,1,0:T(8,128)(2,1)}, bf16[6,24,768]{2,1,0:T(8,128)(2,1)S(1)}, u32[]{:S(2)}, u32[]{:S(2)}) collective-permute-start(bf16[6,24,768]{2,1,0:T(8,128)(2,1)} %get-tuple-element.141), channel_id=1, source_target_pairs={{0,16},{1,17},{2,18},{3,19},{4,20},{5,21},{6,22},{7,23},{8,24},{9,... | collective-permute-start | bytes 663560 | tf_op jit(solution)/shard_map/ppermute | solution.py:851
  216.5 18.7 %collective-permute-start.14 = (bf16[6,24,768]{2,1,0:T(8,128)(2,1)}, bf16[6,24,768]{2,1,0:T(8,128)(2,1)S(1)}, u32[]{:S(2)}, u32[]{:S(2)}) collective-permute-start(bf16[6,24,768]{2,1,0:T(8,128)(2,1)} %get-tuple-element.142), channel_id=1, source_target_pairs={{0,24},{1,25},{2,26},{3,27},{4,28},{5,29},{6,30},{7,31},{8,16},{9,... | collective-permute-start | bytes 663560 | tf_op jit(solution)/shard_map/ppermute | solution.py:851
  239.4 6.3 %copy-start.46 = (bf16[256,768]{1,0:T(8,128)(2,1)S(1)}, bf16[256,768]{1,0:T(8,128)(2,1)}, u32[]{:S(2)}) copy-start(bf16[256,768]{1,0:T(8,128)(2,1)} %get-tuple-element.117) | copy-start | bytes 1179652
  239.4 6.8 %copy-start.6 = (bf16[2,256,768]{2,1,0:T(8,128)(2,1)S(1)}, bf16[2,256,768]{2,1,0:T(8,128)(2,1)}, u32[]{:S(2)}) copy-start(bf16[2,256,768]{2,1,0:T(8,128)(2,1)} %get-tuple-element.146.refs_2_) | copy-start | bytes 2359300
  245.7 4.0 collective-permute-start.17
  245.7 30.6 %collective-permute-start.6 = (bf16[256,768]{1,0:T(8,128)(2,1)S(1)}, bf16[256,768]{1,0:T(8,128)(2,1)S(1)}, u32[]{:S(2)}, u32[]{:S(2)}) collective-permute-start(bf16[256,768]{1,0:T(8,128)(2,1)S(1)} %copy-done.46), channel_id=1, source_target_pairs={{0,1},{1,0},{2,3},{3,2},{4,5},{5,4},{6,7},{7,6},{8,9},{9,8},{10,11... | collective-permute-start | bytes 1179656 | tf_op jit(solution)/shard_map/ppermute | solution.py:851
  246.3 30.1 %collective-permute-start.16 = (bf16[256,768]{1,0:T(8,128)(2,1)S(1)}, bf16[256,768]{1,0:T(8,128)(2,1)S(1)}, u32[]{:S(2)}, u32[]{:S(2)}) collective-permute-start(bf16[256,768]{1,0:T(8,128)(2,1)S(1)} %slice_bitcast_fusion.1), channel_id=1, source_target_pairs={{0,1},{1,0},{2,3},{3,2},{4,5},{5,4},{6,7},{7,6},{8,9},{9,8},{10,11... | collective-permute-start | bytes 1179656 | tf_op jit(solution)/shard_map/ppermute | solution.py:851
  253.3 23.0 %collective-permute-start.18 = (bf16[2,96,768]{2,1,0:T(8,128)(2,1)}, bf16[2,96,768]{2,1,0:T(8,128)(2,1)S(1)}, u32[]{:S(2)}, u32[]{:S(2)}) collective-permute-start(bf16[2,96,768]{2,1,0:T(8,128)(2,1)} %get-tuple-element.152), channel_id=1, source_target_pairs={{0,4},{1,5},{2,6},{3,7},{4,0},{5,1},{6,2},{7,3},{8,12},{9,13},{10,... | collective-permute-start | bytes 884744 | tf_op jit(solution)/shard_map/ppermute | solution.py:851
  255.2 21.1 %collective-permute-start.19 = (bf16[2,96,768]{2,1,0:T(8,128)(2,1)}, bf16[2,96,768]{2,1,0:T(8,128)(2,1)S(1)}, u32[]{:S(2)}, u32[]{:S(2)}) collective-permute-start(bf16[2,96,768]{2,1,0:T(8,128)(2,1)} %get-tuple-element.153), channel_id=1, source_target_pairs={{0,8},{1,9},{2,10},{3,11},{4,12},{5,13},{6,14},{7,15},{8,0},{9,1},... | collective-permute-start | bytes 884744 | tf_op jit(solution)/shard_map/ppermute | solution.py:851
  256.1 23.2 %collective-permute-start.20 = (bf16[2,96,768]{2,1,0:T(8,128)(2,1)}, bf16[2,96,768]{2,1,0:T(8,128)(2,1)S(1)}, u32[]{:S(2)}, u32[]{:S(2)}) collective-permute-start(bf16[2,96,768]{2,1,0:T(8,128)(2,1)} %get-tuple-element.154), channel_id=1, source_target_pairs={{0,12},{1,13},{2,14},{3,15},{4,8},{5,9},{6,10},{7,11},{8,4},{9,5},... | collective-permute-start | bytes 884744 | tf_op jit(solution)/shard_map/ppermute | solution.py:851
  276.3 3.0 copy-start.10
  276.3 3.0 copy-start.11
  276.4 3.0 copy-start.12
  276.4 3.0 copy-start.13
  284.5 2.2 collective-permute-start.21
  289.9 14.2 %collective-permute-start.22 = (bf16[104,768]{1,0:T(8,128)(2,1)}, bf16[104,768]{1,0:T(8,128)(2,1)S(1)}, u32[]{:S(2)}, u32[]{:S(2)}) collective-permute-start(bf16[104,768]{1,0:T(8,128)(2,1)} %get-tuple-element.162), channel_id=1, source_target_pairs={{0,4},{1,5},{2,6},{3,7},{4,0},{5,1},{6,2},{7,3},{8,12},{9,13},{10,... | collective-permute-start | bytes 479240 | tf_op jit(solution)/shard_map/ppermute | solution.py:851
  290.1 14.1 %collective-permute-start.23 = (bf16[104,768]{1,0:T(8,128)(2,1)}, bf16[104,768]{1,0:T(8,128)(2,1)S(1)}, u32[]{:S(2)}, u32[]{:S(2)}) collective-permute-start(bf16[104,768]{1,0:T(8,128)(2,1)} %get-tuple-element.163), channel_id=1, source_target_pairs={{0,8},{1,9},{2,10},{3,11},{4,12},{5,13},{6,14},{7,15},{8,0},{9,1},... | collective-permute-start | bytes 479240 | tf_op jit(solution)/shard_map/ppermute | solution.py:851
  290.1 24.6 %collective-permute-start.24 = (bf16[104,768]{1,0:T(8,128)(2,1)}, bf16[104,768]{1,0:T(8,128)(2,1)S(1)}, u32[]{:S(2)}, u32[]{:S(2)}) collective-permute-start(bf16[104,768]{1,0:T(8,128)(2,1)} %get-tuple-element.164), channel_id=1, source_target_pairs={{0,12},{1,13},{2,14},{3,15},{4,8},{5,9},{6,10},{7,11},{8,4},{9,5},... | collective-permute-start | bytes 479240 | tf_op jit(solution)/shard_map/ppermute | solution.py:851
  304.1 10.6 %copy-start.31 = (bf16[104,768]{1,0:T(8,128)(2,1)}, bf16[104,768]{1,0:T(8,128)(2,1)S(1)}, u32[]{:S(2)}) copy-start(bf16[104,768]{1,0:T(8,128)(2,1)S(1)} %collective-permute-done.22.refs_5_) | copy-start | bytes 479236
  304.1 10.5 %copy-start.32 = (bf16[104,768]{1,0:T(8,128)(2,1)}, bf16[104,768]{1,0:T(8,128)(2,1)S(1)}, u32[]{:S(2)}) copy-start(bf16[104,768]{1,0:T(8,128)(2,1)S(1)} %collective-permute-done.23.refs_6_) | copy-start | bytes 479236
  317.9 34.0 %collective-permute-start.26 = (bf16[2,256,768]{2,1,0:T(8,128)(2,1)}, bf16[2,256,768]{2,1,0:T(8,128)(2,1)S(1)}, u32[]{:S(2)}, u32[]{:S(2)}) collective-permute-start(bf16[2,256,768]{2,1,0:T(8,128)(2,1)} %get-tuple-element.171), channel_id=1, source_target_pairs={{0,2},{1,3},{2,0},{3,1},{4,6},{5,7},{6,4},{7,5},{8,10},{9,11},{10,... | collective-permute-start | bytes 2359304 | tf_op jit(solution)/shard_map/ppermute | solution.py:851
  320.2 18.1 %collective-permute-start.28 = (bf16[80,768]{1,0:T(8,128)(2,1)}, bf16[80,768]{1,0:T(8,128)(2,1)S(1)}, u32[]{:S(2)}, u32[]{:S(2)}) collective-permute-start(bf16[80,768]{1,0:T(8,128)(2,1)} %get-tuple-element.174), channel_id=1, source_target_pairs={{0,2},{1,3},{2,0},{3,1},{4,6},{5,7},{6,4},{7,5},{8,10},{9,11},{10,... | collective-permute-start | bytes 368648 | tf_op jit(solution)/shard_map/ppermute | solution.py:851
  320.2 18.1 %collective-permute-start.29 = (bf16[80,768]{1,0:T(8,128)(2,1)}, bf16[80,768]{1,0:T(8,128)(2,1)S(1)}, u32[]{:S(2)}, u32[]{:S(2)}) collective-permute-start(bf16[80,768]{1,0:T(8,128)(2,1)} %get-tuple-element.175), channel_id=1, source_target_pairs={{0,16},{1,17},{2,18},{3,19},{4,20},{5,21},{6,22},{7,23},{8,24},{9,... | collective-permute-start | bytes 368648 | tf_op jit(solution)/shard_map/ppermute | solution.py:851
  320.2 19.4 %collective-permute-start.30 = (bf16[80,768]{1,0:T(8,128)(2,1)}, bf16[80,768]{1,0:T(8,128)(2,1)S(1)}, u32[]{:S(2)}, u32[]{:S(2)}) collective-permute-start(bf16[80,768]{1,0:T(8,128)(2,1)} %get-tuple-element.176), channel_id=1, source_target_pairs={{0,18},{1,19},{2,16},{3,17},{4,22},{5,23},{6,20},{7,21},{8,26},{9,... | collective-permute-start | bytes 368648 | tf_op jit(solution)/shard_map/ppermute | solution.py:851
  342.0 7.1 %collective-permute-start.31 = (bf16[1,3,24,768]{3,2,1,0:T(8,128)(2,1)}, bf16[1,3,24,768]{3,2,1,0:T(8,128)(2,1)S(1)}, u32[]{:S(2)}, u32[]{:S(2)}) collective-permute-start(bf16[1,3,24,768]{3,2,1,0:T(8,128)(2,1)} %bitcast.33), channel_id=1, source_target_pairs={{0,2},{1,3},{2,0},{3,1},{4,6},{5,7},{6,4},{7,5},{8,10},{9,11},{10,... | collective-permute-start | bytes 331784 | tf_op jit(solution)/shard_map/ppermute | solution.py:851
  343.1 6.4 %collective-permute-start.32 = (bf16[1,3,24,768]{3,2,1,0:T(8,128)(2,1)}, bf16[1,3,24,768]{3,2,1,0:T(8,128)(2,1)S(1)}, u32[]{:S(2)}, u32[]{:S(2)}) collective-permute-start(bf16[1,3,24,768]{3,2,1,0:T(8,128)(2,1)} %bitcast.34), channel_id=1, source_target_pairs={{0,16},{1,17},{2,18},{3,19},{4,20},{5,21},{6,22},{7,23},{8,24},{9,... | collective-permute-start | bytes 331784 | tf_op jit(solution)/shard_map/ppermute | solution.py:851
  343.1 8.8 %collective-permute-start.33 = (bf16[1,3,24,768]{3,2,1,0:T(8,128)(2,1)}, bf16[1,3,24,768]{3,2,1,0:T(8,128)(2,1)S(1)}, u32[]{:S(2)}, u32[]{:S(2)}) collective-permute-start(bf16[1,3,24,768]{3,2,1,0:T(8,128)(2,1)} %bitcast.35), channel_id=1, source_target_pairs={{0,18},{1,19},{2,16},{3,17},{4,22},{5,23},{6,20},{7,21},{8,26},{9,... | collective-permute-start | bytes 331784 | tf_op jit(solution)/shard_map/ppermute | solution.py:851
  349.1 2.8 copy-start.37
  349.5 2.4 copy-start.38
  355.3 21.0 %collective-permute-start.34 = (bf16[4,3,24,768]{3,2,1,0:T(8,128)(2,1)}, bf16[4,3,24,768]{3,2,1,0:T(8,128)(2,1)S(1)}, u32[]{:S(2)}, u32[]{:S(2)}) collective-permute-start(bf16[4,3,24,768]{3,2,1,0:T(8,128)(2,1)} %stack_line.1.refs_0_), channel_id=1, source_target_pairs={{0,4},{1,5},{2,6},{3,7},{4,0},{5,1},{6,2},{7,3},{8,12},{9,13},{10,... | collective-permute-start | bytes 1327112 | tf_op jit(solution)/shard_map/ppermute | solution.py:851
  358.1 18.2 %collective-permute-start.35 = (bf16[4,3,24,768]{3,2,1,0:T(8,128)(2,1)}, bf16[4,3,24,768]{3,2,1,0:T(8,128)(2,1)S(1)}, u32[]{:S(2)}, u32[]{:S(2)}) collective-permute-start(bf16[4,3,24,768]{3,2,1,0:T(8,128)(2,1)} %stack_line.1.refs_0_), channel_id=1, source_target_pairs={{0,8},{1,9},{2,10},{3,11},{4,12},{5,13},{6,14},{7,15},{8,0},{9,1},... | collective-permute-start | bytes 1327112 | tf_op jit(solution)/shard_map/ppermute | solution.py:851
  358.1 20.5 %collective-permute-start.36 = (bf16[4,3,24,768]{3,2,1,0:T(8,128)(2,1)}, bf16[4,3,24,768]{3,2,1,0:T(8,128)(2,1)S(1)}, u32[]{:S(2)}, u32[]{:S(2)}) collective-permute-start(bf16[4,3,24,768]{3,2,1,0:T(8,128)(2,1)} %stack_line.1.refs_0_), channel_id=1, source_target_pairs={{0,12},{1,13},{2,14},{3,15},{4,8},{5,9},{6,10},{7,11},{8,4},{9,5},... | collective-permute-start | bytes 1327112 | tf_op jit(solution)/shard_map/ppermute | solution.py:851
  376.3 2.3 copy-start.17
  376.3 2.3 copy-start.18
  379.3 3.9 copy-start.4
  379.3 4.1 copy-start.40
  379.3 5.4 %copy-start.45 = (f32[1,768]{1,0:T(1,128)S(1)}, f32[1,768]{1,0:T(1,128)}, u32[]{:S(2)}) copy-start(f32[1,768]{1,0:T(1,128)} %get-tuple-element.183) | copy-start | bytes 9220
  382.2 8.6 %collective-permute-start.37 = (bf16[16,3,24,768]{3,2,1,0:T(8,128)(2,1)}, bf16[16,3,24,768]{3,2,1,0:T(8,128)(2,1)S(1)}, u32[]{:S(2)}, u32[]{:S(2)}) collective-permute-start(bf16[16,3,24,768]{3,2,1,0:T(8,128)(2,1)} %stack_plane.1.own), channel_id=1, source_target_pairs={{0,1},{1,0},{2,3},{3,2},{4,5},{5,4},{6,7},{7,6},{8,9},{9,8},{10,11... | collective-permute-start | bytes 5308424 | tf_op jit(solution)/shard_map/ppermute | solution.py:851
  382.8 4.4 %collective-permute-start.25 = (bf16[256,768]{1,0:T(8,128)(2,1)}, bf16[256,768]{1,0:T(8,128)(2,1)S(1)}, u32[]{:S(2)}, u32[]{:S(2)}) collective-permute-start(bf16[256,768]{1,0:T(8,128)(2,1)} %get-tuple-element.170), channel_id=1, source_target_pairs={{0,1},{1,0},{2,3},{3,2},{4,5},{5,4},{6,7},{7,6},{8,9},{9,8},{10,11... | collective-permute-start | bytes 1179656 | tf_op jit(solution)/shard_map/ppermute | solution.py:851
  383.3 3.9 collective-permute-start.27
  392.0 9.8 %copy-start.1 = (s32[4,1024]{1,0:T(4,128)S(1)}, s32[4,1024]{1,0:T(4,128)}, u32[]{:S(2)}) copy-start(s32[4,1024]{1,0:T(4,128)} %param.14) | copy-start | bytes 49156
  (24 other events, 21.6 us)
Sparse Core Ops, SparseCore 0:
  239.5 100.8 all-gather.2

commit v2 on v1

--- a/solution.py
+++ b/solution.py
@@ -12,6 +12,7 @@
 F32, BF16 = jnp.float32, jnp.bfloat16
 FORWARD_HEADS, BACKWARD_HEADS = 4, 2
 VMEM_LIMIT = 60 * 1024 * 1024
+LOG2_E = 1.4426950408889634
 MATMUL_FLOPS = 2 * H * 10 * TILE * TILE * D
 
 
@@ -64,11 +65,12 @@
     for i in range(FORWARD_HEADS):
         j = step * FORWARD_HEADS + i
         for h in range(H):
-            scaled[i, head_rows(h), :] = (q_t[head_rows(h), :].astype(F32) * mix_l[h, j]).astype(BF16)
+            weight = mix_l[h, j] * LOG2_E
+            scaled[i, head_rows(h), :] = (q_t[head_rows(h), :].astype(F32) * weight).astype(BF16)
         for t in reversed(range(TILES)):
             n = (t + 1) * TILE
             logits = mm(k[:n, :], scaled[i, :, span(t)]) + bias[:n, span(t)]
-            e = jnp.exp(logits - jnp.max(logits, axis=0, keepdims=True))
+            e = jnp.exp2(logits - jnp.max(logits, axis=0, keepdims=True))
             p = (e * (1.0 / jnp.sum(e, axis=0, keepdims=True))).astype(BF16)
             soft[i, :n, span(t)] = p
             part = mm(v_t[:, :n], p)
@@ -257,7 +259,7 @@
 epsilon = 1e-06
 GELU_SCALE = 0.7978845608028654
 GELU_CUBIC = 0.044715
-FEED_COLUMNS = 1024
+FEED_COLUMNS = 768
 COST_SHARE = 4
 HALF = D // 2
 ANY = pl.BlockSpec(memory_space=pl.ANY)
@@ -372,11 +374,16 @@
 
 
 def feed_kernel(parts, at, x, attended, *refs):
+    refs, both = refs[:-1], refs[-1]
     cots, (w_out, w_hidden, w_back, gain), rest = refs[:parts], refs[parts : parts + 4], refs[parts + 4 :]
     outs, (cot_row, normed_two, activated, grad_hidden, grad_middle, grad_attn, g, g_t) = rest[:-8], rest[-8:]
     step = pl.program_id(0)
     scale = gain[...]
-    cotangent = chosen(cots, step)
+    rows = cots[0].shape[0]
+    spots = [pl.ds(pl.multiple_of(((at[0] ^ i) % 2) * rows, rows), rows) for i in range(2)]
+    for i in range(2):
+        both[spots[i], :] = chosen(cots[i::2], step)
+    cotangent = both[...]
     cot_row[...] = cotangent
     middle = x[...].astype(F32) + mm(attended[...], w_out[...])
     inverse = inverse_rms(middle)
@@ -399,8 +406,19 @@
         grad_hidden[:, cols] = grad
         total = total + mm(act, w_back[cols, :])
         grad_n2 = grad_n2 + against(grad, w_hidden[:, cols])
-    low = total.astype(BF16)
-    write_parts(outs, step, low)
+    both[...] = total.astype(BF16)
+    near, far = outs[:-1], outs[-1]
+
+    @pl.when(step == 0)
+    def write_near():
+        for i in range(2):
+            near[i][...] = both[spots[i], :]
+
+    @pl.when(step == 1)
+    def write_far():
+        for i in range(2):
+            far[i] = both[spots[i], :]
+
     weighted = grad_n2 * scale
     mean = jnp.mean(weighted * middle, axis=-1, keepdims=True)
     grad_mid = cotangent.astype(F32) + inverse * weighted - middle * (inverse * inverse * inverse * mean)
@@ -414,16 +432,21 @@
 
 def feed(at, x, attended, cots, w_out, w_hidden, w_back, gain):
     ff, parts, rows = w_hidden.shape[1], len(cots), cots[0].shape[0]
-    tile = (tokens(rows), shape((LEN, D)))
-    wide = (pl.BlockSpec((rows, ff), lambda i, at: (at[0] ^ i, 0)), shape((LEN, ff)))
+    def pair(i, at):
+        return (at[0] // 2) ^ i
+
+    two = pl.BlockSpec((2 * rows, D), lambda i, at: (pair(i, at), 0))
+    tile = (two, shape((LEN, D)))
+    wide = (pl.BlockSpec((2 * rows, ff), lambda i, at: (pair(i, at), 0)), shape((LEN, ff)))
     outs = list(zip(*part_outs(parts, rows))) + [
-        tile, tile, wide, wide, (tokens(rows), shape((LEN, D), F32)), tile, tile, (tokens_t(rows), shape((D, LEN)))]
+        tile, tile, wide, wide, (two, shape((LEN, D), F32)), tile, tile,
+        (pl.BlockSpec((D, 2 * rows), lambda i, at: (0, pair(i, at))), shape((D, LEN)))]
     found = step_call(
-        partial(feed_kernel, parts), at, parts,
-        [tokens(rows), tokens(rows)] + [fixed((rows, D))] * parts
+        partial(feed_kernel, parts), at, parts // 2,
+        [two, two] + [fixed((rows, D))] * parts
         + [fixed((D, D)), fixed((D, ff)), fixed((ff, D)), fixed((1, D))],
         (x, attended, *cots, w_out, w_hidden, w_back, gain), [o[0] for o in outs], [o[1] for o in outs],
-        2 + 4 * ff // D, "feed")
+        2 + 4 * ff // D, "feed", [pltpu.VMEM((2 * rows, D), BF16)])
     return found[:-8], found[-8:]
 
 
@@ -693,21 +716,24 @@
 
 
 def project_piece_kernel(mine, *refs):
-    parts, (out, small, total) = refs[:-3], refs[-3:]
+    parts, (out, by_logits, by_weights, total) = refs[:-4], refs[-4:]
     total[...] = added(parts)
     rows = out.shape[1]
     for m in range(3):
         out[m] = total[m * rows : (m + 1) * rows, :].astype(BF16)
-    small[...] = total[3 * rows :, :]
+    small = total[3 * rows :, :]
+    groups = [small[:, g * 128 : g * 128 + H] for g in range(3)]
+    by_logits[...] = jnp.concatenate([groups[0], groups[1][:4]])
+    by_weights[...] = jnp.concatenate([groups[1][4:], groups[2]])
 
 
 def project_piece(mine, parts):
     rows = parts[0].shape[0]
-    (out, small), _ = plain_call(
+    outs, _ = plain_call(
         project_piece_kernel, list(parts), mine,
-        [shape((3, (rows - SMALL_ROWS) // 3, D)), shape((SMALL_ROWS, D), F32)], "project_piece",
+        [shape((3, (rows - SMALL_ROWS) // 3, D))] + [shape((H, H), F32)] * 2, "project_piece",
         [pltpu.VMEM((rows, D), F32)])
-    return out, small
+    return outs
 
 
 def stack_kernel(count, waits, mine, *refs):
@@ -763,13 +789,14 @@
             for c, pieces in enumerate((own, other)):
                 for p in range(plane):
                     for n in range(line):
-                        at = (place[0] ^ c) * plane * line + (place[1] ^ p) * line + (place[2] ^ n)
+                        of_plane, of_line = n % 2 + 2 * (p % 2), p // 2 + 2 * (n // 2)
+                        at = (place[0] ^ c) * plane * line + (place[1] ^ of_plane) * line + (place[2] ^ of_line)
                         out[pl.ds(pl.multiple_of(at * rows, 8), rows), :] = pieces[p * line + n, 0].astype(F32)
             weighed[...] += weigh(out, weight)
 
     @pl.when(matrix == 2)
     def finish():
-        by_gain[...] = as_row(weighed) / gain[...]
+        by_gain[...] = (as_row(weighed) / gain[...])[0]
 
 
 def matrix_outs(down, over):
@@ -796,7 +823,7 @@
     return step_call(
         partial(spread_kernel, sizes), place, count, [block, block, square, square, square, fixed((1, D))] + [ANY] * len(first),
         (own, other, w_query, w_key, w_value, gain, *first),
-        out_specs + [fixed((1, D))], out_shape + [shape((1, D), F32)], 0, "spread", [pltpu.VMEM((D, 128), F32)])
+        out_specs + [fixed((D,))], out_shape + [shape((D,), F32)], 0, "spread", [pltpu.VMEM((D, 128), F32)])
 
 
 def fill_kernel(counts, wide_count, starts, pieces, w_hidden, gain, *refs):
@@ -822,7 +849,7 @@
 
     @pl.when(matrix == begin - 1)
     def finish():
-        by_gain[...] = as_row(weighed) / gain[...]
+        by_gain[...] = (as_row(weighed) / gain[...])[0]
 
 
 def fill(pieces, starts, w_hidden, gain):
@@ -835,8 +862,8 @@
         partial(fill_kernel, tuple(d * o for d, o in zip(down, over)), wide_and_thin(blocks)[0], starts),
         grid=(count,),
         in_specs=[pl.BlockSpec((devices, 1, rows, D), lambda m: (0, m, 0, 0)), pl.BlockSpec((D, D), places[1]), line],
-        out_specs=out_specs + [line],
-        out_shape=out_shape + [shape((1, D), F32)],
+        out_specs=out_specs + [whole((D,))],
+        out_shape=out_shape + [shape((D,), F32)],
         scratch_shapes=[pltpu.VMEM((D, 128), F32)],
         compiler_params=params(),
         name="fill",
@@ -938,8 +965,7 @@
     where = jnp.stack([place([1]), place(plane), place(line)])
     core, spots = where[:1], where[1:]
     mixed = plane + line
-    pair_plane, pair_line = mixed[1:3], mixed[:1] + mixed[3:]
-    pair_spots = jnp.stack([place(pair_plane), place(pair_line)])
+    late_plane, early_line = mixed[1:3], mixed[:1] + mixed[3:]
     sizes = (1 << len(plane), 1 << len(line))
     parts, seq = lax.axis_size("seq"), lax.axis_index("seq")
     row_bits, at = device_bits()[: parts.bit_length() - 1], seq.reshape(1)
@@ -971,37 +997,35 @@
     out = hand_on((*out[:2], *far))
     pieces = lax.all_gather(finish_sum(piece, others), BOTH, axis=0)
     pair_kept, pair_sent = project_weight_grads(core, normed_t, [grad_q, grad_k], (), [piece])
-    pair = split(pair_spots[:1], pair_kept, swap(pair_sent, 1), sizes[0], "split_pair")
+    pair = split(spots[:1], pair_kept, swap(pair_sent, 1), sizes[0], "split_pair")
     grad_v, by_weights = value_grads(mix_w, soft, v, g, [piece, pair[0]])
-    pair = exchange(pair, pair_plane)
+    pair = exchange(pair, plane)
     one_kept, one_sent = project_weight_grads(core, normed_t, [grad_v], [by_logits, by_weights], [*pair[1:], out[1], out[3]])
-    one = split_small(pair_spots[:1], one_kept, swap(one_sent, 1), sizes[0], "split_one")
+    one = split_small(spots[:1], one_kept, swap(one_sent, 1), sizes[0], "split_one")
     grad_in = input_grads(
         at, parts, grad_q, grad_k, grad_v, x, grad_middle, w_query, w_key, w_value, gain_one, one[0])
-    shares, grad_in = project_reshare(pair_spots, pair, exchange(one, pair_plane), sizes[1], grad_in)
-    own, small = project_piece(pair_spots, exchange(shares, pair_line))
-    own, small = finish_sum(own, others)[None], finish_sum(small, others)
+    shares, grad_in = project_reshare(spots, pair, exchange(one, plane), sizes[1], grad_in)
+    own, by_logits, by_weights = [finish_sum(a, others) for a in project_piece(spots, exchange(shares, line))]
     block_out = tokens_of(at, out, "block_out")
     grad_in = send_far(grad_in)
-    own = widen(spots, own, pair_line, "stack_line", [block_out, grad_in[2]])
+    own = widen(spots, own[None], early_line, "stack_line", [block_out, grad_in[2]])
     grad_w_back, grad_w_hidden, grad_w_out, grad_gain_two = fill(
         pieces, (row_starts(plane, line), row_starts(line, plane)), w_hidden, gain_two)
     grad_inputs = tokens_of(at, hand_on(grad_in), "grad_inputs", [grad_w_out])
-    own = widen(spots, own, pair_plane, "stack_plane", [grad_w_out])
+    own = widen(spots, own, late_plane, "stack_plane", [grad_w_out])
     grad_w_query, grad_w_key, grad_w_value, grad_gain_one = spread(
-        jnp.stack([core[0], *pair_spots]), sizes, own, swap(own, 1), w_query, w_key, w_value, gain_one, [grad_w_out])
-    small = small[:, : 3 * 128].reshape(SMALL_ROWS, 3, 128).transpose(1, 0, 2).reshape(2, H, 128)[:, :, :H]
+        where, sizes, own, swap(own, 1), w_query, w_key, w_value, gain_one, [grad_w_out])
     return (
         block_out,
         grad_inputs,
-        grad_gain_one.reshape(D),
+        grad_gain_one,
         grad_w_query,
         grad_w_key,
         grad_w_value,
         grad_w_out,
-        small[0].T * scale,
-        small[1],
-        grad_gain_two.reshape(D),
+        by_logits.T * scale,
+        by_weights,
+        grad_gain_two,
         grad_w_hidden,
         grad_w_back,
     )

time: 413 us -> 407 us (0.985)
    unnamed x95 -> x93, local copies, waits for them, and re-layouts: 16.8 us -> 17.2 us
  transfers between devices with their start and end apart: 41 -> 41, of which waited for: 12 -> 12; matrix products, arithmetic and copies ran while one was open for 2% -> 1% of each run, Pallas kernels for 48% -> 48%
where the time goes in v2:
time: 407 us; the launch traced here: 403 us
  Pallas kernels  272 us (67%)
  starting transfers between devices  46.8 us (11%)
  waiting for transfers between devices  44.6 us (11%)
  local copies, waits for them, and re-layouts  22.3 us (5%)
  between operations  14.8 us (4%)
    pallas_call x11, Pallas kernels, step_call(): pl.pallas_call(kernel, grid_spec=pltpu.PrefetchScalarGridSpec(num_scalar_...  114 us
    pallas_call x3, Pallas kernels, run(): pl.pallas_call(kernel, grid=(heads // BACKWARD_HEADS,), in_specs=in_specs...  76.7 us
    ppermute x38, waiting for transfers between devices, swap(): return lax.ppermute(values, BOTH, [(s, s ^ mask) for s in range(n)])  44.5 us
    pallas_call x1, Pallas kernels, attend(): pl.pallas_call(attend_kernel, grid=(H // heads,), in_specs=[SMEM, SMEM, w...  40.8 us
    ppermute x38, starting transfers between devices, swap(): return lax.ppermute(values, BOTH, [(s, s ^ mask) for s in range(n)])  39.1 us
    pallas_call x9, Pallas kernels, plain_call(): pl.pallas_call(kernel, in_specs=[SMEM] + [VMEM] * len(operands) + [ANY] *...  23.6 us
    unnamed x93, local copies, waits for them, and re-layouts  17.2 us
    pallas_call x1, Pallas kernels, fill(): pl.pallas_call(partial(fill_kernel, tuple((d * o for d, o in zip(down, ov...  16.7 us
  transfers between devices with their start and end apart: 41, of which 12 were waited for; matrix products, arithmetic and copies ran while one was open for 1% of the time, Pallas kernels for 48%

profile of v2, /device:TPU:0, one launch (start us, length us, event | category | flops | bytes accessed | tf_op | source)
XLA Modules:
  0.0 402.5 jit_solution(10688122174414364900)
XLA Ops:
  7.3 2.2 dynamic-slice_bitcast_fusion
  9.9 2.5 collective-permute-start
  13.2 1.0 copy.41.id_col
  16.8 7.7 %project.2 = (bf16[1024,768]{1,0:T(8,128)(2,1)}, bf16[768,1024]{1,0:T(8,128)(2,1)}, bf16[1024,768]{1,0:T(8,128)(2,1)}, bf16[768,1024]{1,0:T(8,128)(2,1)}, bf16[1...) custom-call(s32[1]{0:T(128)} %bitcast.at, ...), custom_call_target="tpu_custom_call" | custom-call | flops 226492416 | bytes 786432 | tf_op jit(solution)/shard_map/project/pallas_call | solution.py:298
  24.7 1.9 collective-permute-start.4
  27.2 3.3 collective-permute-done.1.refs_1_
  31.2 6.1 %project.3 = (bf16[1024,768]{1,0:T(8,128)(2,1)}, bf16[768,1024]{1,0:T(8,128)(2,1)}, bf16[1024,768]{1,0:T(8,128)(2,1)}, bf16[768,1024]{1,0:T(8,128)(2,1)}, bf16[1...) custom-call(s32[1]{0:T(128)} %bitcast.at, ...), custom_call_target="tpu_custom_call", output_to_operand_aliasing={{0}: (7, {}), {1}: (8, {}), {2}: (9, {}), {3}: (10, {}), {4... | custom-call | flops 226492416 | bytes 786432 | tf_op jit(solution)/shard_map/project/pallas_call | solution.py:298
  37.3 40.8 %attend.1 = (bf16[12,1024,1024]{2,1,0:T(8,128)(2,1)}, bf16[1024,768]{1,0:T(8,128)(2,1)}) custom-call(f32[12,12]{1,0:T(8,128)} %convert_multiply_fusion.mix_l, f32[12,12]{1,0:T(8,128)} %convert_element_type.7.mix_w, s32[1,1024]{1,0:T(1,128)} %constant_dynamic-slice_fusion.id_row, s32[1024,1]{1,0:T(8,128)} %copy.41.id_col, ...), custom_call_target="tpu_custom_call" | custom-call | flops 3019898880 | bytes 1048576 | tf_op jit(solution)/shard_map/attend/pallas_call | solution.py:88
  79.1 36.1 %feed.1 = (bf16[256,768]{1,0:T(8,128)(2,1)}, bf16[256,768]{1,0:T(8,128)(2,1)}, bf16[2,256,768]{2,1,0:T(8,128)(2,1)}, bf16[1024,768]{1,0:T(8,128)(2,1)}, bf16[102...) custom-call(s32[1]{0:T(128)} %bitcast.at, ...), custom_call_target="tpu_custom_call" | custom-call | flops 2717908992 | bytes 786432 | tf_op jit(solution)/shard_map/feed/pallas_call | solution.py:298
  115.2 14.0 %wide_weight_grads.1 = (bf16[6,384,768]{2,1,0:T(8,128)(2,1)}, bf16[6,384,768]{2,1,0:T(8,128)(2,1)}) custom-call(s32[1]{0:T(128)} %bitcast.8.core, bf16[1024,3072]{1,0:T(8,128)(2,1)} %get-tuple-element.119.act_kept.act_sent, bf16[1024,3072]{1,0:T(8,128)(2,1)} %get-tuple-element.119.act_kept.act_sent, bf16[1024,768]{1,0:T(8,128)(2,1)} %get-tuple-element.120.cot, ...), custom_call_target="tpu_custom_call" | custom-call | flops 905969664 | bytes 786432 | tf_op jit(solution)/shard_map/wide_weight_grads/pallas_call | solution.py:298
  129.4 8.2 %thin_weight_grads.1 = (bf16[3,384,768]{2,1,0:T(8,128)(2,1)}, bf16[3,384,768]{2,1,0:T(8,128)(2,1)}) custom-call(s32[1]{0:T(128)} %bitcast.8.core, bf16[1024,768]{1,0:T(8,128)(2,1)} %get-tuple-element.121.n2_kept.n2_sent, bf16[1024,768]{1,0:T(8,128)(2,1)} %get-tuple-element.121.n2_kept.n2_sent, bf16[1024,3072]{1,0:T(8,128)(2,1)} %get-tuple-element.122.grad_hidden, ...), custom_call_target="tpu_custom_call" | custom-call | flops 452984832 | bytes 786432 | tf_op jit(solution)/shard_map/thin_weight_grads/pallas_call | solution.py:298
  138.0 3.7 collective-permute-done.8.d
  141.7 1.8 copy-done.7
  143.5 8.3 %shares.1 = (bf16[4,6,96,768]{3,2,1,0:T(8,128)(2,1)}, bf16[3,96,768]{2,1,0:T(8,128)(2,1)}, bf16[3,96,768]{2,1,0:T(8,128)(2,1)}, bf16[3,96,768]{2,1,0:T(8,128)(2,1)}, bf16[3,96,768]{2,1,0:T(8,128)(2,1)}) custom-call(s32[1]{0:T(128)} %bitcast.7.mine, bf16[6,384,768]{2,1,0:T(8,128)(2,1)} %get-tuple-element.123.refs_0_.a, bf16[6,384,768]{2,1,0:T(8,128)(2,1)} %copy-done.7, ...), custom_call_target="tpu_custom_call" | custom-call | bytes 786432 | tf_op jit(solution)/shard_map/shares/pallas_call | solution.py:298
  151.7 4.2 %all-to-all-start = ((bf16[4,6,96,768]{3,2,1,0:T(8,128)(2,1)}), bf16[4,6,96,768]{3,2,1,0:T(8,128)(2,1)S(1)}, u32[]{:S(2)}, u32[]{:S(2)}) async-start(bf16[4,6,96,768]{3,2,1,0:T(8,128)(2,1)} %get-tuple-element.128.rest_0_), calls=%async_computation | async-start | bytes 7077888 | tf_op jit(solution)/shard_map/all_to_all | solution.py:933
  155.9 2.7 collective-permute-start.10
  158.6 1.4 collective-permute-start.11
  160.8 39.4 %query_grads.1 = (bf16[1024,768]{1,0:T(8,128)(2,1)}, bf16[12,1024,1024]{2,1,0:T(8,128)(2,1)}, f32[12,1,768]{2,1,0:T(1,128)}) custom-call(f32[12,12]{1,0:T(8,128)} %convert_element_type.7.mix_w, f32[12,12]{1,0:T(8,128)} %convert_multiply_fusion.mix_l, bf16[12,1024,1024]{2,1,0:T(8,128)(2,1)} %get-tuple-element.133.soft, ...), custom_call_target="tpu_custom_call" | custom-call | flops 3019898880 | bytes 1048576 | tf_op jit(solution)/shard_map/query_grads/pallas_call | solution.py:200
  200.3 1.8 copy-done.2
  202.1 4.5 %reshare.1 = (bf16[6,24,768]{2,1,0:T(8,128)(2,1)}, bf16[6,24,768]{2,1,0:T(8,128)(2,1)}, bf16[6,24,768]{2,1,0:T(8,128)(2,1)}, bf16[6,24,768]{2,1,0:T(8,128)(2,1)}...) custom-call(s32[2]{0:T(128)} %pad_add_fusion.mine, ...), custom_call_target="tpu_custom_call", output_to_operand_aliasing={{5}: (7, {})} | custom-call | tf_op jit(solution)/shard_map/reshare/pallas_call | solution.py:618
  206.6 1.9 collective-permute-start.15
  208.5 3.5 all-to-all-start.1
  212.0 1.9 collective-permute-start.12
  213.9 1.7 collective-permute-start.13
  215.6 0.9 collective-permute-start.14
  216.5 17.8 %key_grads.1.refs_4_.refs_1_.grad_k = bf16[1024,768]{1,0:T(8,128)(2,1)} custom-call(f32[12,12]{1,0:T(8,128)} %convert_multiply_fusion.mix_l, bf16[12,1024,1024]{2,1,0:T(8,128)(2,1)} %get-tuple-element.144.grad_logits, bf16[1024,768]{1,0:T(8,128)(2,1)} %get-tuple-element.145.q, bf16[6,24,768]{2,1,0:T(8,128)(2,1)} %get-tuple-element.140.rest_0_.refs_0_), custom_call_target="tpu_custom_call" | custom-call | flops 1509949440 | bytes 1048576 | tf_op jit(solution)/shard_map/key_grads/pallas_call | solution.py:200
  235.2 0.9 copy-done.5
  236.1 2.3 piece.1
  238.4 6.3 %project_weight_grads.2 = (bf16[2,384,768]{2,1,0:T(8,128)(2,1)}, bf16[2,384,768]{2,1,0:T(8,128)(2,1)}) custom-call(s32[1]{0:T(128)} %bitcast.8.core, bf16[768,1024]{1,0:T(8,128)(2,1)} %get-tuple-element.148.nt_kept.nt_sent, bf16[768,1024]{1,0:T(8,128)(2,1)} %get-tuple-element.148.nt_kept.nt_sent, ...), custom_call_target="tpu_custom_call" | custom-call | flops 301989888 | bytes 786432 | tf_op jit(solution)/shard_map/project_weight_grads/pallas_call | solution.py:298
  245.4 3.3 collective-permute-done.17.came
  248.8 1.0 copy-done.15
  249.8 2.6 split_pair.1
  252.4 1.9 collective-permute-start.18
  254.3 1.5 collective-permute-start.19
  255.9 19.5 %value_grads.1 = (bf16[1024,768]{1,0:T(8,128)(2,1)}, f32[12,1,768]{2,1,0:T(1,128)}) custom-call(f32[12,12]{1,0:T(8,128)} %convert_element_type.7.mix_w, bf16[12,1024,1024]{2,1,0:T(8,128)(2,1)} %get-tuple-element.133.soft, bf16[1024,768]{1,0:T(8,128)(2,1)} %get-tuple-element.134.v, bf16[1024,768]{1,0:T(8,128)(2,1)} %get-tuple-element.156.g, ...), custom_call_target="tpu_custom_call" | custom-call | flops 1509949440 | bytes 1048576 | tf_op jit(solution)/shard_map/value_grads/pallas_call | solution.py:200
  276.5 4.5 %project_weight_grads.3 = (bf16[1,400,768]{2,1,0:T(8,128)(2,1)}, bf16[1,400,768]{2,1,0:T(8,128)(2,1)}) custom-call(s32[1]{0:T(128)} %bitcast.8.core, bf16[768,1024]{1,0:T(8,128)(2,1)} %get-tuple-element.148.nt_kept.nt_sent, bf16[768,1024]{1,0:T(8,128)(2,1)} %get-tuple-element.148.nt_kept.nt_sent, bf16[1024,768]{1,0:T(8,128)(2,1)} %get-tuple-element.157.refs_0_.grad_v, ...), custom_call_target="tpu_custom_call" | custom-call | flops 150994944 | bytes 786432 | tf_op jit(solution)/shard_map/project_weight_grads/pallas_call | solution.py:298
  281.0 2.2 collective-permute-done.21.came
  284.1 2.3 split_one.1
  286.4 1.9 collective-permute-start.22
  288.3 1.5 collective-permute-start.23
  289.9 11.5 %input_grads.1 = (bf16[256,768]{1,0:T(8,128)(2,1)}, bf16[256,768]{1,0:T(8,128)(2,1)}, bf16[2,256,768]{2,1,0:T(8,128)(2,1)}) custom-call(s32[1]{0:T(128)} %bitcast.at, bf16[1024,768]{1,0:T(8,128)(2,1)} %get-tuple-element.137.refs_4_.refs_0_.grad_q, bf16[1024,768]{1,0:T(8,128)(2,1)} %key_grads.1.refs_4_.refs_1_.grad_k, ...), custom_call_target="tpu_custom_call" | custom-call | flops 452984832 | bytes 786432 | tf_op jit(solution)/shard_map/input_grads/pallas_call | solution.py:298
  302.3 2.6 project_reshare.1
  304.9 2.4 collective-permute-start.26
  307.7 2.7 collective-permute-start.29
  310.4 1.3 collective-permute-start.30
  311.7 2.1 collective-permute-done.28.refs_1_
  313.8 9.1 %collective-permute-done.29.refs_2_ = bf16[80,768]{1,0:T(8,128)(2,1)S(1)} collective-permute-done((bf16[80,768]{1,0:T(8,128)(2,1)}, bf16[80,768]{1,0:T(8,128)(2,1)S(1)}, u32[]{:S(2)}, u32[]{:S(2)}) %collective-permute-start.29) | collective-permute-done | bytes 122912 | tf_op jit(solution)/shard_map/ppermute | solution.py:878
  323.6 1.8 project_piece.1
  325.5 3.0 collective-permute-start.32
  328.6 1.2 collective-permute-start.33
  329.8 2.7 block_out.1.refs_4_
  332.5 2.0 collective-permute-done.31.refs_1_
  334.5 8.2 %collective-permute-done.32.refs_2_ = bf16[1,3,24,768]{3,2,1,0:T(8,128)(2,1)S(1)} collective-permute-done((bf16[1,3,24,768]{3,2,1,0:T(8,128)(2,1)}, bf16[1,3,24,768]{3,2,1,0:T(8,128)(2,1)S(1)}, u32[]{:S(2)}, u32[]{:S(2)}) %collective-permute-start.32) | collective-permute-done | bytes 110624 | tf_op jit(solution)/shard_map/ppermute | solution.py:878
  342.7 4.5 %collective-permute-done.33.refs_3_ = bf16[1,3,24,768]{3,2,1,0:T(8,128)(2,1)S(1)} collective-permute-done((bf16[1,3,24,768]{3,2,1,0:T(8,128)(2,1)}, bf16[1,3,24,768]{3,2,1,0:T(8,128)(2,1)S(1)}, u32[]{:S(2)}, u32[]{:S(2)}) %collective-permute-start.33) | collective-permute-done | bytes 110624 | tf_op jit(solution)/shard_map/ppermute | solution.py:878
  348.8 1.9 stack_line.1.refs_0_
  350.6 1.6 collective-permute-start.34
  352.2 1.9 collective-permute-start.36
  354.1 16.7 %fill.1 = (f32[3072,768]{1,0:T(8,128)}, f32[768,3072]{1,0:T(8,128)}, f32[768,768]{1,0:T(8,128)}, f32[768]{0:T(1024)}) custom-call(bf16[32,9,24,768]{3,2,1,0:T(8,128)(2,1)} %bitcast.22, bf16[768,3072]{1,0:T(8,128)(2,1)} %w_hidden.1, f32[1,768]{1,0:T(1,128)} %reshape.39.refs_7_.gain), custom_call_target="tpu_custom_call" | custom-call | tf_op jit(solution)/shard_map/fill/pallas_call | solution.py:861
  370.9 2.6 collective-permute-done.36.refs_3_
  374.3 2.8 stack_plane.1.own
  379.0 3.1 collective-permute-done.25.refs_1_
  383.0 2.7 grad_inputs.1
  385.7 1.2 copy-done.9
  386.9 8.5 %spread.1 = (f32[768,768]{1,0:T(8,128)}, f32[768,768]{1,0:T(8,128)}, f32[768,768]{1,0:T(8,128)}, f32[768]{0:T(1024)}) custom-call(s32[3]{0:T(128)} %pad_add_fusion.1.place, bf16[16,3,24,768]{3,2,1,0:T(8,128)(2,1)} %stack_plane.1.own, bf16[16,3,24,768]{3,2,1,0:T(8,128)(2,1)} %copy-done.9, bf16[768,768]{1,0:T(8,128)(2,1)} %w_query.3, bf16[768,768]{1,0:T(8,128)(2,1)} %w_key.3, ...), custom_call_target="tpu_custom_call" | custom-call | bytes 786432 | tf_op jit(solution)/shard_map/spread/pallas_call | solution.py:298
  (150 shorter events, 18.7 us)
Async XLA Ops:
  7.2 5.4 %copy-start = (s32[4,1024]{1,0:T(4,128)S(1)}, s32[4,1024]{1,0:T(4,128)}, u32[]{:S(2)}) copy-start(s32[4,1024]{1,0:T(4,128)} %param.14) | copy-start | bytes 49156
  7.2 5.4 %copy-start.43 = (f32[768]{0:T(1024)S(1)}, f32[768]{0:T(1024)}, u32[]{:S(2)}) copy-start(f32[768]{0:T(1024)} %param.15) | copy-start | bytes 9220
  7.2 7.0 %copy-start.41 = (bf16[12,12]{1,0:T(8,128)(2,1)S(1)}, bf16[12,12]{1,0:T(8,128)(2,1)}, u32[]{:S(2)}) copy-start(bf16[12,12]{1,0:T(8,128)(2,1)} %param.21) | copy-start | bytes 868
  7.2 7.6 %copy-start.44 = (f32[768]{0:T(1024)S(1)}, f32[768]{0:T(1024)}, u32[]{:S(2)}) copy-start(f32[768]{0:T(1024)} %param.22) | copy-start | bytes 9220
  7.2 8.2 %copy-start.42 = (bf16[12,12]{1,0:T(8,128)(2,1)S(1)}, bf16[12,12]{1,0:T(8,128)(2,1)}, u32[]{:S(2)}) copy-start(bf16[12,12]{1,0:T(8,128)(2,1)} %param.20) | copy-start | bytes 868
  9.5 6.6 %collective-permute-start.2 = (bf16[256,768]{1,0:T(8,128)(2,1)S(1)}, bf16[256,768]{1,0:T(8,128)(2,1)S(1)}, u32[]{:S(2)}, u32[]{:S(2)}) collective-permute-start(bf16[256,768]{1,0:T(8,128)(2,1)S(1)} %get-tuple-element.224), channel_id=1, source_target_pairs={{0,1},{1,0},{2,3},{3,2},{4,5},{5,4},{6,7},{7,6},{8,9},{9,8},{10,11... | collective-permute-start | bytes 1179656 | tf_op jit(solution)/shard_map/ppermute | solution.py:878
  9.9 17.3 %collective-permute-start = (bf16[256,768]{1,0:T(8,128)(2,1)S(1)}, bf16[256,768]{1,0:T(8,128)(2,1)S(1)}, u32[]{:S(2)}, u32[]{:S(2)}) collective-permute-start(bf16[256,768]{1,0:T(8,128)(2,1)S(1)} %get-tuple-element.226), channel_id=1, source_target_pairs={{0,2},{1,3},{2,0},{3,1},{4,6},{5,7},{6,4},{7,5},{8,10},{9,11},{10,... | collective-permute-start | bytes 1179656 | tf_op jit(solution)/shard_map/ppermute | solution.py:878
  12.4 18.0 %collective-permute-start.1 = (bf16[256,768]{1,0:T(8,128)(2,1)S(1)}, bf16[256,768]{1,0:T(8,128)(2,1)S(1)}, u32[]{:S(2)}, u32[]{:S(2)}) collective-permute-start(bf16[256,768]{1,0:T(8,128)(2,1)S(1)} %get-tuple-element.225), channel_id=1, source_target_pairs={{0,3},{1,2},{2,1},{3,0},{4,7},{5,6},{6,5},{7,4},{8,11},{9,10},{10,... | collective-permute-start | bytes 1179656 | tf_op jit(solution)/shard_map/ppermute | solution.py:878
  24.5 53.6 %collective-permute-start.3 = (bf16[256,768]{1,0:T(8,128)(2,1)}, bf16[256,768]{1,0:T(8,128)(2,1)S(1)}, u32[]{:S(2)}, u32[]{:S(2)}) collective-permute-start(bf16[256,768]{1,0:T(8,128)(2,1)} %get-tuple-element.114), channel_id=1, source_target_pairs={{0,1},{1,0},{2,3},{3,2},{4,5},{5,4},{6,7},{7,6},{8,9},{9,8},{10,11... | collective-permute-start | bytes 1179656 | tf_op jit(solution)/shard_map/ppermute | solution.py:878
  24.7 53.5 %collective-permute-start.4 = (bf16[256,768]{1,0:T(8,128)(2,1)}, bf16[256,768]{1,0:T(8,128)(2,1)S(1)}, u32[]{:S(2)}, u32[]{:S(2)}) collective-permute-start(bf16[256,768]{1,0:T(8,128)(2,1)} %get-tuple-element.115), channel_id=1, source_target_pairs={{0,2},{1,3},{2,0},{3,1},{4,6},{5,7},{6,4},{7,5},{8,10},{9,11},{10,... | collective-permute-start | bytes 1179656 | tf_op jit(solution)/shard_map/ppermute | solution.py:878
  26.6 51.6 %collective-permute-start.5 = (bf16[256,768]{1,0:T(8,128)(2,1)}, bf16[256,768]{1,0:T(8,128)(2,1)S(1)}, u32[]{:S(2)}, u32[]{:S(2)}) collective-permute-start(bf16[256,768]{1,0:T(8,128)(2,1)} %get-tuple-element.116), channel_id=1, source_target_pairs={{0,3},{1,2},{2,1},{3,0},{4,7},{5,6},{6,5},{7,4},{8,11},{9,10},{10,... | collective-permute-start | bytes 1179656 | tf_op jit(solution)/shard_map/ppermute | solution.py:878
  27.2 3.3 copy-start.23
  78.2 1.0 copy-start.27
  129.3 12.4 %collective-permute-start.7 = (bf16[6,384,768]{2,1,0:T(8,128)(2,1)}, bf16[6,384,768]{2,1,0:T(8,128)(2,1)S(1)}, u32[]{:S(2)}, u32[]{:S(2)}) collective-permute-start(bf16[6,384,768]{2,1,0:T(8,128)(2,1)} %get-tuple-element.124), channel_id=1, source_target_pairs={{0,1},{1,0},{2,3},{3,2},{4,5},{5,4},{6,7},{7,6},{8,9},{9,8},{10,11... | collective-permute-start | bytes 10616840 | tf_op jit(solution)/shard_map/ppermute | solution.py:878
  137.6 4.0 %collective-permute-start.8 = (bf16[3,384,768]{2,1,0:T(8,128)(2,1)}, bf16[3,384,768]{2,1,0:T(8,128)(2,1)}, u32[]{:S(2)}, u32[]{:S(2)}) collective-permute-start(bf16[3,384,768]{2,1,0:T(8,128)(2,1)} %get-tuple-element.127), channel_id=1, source_target_pairs={{0,1},{1,0},{2,3},{3,2},{4,5},{5,4},{6,7},{7,6},{8,9},{9,8},{10,11... | collective-permute-start | bytes 5308424 | tf_op jit(solution)/shard_map/ppermute | solution.py:878
  141.7 1.8 copy-start.7
  151.7 48.5 %all-to-all-start = ((bf16[4,6,96,768]{3,2,1,0:T(8,128)(2,1)}), bf16[4,6,96,768]{3,2,1,0:T(8,128)(2,1)S(1)}, u32[]{:S(2)}, u32[]{:S(2)}) async-start(bf16[4,6,96,768]{3,2,1,0:T(8,128)(2,1)} %get-tuple-element.128.rest_0_), calls=%async_computation | async-start | bytes 7077888 | tf_op jit(solution)/shard_map/all_to_all | solution.py:933
  155.9 44.3 %collective-permute-start.10 = (bf16[3,96,768]{2,1,0:T(8,128)(2,1)}, bf16[3,96,768]{2,1,0:T(8,128)(2,1)}, u32[]{:S(2)}, u32[]{:S(2)}) collective-permute-start(bf16[3,96,768]{2,1,0:T(8,128)(2,1)} %get-tuple-element.131), channel_id=1, source_target_pairs={{0,16},{1,17},{2,18},{3,19},{4,20},{5,21},{6,22},{7,23},{8,24},{9,... | collective-permute-start | bytes 1327112 | tf_op jit(solution)/shard_map/ppermute | solution.py:878
  158.6 41.7 %collective-permute-start.11 = (bf16[3,96,768]{2,1,0:T(8,128)(2,1)}, bf16[3,96,768]{2,1,0:T(8,128)(2,1)}, u32[]{:S(2)}, u32[]{:S(2)}) collective-permute-start(bf16[3,96,768]{2,1,0:T(8,128)(2,1)} %get-tuple-element.132), channel_id=1, source_target_pairs={{0,24},{1,25},{2,26},{3,27},{4,28},{5,29},{6,30},{7,31},{8,16},{9,... | collective-permute-start | bytes 1327112 | tf_op jit(solution)/shard_map/ppermute | solution.py:878
  160.0 40.3 %collective-permute-start.9 = (bf16[3,96,768]{2,1,0:T(8,128)(2,1)}, bf16[3,96,768]{2,1,0:T(8,128)(2,1)}, u32[]{:S(2)}, u32[]{:S(2)}) collective-permute-start(bf16[3,96,768]{2,1,0:T(8,128)(2,1)} %get-tuple-element.130), channel_id=1, source_target_pairs={{0,8},{1,9},{2,10},{3,11},{4,12},{5,13},{6,14},{7,15},{8,0},{9,1},... | collective-permute-start | bytes 1327112 | tf_op jit(solution)/shard_map/ppermute | solution.py:878
  200.3 1.8 copy-start.2
  206.6 27.7 %collective-permute-start.15 = (bf16[2,256,768]{2,1,0:T(8,128)(2,1)}, bf16[2,256,768]{2,1,0:T(8,128)(2,1)S(1)}, u32[]{:S(2)}, u32[]{:S(2)}) collective-permute-start(bf16[2,256,768]{2,1,0:T(8,128)(2,1)} %get-tuple-element.146), channel_id=1, source_target_pairs={{0,2},{1,3},{2,0},{3,1},{4,6},{5,7},{6,4},{7,5},{8,10},{9,11},{10,... | collective-permute-start | bytes 2359304 | tf_op jit(solution)/shard_map/ppermute | solution.py:878
  208.5 25.8 %all-to-all-start.1 = ((bf16[4,3,24,768]{3,2,1,0:T(8,128)(2,1)}), bf16[4,3,24,768]{3,2,1,0:T(8,128)(2,1)S(1)}, u32[]{:S(2)}, u32[]{:S(2)}) async-start(bf16[4,3,24,768]{3,2,1,0:T(8,128)(2,1)} %get-tuple-element.139), calls=%async_computation.1 | async-start | bytes 884736 | tf_op jit(solution)/shard_map/all_to_all | solution.py:933
  212.0 142.2 %all-gather.3.cloned.1.call-start = ((), (), s32[]{:S(2)}) async-start(), calls=%async_computation.2 | async-start | bytes 10948608 | tf_op jit(solution)/shard_map/all_gather | solution.py:998
  212.0 22.2 %collective-permute-start.12 = (bf16[6,24,768]{2,1,0:T(8,128)(2,1)}, bf16[6,24,768]{2,1,0:T(8,128)(2,1)S(1)}, u32[]{:S(2)}, u32[]{:S(2)}) collective-permute-start(bf16[6,24,768]{2,1,0:T(8,128)(2,1)} %get-tuple-element.141), channel_id=1, source_target_pairs={{0,8},{1,9},{2,10},{3,11},{4,12},{5,13},{6,14},{7,15},{8,0},{9,1},... | collective-permute-start | bytes 663560 | tf_op jit(solution)/shard_map/ppermute | solution.py:878
  213.9 20.4 %collective-permute-start.13 = (bf16[6,24,768]{2,1,0:T(8,128)(2,1)}, bf16[6,24,768]{2,1,0:T(8,128)(2,1)S(1)}, u32[]{:S(2)}, u32[]{:S(2)}) collective-permute-start(bf16[6,24,768]{2,1,0:T(8,128)(2,1)} %get-tuple-element.142), channel_id=1, source_target_pairs={{0,16},{1,17},{2,18},{3,19},{4,20},{5,21},{6,22},{7,23},{8,24},{9,... | collective-permute-start | bytes 663560 | tf_op jit(solution)/shard_map/ppermute | solution.py:878
  215.6 18.7 %collective-permute-start.14 = (bf16[6,24,768]{2,1,0:T(8,128)(2,1)}, bf16[6,24,768]{2,1,0:T(8,128)(2,1)S(1)}, u32[]{:S(2)}, u32[]{:S(2)}) collective-permute-start(bf16[6,24,768]{2,1,0:T(8,128)(2,1)} %get-tuple-element.143), channel_id=1, source_target_pairs={{0,24},{1,25},{2,26},{3,27},{4,28},{5,29},{6,30},{7,31},{8,16},{9,... | collective-permute-start | bytes 663560 | tf_op jit(solution)/shard_map/ppermute | solution.py:878
  238.4 6.3 %copy-start.45 = (bf16[256,768]{1,0:T(8,128)(2,1)S(1)}, bf16[256,768]{1,0:T(8,128)(2,1)}, u32[]{:S(2)}) copy-start(bf16[256,768]{1,0:T(8,128)(2,1)} %get-tuple-element.118) | copy-start | bytes 1179652
  238.4 6.8 %copy-start.6 = (bf16[2,256,768]{2,1,0:T(8,128)(2,1)S(1)}, bf16[2,256,768]{2,1,0:T(8,128)(2,1)}, u32[]{:S(2)}) copy-start(bf16[2,256,768]{2,1,0:T(8,128)(2,1)} %get-tuple-element.147.refs_2_) | copy-start | bytes 2359300
  244.7 4.0 collective-permute-start.17
  244.8 30.6 %collective-permute-start.6 = (bf16[256,768]{1,0:T(8,128)(2,1)S(1)}, bf16[256,768]{1,0:T(8,128)(2,1)S(1)}, u32[]{:S(2)}, u32[]{:S(2)}) collective-permute-start(bf16[256,768]{1,0:T(8,128)(2,1)S(1)} %copy-done.45), channel_id=1, source_target_pairs={{0,1},{1,0},{2,3},{3,2},{4,5},{5,4},{6,7},{7,6},{8,9},{9,8},{10,11... | collective-permute-start | bytes 1179656 | tf_op jit(solution)/shard_map/ppermute | solution.py:878
  245.3 30.1 %collective-permute-start.16 = (bf16[256,768]{1,0:T(8,128)(2,1)S(1)}, bf16[256,768]{1,0:T(8,128)(2,1)S(1)}, u32[]{:S(2)}, u32[]{:S(2)}) collective-permute-start(bf16[256,768]{1,0:T(8,128)(2,1)S(1)} %slice_bitcast_fusion.1), channel_id=1, source_target_pairs={{0,1},{1,0},{2,3},{3,2},{4,5},{5,4},{6,7},{7,6},{8,9},{9,8},{10,11... | collective-permute-start | bytes 1179656 | tf_op jit(solution)/shard_map/ppermute | solution.py:878
  248.8 1.0 copy-start.15
  252.4 23.0 %collective-permute-start.18 = (bf16[2,96,768]{2,1,0:T(8,128)(2,1)}, bf16[2,96,768]{2,1,0:T(8,128)(2,1)S(1)}, u32[]{:S(2)}, u32[]{:S(2)}) collective-permute-start(bf16[2,96,768]{2,1,0:T(8,128)(2,1)} %get-tuple-element.153), channel_id=1, source_target_pairs={{0,2},{1,3},{2,0},{3,1},{4,6},{5,7},{6,4},{7,5},{8,10},{9,11},{10,... | collective-permute-start | bytes 884744 | tf_op jit(solution)/shard_map/ppermute | solution.py:878
  254.3 21.1 %collective-permute-start.19 = (bf16[2,96,768]{2,1,0:T(8,128)(2,1)}, bf16[2,96,768]{2,1,0:T(8,128)(2,1)S(1)}, u32[]{:S(2)}, u32[]{:S(2)}) collective-permute-start(bf16[2,96,768]{2,1,0:T(8,128)(2,1)} %get-tuple-element.154), channel_id=1, source_target_pairs={{0,4},{1,5},{2,6},{3,7},{4,0},{5,1},{6,2},{7,3},{8,12},{9,13},{10,... | collective-permute-start | bytes 884744 | tf_op jit(solution)/shard_map/ppermute | solution.py:878
  255.7 19.7 %collective-permute-start.20 = (bf16[2,96,768]{2,1,0:T(8,128)(2,1)}, bf16[2,96,768]{2,1,0:T(8,128)(2,1)S(1)}, u32[]{:S(2)}, u32[]{:S(2)}) collective-permute-start(bf16[2,96,768]{2,1,0:T(8,128)(2,1)} %get-tuple-element.155), channel_id=1, source_target_pairs={{0,6},{1,7},{2,4},{3,5},{4,2},{5,3},{6,0},{7,1},{8,14},{9,15},{10,... | collective-permute-start | bytes 884744 | tf_op jit(solution)/shard_map/ppermute | solution.py:878
  275.4 1.0 copy-start.13
  275.4 1.1 copy-start.14
  281.0 2.2 collective-permute-start.21
  286.4 15.0 %collective-permute-start.22 = (bf16[104,768]{1,0:T(8,128)(2,1)}, bf16[104,768]{1,0:T(8,128)(2,1)S(1)}, u32[]{:S(2)}, u32[]{:S(2)}) collective-permute-start(bf16[104,768]{1,0:T(8,128)(2,1)} %get-tuple-element.163), channel_id=1, source_target_pairs={{0,2},{1,3},{2,0},{3,1},{4,6},{5,7},{6,4},{7,5},{8,10},{9,11},{10,... | collective-permute-start | bytes 479240 | tf_op jit(solution)/shard_map/ppermute | solution.py:878
  288.3 13.2 %collective-permute-start.23 = (bf16[104,768]{1,0:T(8,128)(2,1)}, bf16[104,768]{1,0:T(8,128)(2,1)S(1)}, u32[]{:S(2)}, u32[]{:S(2)}) collective-permute-start(bf16[104,768]{1,0:T(8,128)(2,1)} %get-tuple-element.164), channel_id=1, source_target_pairs={{0,4},{1,5},{2,6},{3,7},{4,0},{5,1},{6,2},{7,3},{8,12},{9,13},{10,... | collective-permute-start | bytes 479240 | tf_op jit(solution)/shard_map/ppermute | solution.py:878
  289.7 11.9 %collective-permute-start.24 = (bf16[104,768]{1,0:T(8,128)(2,1)}, bf16[104,768]{1,0:T(8,128)(2,1)S(1)}, u32[]{:S(2)}, u32[]{:S(2)}) collective-permute-start(bf16[104,768]{1,0:T(8,128)(2,1)} %get-tuple-element.165), channel_id=1, source_target_pairs={{0,6},{1,7},{2,4},{3,5},{4,2},{5,3},{6,0},{7,1},{8,14},{9,15},{10,... | collective-permute-start | bytes 479240 | tf_op jit(solution)/shard_map/ppermute | solution.py:878
  304.9 42.3 %collective-permute-start.26 = (bf16[2,256,768]{2,1,0:T(8,128)(2,1)}, bf16[2,256,768]{2,1,0:T(8,128)(2,1)S(1)}, u32[]{:S(2)}, u32[]{:S(2)}) collective-permute-start(bf16[2,256,768]{2,1,0:T(8,128)(2,1)} %get-tuple-element.172), channel_id=1, source_target_pairs={{0,2},{1,3},{2,0},{3,1},{4,6},{5,7},{6,4},{7,5},{8,10},{9,11},{10,... | collective-permute-start | bytes 2359304 | tf_op jit(solution)/shard_map/ppermute | solution.py:878
  307.3 6.5 %collective-permute-start.28 = (bf16[80,768]{1,0:T(8,128)(2,1)}, bf16[80,768]{1,0:T(8,128)(2,1)S(1)}, u32[]{:S(2)}, u32[]{:S(2)}) collective-permute-start(bf16[80,768]{1,0:T(8,128)(2,1)} %get-tuple-element.175), channel_id=1, source_target_pairs={{0,8},{1,9},{2,10},{3,11},{4,12},{5,13},{6,14},{7,15},{8,0},{9,1},... | collective-permute-start | bytes 368648 | tf_op jit(solution)/shard_map/ppermute | solution.py:878
  307.7 15.2 %collective-permute-start.29 = (bf16[80,768]{1,0:T(8,128)(2,1)}, bf16[80,768]{1,0:T(8,128)(2,1)S(1)}, u32[]{:S(2)}, u32[]{:S(2)}) collective-permute-start(bf16[80,768]{1,0:T(8,128)(2,1)} %get-tuple-element.176), channel_id=1, source_target_pairs={{0,16},{1,17},{2,18},{3,19},{4,20},{5,21},{6,22},{7,23},{8,24},{9,... | collective-permute-start | bytes 368648 | tf_op jit(solution)/shard_map/ppermute | solution.py:878
  310.4 12.5 %collective-permute-start.30 = (bf16[80,768]{1,0:T(8,128)(2,1)}, bf16[80,768]{1,0:T(8,128)(2,1)S(1)}, u32[]{:S(2)}, u32[]{:S(2)}) collective-permute-start(bf16[80,768]{1,0:T(8,128)(2,1)} %get-tuple-element.177), channel_id=1, source_target_pairs={{0,24},{1,25},{2,26},{3,27},{4,28},{5,29},{6,30},{7,31},{8,16},{9,... | collective-permute-start | bytes 368648 | tf_op jit(solution)/shard_map/ppermute | solution.py:878
  313.8 9.1 %copy-start.34 = (bf16[80,768]{1,0:T(8,128)(2,1)}, bf16[80,768]{1,0:T(8,128)(2,1)S(1)}, u32[]{:S(2)}) copy-start(bf16[80,768]{1,0:T(8,128)(2,1)S(1)} %collective-permute-done.28.refs_1_) | copy-start | bytes 368644
  325.4 9.1 %collective-permute-start.31 = (bf16[1,3,24,768]{3,2,1,0:T(8,128)(2,1)}, bf16[1,3,24,768]{3,2,1,0:T(8,128)(2,1)S(1)}, u32[]{:S(2)}, u32[]{:S(2)}) collective-permute-start(bf16[1,3,24,768]{3,2,1,0:T(8,128)(2,1)} %bitcast.23), channel_id=1, source_target_pairs={{0,2},{1,3},{2,0},{3,1},{4,6},{5,7},{6,4},{7,5},{8,10},{9,11},{10,... | collective-permute-start | bytes 331784 | tf_op jit(solution)/shard_map/ppermute | solution.py:878
  325.5 17.2 %collective-permute-start.32 = (bf16[1,3,24,768]{3,2,1,0:T(8,128)(2,1)}, bf16[1,3,24,768]{3,2,1,0:T(8,128)(2,1)S(1)}, u32[]{:S(2)}, u32[]{:S(2)}) collective-permute-start(bf16[1,3,24,768]{3,2,1,0:T(8,128)(2,1)} %bitcast.24), channel_id=1, source_target_pairs={{0,16},{1,17},{2,18},{3,19},{4,20},{5,21},{6,22},{7,23},{8,24},{9,... | collective-permute-start | bytes 331784 | tf_op jit(solution)/shard_map/ppermute | solution.py:878
  328.6 18.7 %collective-permute-start.33 = (bf16[1,3,24,768]{3,2,1,0:T(8,128)(2,1)}, bf16[1,3,24,768]{3,2,1,0:T(8,128)(2,1)S(1)}, u32[]{:S(2)}, u32[]{:S(2)}) collective-permute-start(bf16[1,3,24,768]{3,2,1,0:T(8,128)(2,1)} %bitcast.25), channel_id=1, source_target_pairs={{0,18},{1,19},{2,16},{3,17},{4,22},{5,23},{6,20},{7,21},{8,26},{9,... | collective-permute-start | bytes 331784 | tf_op jit(solution)/shard_map/ppermute | solution.py:878
  334.5 12.8 %copy-start.37 = (bf16[1,3,24,768]{3,2,1,0:T(8,128)(2,1)}, bf16[1,3,24,768]{3,2,1,0:T(8,128)(2,1)S(1)}, u32[]{:S(2)}) copy-start(bf16[1,3,24,768]{3,2,1,0:T(8,128)(2,1)S(1)} %collective-permute-done.31.refs_1_) | copy-start | bytes 331780
  342.7 4.5 %copy-start.38 = (bf16[1,3,24,768]{3,2,1,0:T(8,128)(2,1)}, bf16[1,3,24,768]{3,2,1,0:T(8,128)(2,1)S(1)}, u32[]{:S(2)}) copy-start(bf16[1,3,24,768]{3,2,1,0:T(8,128)(2,1)S(1)} %collective-permute-done.32.refs_2_) | copy-start | bytes 331780
  350.6 20.2 %collective-permute-start.34 = (bf16[4,3,24,768]{3,2,1,0:T(8,128)(2,1)}, bf16[4,3,24,768]{3,2,1,0:T(8,128)(2,1)S(1)}, u32[]{:S(2)}, u32[]{:S(2)}) collective-permute-start(bf16[4,3,24,768]{3,2,1,0:T(8,128)(2,1)} %stack_line.1.refs_0_), channel_id=1, source_target_pairs={{0,4},{1,5},{2,6},{3,7},{4,0},{5,1},{6,2},{7,3},{8,12},{9,13},{10,... | collective-permute-start | bytes 1327112 | tf_op jit(solution)/shard_map/ppermute | solution.py:878
  352.2 18.6 %collective-permute-start.35 = (bf16[4,3,24,768]{3,2,1,0:T(8,128)(2,1)}, bf16[4,3,24,768]{3,2,1,0:T(8,128)(2,1)S(1)}, u32[]{:S(2)}, u32[]{:S(2)}) collective-permute-start(bf16[4,3,24,768]{3,2,1,0:T(8,128)(2,1)} %stack_line.1.refs_0_), channel_id=1, source_target_pairs={{0,8},{1,9},{2,10},{3,11},{4,12},{5,13},{6,14},{7,15},{8,0},{9,1},... | collective-permute-start | bytes 1327112 | tf_op jit(solution)/shard_map/ppermute | solution.py:878
  352.2 21.3 %collective-permute-start.36 = (bf16[4,3,24,768]{3,2,1,0:T(8,128)(2,1)}, bf16[4,3,24,768]{3,2,1,0:T(8,128)(2,1)S(1)}, u32[]{:S(2)}, u32[]{:S(2)}) collective-permute-start(bf16[4,3,24,768]{3,2,1,0:T(8,128)(2,1)} %stack_line.1.refs_0_), channel_id=1, source_target_pairs={{0,12},{1,13},{2,14},{3,15},{4,8},{5,9},{6,10},{7,11},{8,4},{9,5},... | collective-permute-start | bytes 1327112 | tf_op jit(solution)/shard_map/ppermute | solution.py:878
  370.8 2.7 copy-start.17
  370.9 2.6 copy-start.18
  374.3 3.3 copy-start.4
  374.3 4.0 %copy-start.40 = (f32[12,12]{1,0:T(8,128)S(1)}, f32[12,12]{1,0:T(8,128)}, u32[]{:S(2)}) copy-start(f32[12,12]{1,0:T(8,128)} %get-tuple-element.183) | copy-start | bytes 1732
  377.1 8.6 %collective-permute-start.37 = (bf16[16,3,24,768]{3,2,1,0:T(8,128)(2,1)}, bf16[16,3,24,768]{3,2,1,0:T(8,128)(2,1)S(1)}, u32[]{:S(2)}, u32[]{:S(2)}) collective-permute-start(bf16[16,3,24,768]{3,2,1,0:T(8,128)(2,1)} %stack_plane.1.own), channel_id=1, source_target_pairs={{0,1},{1,0},{2,3},{3,2},{4,5},{5,4},{6,7},{7,6},{8,9},{9,8},{10,11... | collective-permute-start | bytes 5308424 | tf_op jit(solution)/shard_map/ppermute | solution.py:878
  377.1 5.0 %collective-permute-start.25 = (bf16[256,768]{1,0:T(8,128)(2,1)}, bf16[256,768]{1,0:T(8,128)(2,1)S(1)}, u32[]{:S(2)}, u32[]{:S(2)}) collective-permute-start(bf16[256,768]{1,0:T(8,128)(2,1)} %get-tuple-element.171), channel_id=1, source_target_pairs={{0,1},{1,0},{2,3},{3,2},{4,5},{5,4},{6,7},{7,6},{8,9},{9,8},{10,11... | collective-permute-start | bytes 1179656 | tf_op jit(solution)/shard_map/ppermute | solution.py:878
  377.6 4.5 %collective-permute-start.27 = (bf16[256,768]{1,0:T(8,128)(2,1)S(1)}, bf16[256,768]{1,0:T(8,128)(2,1)S(1)}, u32[]{:S(2)}, u32[]{:S(2)}) collective-permute-start(bf16[256,768]{1,0:T(8,128)(2,1)S(1)} %slice_bitcast_fusion), channel_id=1, source_target_pairs={{0,1},{1,0},{2,3},{3,2},{4,5},{5,4},{6,7},{7,6},{8,9},{9,8},{10,11... | collective-permute-start | bytes 1179656 | tf_op jit(solution)/shard_map/ppermute | solution.py:878
  385.7 1.2 copy-start.9
  386.9 8.5 %copy-start.1 = (s32[4,1024]{1,0:T(4,128)S(1)}, s32[4,1024]{1,0:T(4,128)}, u32[]{:S(2)}) copy-start(s32[4,1024]{1,0:T(4,128)} %param.14) | copy-start | bytes 49156
  (23 other events, 17.9 us)
Sparse Core Ops, SparseCore 0:
  238.5 109.9 all-gather.2

commit v3 on v2

--- a/solution.py
+++ b/solution.py
@@ -11,7 +11,7 @@
 TILES = LEN // TILE
 F32, BF16 = jnp.float32, jnp.bfloat16
 FORWARD_HEADS, BACKWARD_HEADS = 4, 2
-VMEM_LIMIT = 60 * 1024 * 1024
+VMEM_LIMIT = 65480 * 1024
 LOG2_E = 1.4426950408889634
 MATMUL_FLOPS = 2 * H * 10 * TILE * TILE * D
 
@@ -723,7 +723,10 @@
         out[m] = total[m * rows : (m + 1) * rows, :].astype(BF16)
     small = total[3 * rows :, :]
     groups = [small[:, g * 128 : g * 128 + H] for g in range(3)]
-    by_logits[...] = jnp.concatenate([groups[0], groups[1][:4]])
+    eye = lax.broadcasted_iota(jnp.int32, (H, H), 0) == lax.broadcasted_iota(jnp.int32, (H, H), 1)
+    by_logits[...] = lax.dot_general(
+        jnp.concatenate([groups[0], groups[1][:4]]), jnp.where(eye, DH ** -0.5, 0.0), (((0,), (0,)), ((), ())),
+        precision=lax.Precision.HIGHEST, preferred_element_type=F32)
     by_weights[...] = jnp.concatenate([groups[1][4:], groups[2]])
 
 
@@ -757,10 +760,11 @@
         out[at[0] ^ i] = ref[...]
 
 
-def tokens_of(at, came, name, first=()):
-    (out,), _ = plain_call(
-        partial(tokens_kernel, len(first)), list(came), at, [shape((4,) + came[0].shape)], name, (), first)
-    return out
+def tokens_of(at, came, name, first=(), through=()):
+    (out,), through = plain_call(
+        partial(tokens_kernel, len(first) + len(through)), list(came), at, [shape((4,) + came[0].shape)], name, (), first,
+        through)
+    return (out, *through) if through else out
 
 
 def weigh(out, weight):
@@ -1006,12 +1010,12 @@
         at, parts, grad_q, grad_k, grad_v, x, grad_middle, w_query, w_key, w_value, gain_one, one[0])
     shares, grad_in = project_reshare(spots, pair, exchange(one, plane), sizes[1], grad_in)
     own, by_logits, by_weights = [finish_sum(a, others) for a in project_piece(spots, exchange(shares, line))]
-    block_out = tokens_of(at, out, "block_out")
     grad_in = send_far(grad_in)
-    own = widen(spots, own[None], early_line, "stack_line", [block_out, grad_in[2]])
+    block_out, far = tokens_of(at, out, "block_out", [own], grad_in[2:])
+    grad_inputs = tokens_of(at, hand_on((*grad_in[:2], far)), "grad_inputs")
+    own = widen(spots, own[None], early_line, "stack_line", [grad_inputs])
     grad_w_back, grad_w_hidden, grad_w_out, grad_gain_two = fill(
         pieces, (row_starts(plane, line), row_starts(line, plane)), w_hidden, gain_two)
-    grad_inputs = tokens_of(at, hand_on(grad_in), "grad_inputs", [grad_w_out])
     own = widen(spots, own, late_plane, "stack_plane", [grad_w_out])
     grad_w_query, grad_w_key, grad_w_value, grad_gain_one = spread(
         where, sizes, own, swap(own, 1), w_query, w_key, w_value, gain_one, [grad_w_out])
@@ -1023,7 +1027,7 @@
         grad_w_key,
         grad_w_value,
         grad_w_out,
-        by_logits.T * scale,
+        by_logits,
         by_weights,
         grad_gain_two,
         grad_w_hidden,

time: 407 us -> 394 us (0.968)
  local copies, waits for them, and re-layouts: 22.3 us -> 10.3 us
    unnamed x93 -> x10, local copies, waits for them, and re-layouts: 17.2 us -> 0.76 us
  transfers between devices with their start and end apart: 41 -> 41, of which waited for: 12 -> 12; matrix products, arithmetic and copies ran while one was open for 1% -> 2% of each run, Pallas kernels for 48% -> 50%
where the time goes in v3:
time: 394 us; the launch traced here: 390 us
  Pallas kernels  271 us (69%)
  starting transfers between devices  47.4 us (12%)
  waiting for transfers between devices  43.9 us (11%)
  between operations  14.6 us (4%)
  local copies, waits for them, and re-layouts  10.3 us (3%)
    pallas_call x11, Pallas kernels, step_call(): pl.pallas_call(kernel, grid_spec=pltpu.PrefetchScalarGridSpec(num_scalar_...  113 us
    pallas_call x3, Pallas kernels, run(): pl.pallas_call(kernel, grid=(heads // BACKWARD_HEADS,), in_specs=in_specs...  76.6 us
    ppermute x38, waiting for transfers between devices, swap(): return lax.ppermute(values, BOTH, [(s, s ^ mask) for s in range(n)])  43.8 us
    pallas_call x1, Pallas kernels, attend(): pl.pallas_call(attend_kernel, grid=(H // heads,), in_specs=[SMEM, SMEM, w...  40.8 us
    ppermute x38, starting transfers between devices, swap(): return lax.ppermute(values, BOTH, [(s, s ^ mask) for s in range(n)])  38.5 us
    pallas_call x9, Pallas kernels, plain_call(): pl.pallas_call(kernel, in_specs=[SMEM] + [VMEM] * len(operands) + [ANY] *...  23.8 us
    pallas_call x1, Pallas kernels, fill(): pl.pallas_call(partial(fill_kernel, tuple((d * o for d, o in zip(down, ov...  16.7 us
    all_to_all x2, starting transfers between devices, trade(): lax.all_to_all(values, BOTH, split_axis=0, concat_axis=0, tiled=True, axi...  8.88 us
  transfers between devices with their start and end apart: 41, of which 12 were waited for; matrix products, arithmetic and copies ran while one was open for 2% of the time, Pallas kernels for 50%

profile of v3, /device:TPU:0, one launch (start us, length us, event | category | flops | bytes accessed | tf_op | source)
XLA Modules:
  0.0 389.6 jit_solution(10882636649584201596)
XLA Ops:
  7.2 2.4 dynamic-slice_bitcast_fusion
  10.1 2.5 collective-permute-start
  14.0 1.0 copy.40.id_col
  16.9 7.7 %project.2 = (bf16[1024,768]{1,0:T(8,128)(2,1)}, bf16[768,1024]{1,0:T(8,128)(2,1)}, bf16[1024,768]{1,0:T(8,128)(2,1)}, bf16[768,1024]{1,0:T(8,128)(2,1)}, bf16[1...) custom-call(s32[1]{0:T(128)} %bitcast.at, ...), custom_call_target="tpu_custom_call" | custom-call | flops 226492416 | bytes 786432 | tf_op jit(solution)/shard_map/project/pallas_call | solution.py:298
  24.8 1.9 collective-permute-start.4
  26.7 1.3 constant_dynamic-slice_fusion.id_row
  28.0 2.9 collective-permute-done.1.refs_1_
  30.9 6.3 %project.3 = (bf16[1024,768]{1,0:T(8,128)(2,1)}, bf16[768,1024]{1,0:T(8,128)(2,1)}, bf16[1024,768]{1,0:T(8,128)(2,1)}, bf16[768,1024]{1,0:T(8,128)(2,1)}, bf16[1...) custom-call(s32[1]{0:T(128)} %bitcast.at, ...), custom_call_target="tpu_custom_call", output_to_operand_aliasing={{0}: (7, {}), {1}: (8, {}), {2}: (9, {}), {3}: (10, {}), {4... | custom-call | flops 226492416 | bytes 786432 | tf_op jit(solution)/shard_map/project/pallas_call | solution.py:298
  37.2 40.8 %attend.1 = (bf16[12,1024,1024]{2,1,0:T(8,128)(2,1)}, bf16[1024,768]{1,0:T(8,128)(2,1)}) custom-call(f32[12,12]{1,0:T(8,128)} %convert_multiply_fusion.mix_l, f32[12,12]{1,0:T(8,128)} %convert_element_type.7.mix_w, s32[1,1024]{1,0:T(1,128)} %constant_dynamic-slice_fusion.id_row, s32[1024,1]{1,0:T(8,128)} %copy.40.id_col, ...), custom_call_target="tpu_custom_call" | custom-call | flops 3019898880 | bytes 1048576 | tf_op jit(solution)/shard_map/attend/pallas_call | solution.py:88
  78.0 36.1 %feed.1 = (bf16[256,768]{1,0:T(8,128)(2,1)}, bf16[256,768]{1,0:T(8,128)(2,1)}, bf16[2,256,768]{2,1,0:T(8,128)(2,1)}, bf16[1024,768]{1,0:T(8,128)(2,1)}, bf16[102...) custom-call(s32[1]{0:T(128)} %bitcast.at, ...), custom_call_target="tpu_custom_call" | custom-call | flops 2717908992 | bytes 786432 | tf_op jit(solution)/shard_map/feed/pallas_call | solution.py:298
  114.2 14.0 %wide_weight_grads.1 = (bf16[6,384,768]{2,1,0:T(8,128)(2,1)}, bf16[6,384,768]{2,1,0:T(8,128)(2,1)}) custom-call(s32[1]{0:T(128)} %bitcast.8.core, bf16[1024,3072]{1,0:T(8,128)(2,1)} %get-tuple-element.121.act_kept.act_sent, bf16[1024,3072]{1,0:T(8,128)(2,1)} %get-tuple-element.121.act_kept.act_sent, bf16[1024,768]{1,0:T(8,128)(2,1)} %get-tuple-element.122.cot, ...), custom_call_target="tpu_custom_call" | custom-call | flops 905969664 | bytes 786432 | tf_op jit(solution)/shard_map/wide_weight_grads/pallas_call | solution.py:298
  128.4 8.2 %thin_weight_grads.1 = (bf16[3,384,768]{2,1,0:T(8,128)(2,1)}, bf16[3,384,768]{2,1,0:T(8,128)(2,1)}) custom-call(s32[1]{0:T(128)} %bitcast.8.core, bf16[1024,768]{1,0:T(8,128)(2,1)} %get-tuple-element.123.n2_kept.n2_sent, bf16[1024,768]{1,0:T(8,128)(2,1)} %get-tuple-element.123.n2_kept.n2_sent, bf16[1024,3072]{1,0:T(8,128)(2,1)} %get-tuple-element.124.grad_hidden, ...), custom_call_target="tpu_custom_call" | custom-call | flops 452984832 | bytes 786432 | tf_op jit(solution)/shard_map/thin_weight_grads/pallas_call | solution.py:298
  136.9 3.8 collective-permute-done.8.d
  140.7 8.3 %shares.1 = (bf16[4,6,96,768]{3,2,1,0:T(8,128)(2,1)}, bf16[3,96,768]{2,1,0:T(8,128)(2,1)}, bf16[3,96,768]{2,1,0:T(8,128)(2,1)}, bf16[3,96,768]{2,1,0:T(8,128)(2,1)}, bf16[3,96,768]{2,1,0:T(8,128)(2,1)}) custom-call(s32[1]{0:T(128)} %bitcast.7.mine, bf16[6,384,768]{2,1,0:T(8,128)(2,1)} %get-tuple-element.125.refs_0_.a, ...), custom_call_target="tpu_custom_call" | custom-call | bytes 786432 | tf_op jit(solution)/shard_map/shares/pallas_call | solution.py:298
  149.0 4.7 %all-to-all-start = ((bf16[4,6,96,768]{3,2,1,0:T(8,128)(2,1)}), bf16[4,6,96,768]{3,2,1,0:T(8,128)(2,1)}, u32[]{:S(2)}, u32[]{:S(2)}) async-start(bf16[4,6,96,768]{3,2,1,0:T(8,128)(2,1)} %get-tuple-element.130.rest_0_), calls=%async_computation | async-start | bytes 7077888 | tf_op jit(solution)/shard_map/all_to_all | solution.py:937
  153.7 3.1 collective-permute-start.10
  156.8 1.3 collective-permute-start.11
  159.1 39.4 %query_grads.1 = (bf16[1024,768]{1,0:T(8,128)(2,1)}, bf16[12,1024,1024]{2,1,0:T(8,128)(2,1)}, f32[12,1,768]{2,1,0:T(1,128)}) custom-call(f32[12,12]{1,0:T(8,128)} %convert_element_type.7.mix_w, f32[12,12]{1,0:T(8,128)} %convert_multiply_fusion.mix_l, bf16[12,1024,1024]{2,1,0:T(8,128)(2,1)} %get-tuple-element.135.soft, ...), custom_call_target="tpu_custom_call" | custom-call | flops 3019898880 | bytes 1048576 | tf_op jit(solution)/shard_map/query_grads/pallas_call | solution.py:200
  198.5 4.5 %reshare.1 = (bf16[6,24,768]{2,1,0:T(8,128)(2,1)}, bf16[6,24,768]{2,1,0:T(8,128)(2,1)}, bf16[6,24,768]{2,1,0:T(8,128)(2,1)}, bf16[6,24,768]{2,1,0:T(8,128)(2,1)}...) custom-call(s32[2]{0:T(128)} %pad_add_fusion.mine, ...), custom_call_target="tpu_custom_call", output_to_operand_aliasing={{5}: (7, {})} | custom-call | tf_op jit(solution)/shard_map/reshare/pallas_call | solution.py:618
  203.0 1.9 collective-permute-start.15
  204.9 4.1 %all-to-all-start.1 = ((bf16[4,3,24,768]{3,2,1,0:T(8,128)(2,1)}), bf16[4,3,24,768]{3,2,1,0:T(8,128)(2,1)}, u32[]{:S(2)}, u32[]{:S(2)}) async-start(bf16[4,3,24,768]{3,2,1,0:T(8,128)(2,1)} %get-tuple-element.141), calls=%async_computation.1 | async-start | bytes 884736 | tf_op jit(solution)/shard_map/all_to_all | solution.py:937
  209.1 1.8 collective-permute-start.12
  211.0 1.7 collective-permute-start.13
  212.7 0.9 collective-permute-start.14
  213.6 17.8 %key_grads.1.refs_4_.refs_1_.grad_k = bf16[1024,768]{1,0:T(8,128)(2,1)} custom-call(f32[12,12]{1,0:T(8,128)} %convert_multiply_fusion.mix_l, bf16[12,1024,1024]{2,1,0:T(8,128)(2,1)} %get-tuple-element.146.grad_logits, bf16[1024,768]{1,0:T(8,128)(2,1)} %get-tuple-element.147.q, bf16[6,24,768]{2,1,0:T(8,128)(2,1)} %get-tuple-element.142.rest_0_.refs_0_), custom_call_target="tpu_custom_call" | custom-call | flops 1509949440 | bytes 1048576 | tf_op jit(solution)/shard_map/key_grads/pallas_call | solution.py:200
  231.4 2.3 piece.1
  233.7 6.2 %project_weight_grads.2 = (bf16[2,384,768]{2,1,0:T(8,128)(2,1)}, bf16[2,384,768]{2,1,0:T(8,128)(2,1)}) custom-call(s32[1]{0:T(128)} %bitcast.8.core, bf16[768,1024]{1,0:T(8,128)(2,1)} %get-tuple-element.150.nt_kept.nt_sent, bf16[768,1024]{1,0:T(8,128)(2,1)} %get-tuple-element.150.nt_kept.nt_sent, ...), custom_call_target="tpu_custom_call" | custom-call | flops 301989888 | bytes 786432 | tf_op jit(solution)/shard_map/project_weight_grads/pallas_call | solution.py:298
  240.4 1.8 slice_bitcast_fusion.1
  242.2 0.9 collective-permute-done.17.came
  243.1 2.7 split_pair.1
  245.8 1.9 collective-permute-start.18
  247.7 1.5 collective-permute-start.19
  249.3 19.4 %value_grads.1 = (bf16[1024,768]{1,0:T(8,128)(2,1)}, f32[12,1,768]{2,1,0:T(1,128)}) custom-call(f32[12,12]{1,0:T(8,128)} %convert_element_type.7.mix_w, bf16[12,1024,1024]{2,1,0:T(8,128)(2,1)} %get-tuple-element.135.soft, bf16[1024,768]{1,0:T(8,128)(2,1)} %get-tuple-element.136.v, bf16[1024,768]{1,0:T(8,128)(2,1)} %get-tuple-element.158.g, ...), custom_call_target="tpu_custom_call" | custom-call | flops 1509949440 | bytes 1048576 | tf_op jit(solution)/shard_map/value_grads/pallas_call | solution.py:200
  268.8 4.5 %project_weight_grads.3 = (bf16[1,400,768]{2,1,0:T(8,128)(2,1)}, bf16[1,400,768]{2,1,0:T(8,128)(2,1)}) custom-call(s32[1]{0:T(128)} %bitcast.8.core, bf16[768,1024]{1,0:T(8,128)(2,1)} %get-tuple-element.150.nt_kept.nt_sent, bf16[768,1024]{1,0:T(8,128)(2,1)} %get-tuple-element.150.nt_kept.nt_sent, bf16[1024,768]{1,0:T(8,128)(2,1)} %get-tuple-element.159.refs_0_.grad_v, ...), custom_call_target="tpu_custom_call" | custom-call | flops 150994944 | bytes 786432 | tf_op jit(solution)/shard_map/project_weight_grads/pallas_call | solution.py:298
  273.3 2.4 collective-permute-done.21.came
  275.7 2.3 split_one.1
  278.0 1.8 collective-permute-start.22
  279.9 1.5 collective-permute-start.23
  281.5 10.6 %input_grads.1 = (bf16[256,768]{1,0:T(8,128)(2,1)}, bf16[256,768]{1,0:T(8,128)(2,1)}, bf16[2,256,768]{2,1,0:T(8,128)(2,1)}) custom-call(s32[1]{0:T(128)} %bitcast.at, bf16[1024,768]{1,0:T(8,128)(2,1)} %get-tuple-element.139.refs_4_.refs_0_.grad_q, bf16[1024,768]{1,0:T(8,128)(2,1)} %key_grads.1.refs_4_.refs_1_.grad_k, ...), custom_call_target="tpu_custom_call" | custom-call | flops 452984832 | bytes 786432 | tf_op jit(solution)/shard_map/input_grads/pallas_call | solution.py:298
  292.1 2.6 project_reshare.1
  294.7 1.8 collective-permute-start.28
  296.6 1.2 collective-permute-start.25
  297.8 2.4 collective-permute-start.26
  300.1 0.8 collective-permute-start.27
  300.9 8.4 %collective-permute-done.25.refs_1_ = bf16[80,768]{1,0:T(8,128)(2,1)} collective-permute-done((bf16[80,768]{1,0:T(8,128)(2,1)}, bf16[80,768]{1,0:T(8,128)(2,1)}, u32[]{:S(2)}, u32[]{:S(2)}) %collective-permute-start.25) | collective-permute-done | bytes 122912 | tf_op jit(solution)/shard_map/ppermute | solution.py:882
  309.4 2.9 collective-permute-done.26.refs_2_
  312.2 4.4 %collective-permute-done.27.refs_3_ = bf16[80,768]{1,0:T(8,128)(2,1)} collective-permute-done((bf16[80,768]{1,0:T(8,128)(2,1)}, bf16[80,768]{1,0:T(8,128)(2,1)}, u32[]{:S(2)}, u32[]{:S(2)}) %collective-permute-start.27) | collective-permute-done | bytes 122912 | tf_op jit(solution)/shard_map/ppermute | solution.py:882
  316.6 1.9 project_piece.1
  318.5 5.3 %collective-permute-done.28.refs_5_ = bf16[2,256,768]{2,1,0:T(8,128)(2,1)} collective-permute-done((bf16[2,256,768]{2,1,0:T(8,128)(2,1)}, bf16[2,256,768]{2,1,0:T(8,128)(2,1)}, u32[]{:S(2)}, u32[]{:S(2)}) %collective-permute-start.28) | collective-permute-done | bytes 786464 | tf_op jit(solution)/shard_map/ppermute | solution.py:882
  323.9 2.9 block_out.1
  326.7 1.1 slice_bitcast_fusion
  328.0 1.6 collective-permute-start.31
  329.5 2.1 collective-permute-start.32
  333.2 2.7 grad_inputs.1.refs_4_
  335.9 5.4 %collective-permute-done.32.refs_2_ = bf16[1,3,24,768]{3,2,1,0:T(8,128)(2,1)} collective-permute-done((bf16[1,3,24,768]{3,2,1,0:T(8,128)(2,1)}, bf16[1,3,24,768]{3,2,1,0:T(8,128)(2,1)}, u32[]{:S(2)}, u32[]{:S(2)}) %collective-permute-start.32) | collective-permute-done | bytes 110624 | tf_op jit(solution)/shard_map/ppermute | solution.py:882
  341.2 1.7 collective-permute-done.33.refs_3_
  342.9 1.9 stack_line.1.refs_0_
  344.8 1.5 collective-permute-start.34
  346.5 1.8 collective-permute-start.36
  348.3 16.7 %fill.1 = (f32[3072,768]{1,0:T(8,128)}, f32[768,3072]{1,0:T(8,128)}, f32[768,768]{1,0:T(8,128)}, f32[768]{0:T(1024)}) custom-call(bf16[32,9,24,768]{3,2,1,0:T(8,128)(2,1)} %bitcast.20, bf16[768,3072]{1,0:T(8,128)(2,1)} %w_hidden.1, f32[1,768]{1,0:T(1,128)} %reshape.39.refs_7_.gain), custom_call_target="tpu_custom_call" | custom-call | tf_op jit(solution)/shard_map/fill/pallas_call | solution.py:865
  365.0 2.3 collective-permute-done.36.refs_3_
  367.3 2.8 stack_plane.1.own
  370.7 3.4 collective-permute-done.37.other
  374.1 8.4 %spread.1 = (f32[768,768]{1,0:T(8,128)}, f32[768,768]{1,0:T(8,128)}, f32[768,768]{1,0:T(8,128)}, f32[768]{0:T(1024)}) custom-call(s32[3]{0:T(128)} %pad_add_fusion.1.place, bf16[16,3,24,768]{3,2,1,0:T(8,128)(2,1)} %stack_plane.1.own, bf16[16,3,24,768]{3,2,1,0:T(8,128)(2,1)} %collective-permute-done.37.other, bf16[768,768]{1,0:T(8,128)(2,1)} %w_query.3, ...), custom_call_target="tpu_custom_call" | custom-call | bytes 786432 | tf_op jit(solution)/shard_map/spread/pallas_call | solution.py:298
  (66 shorter events, 8.6 us)
Async XLA Ops:
  7.2 6.2 %copy-start.3 = (f32[768]{0:T(1024)S(1)}, f32[768]{0:T(1024)}, u32[]{:S(2)}) copy-start(f32[768]{0:T(1024)} %param.15) | copy-start | bytes 9220
  7.2 7.9 %copy-start.1 = (bf16[12,12]{1,0:T(8,128)(2,1)S(1)}, bf16[12,12]{1,0:T(8,128)(2,1)}, u32[]{:S(2)}) copy-start(bf16[12,12]{1,0:T(8,128)(2,1)} %param.21) | copy-start | bytes 868
  7.2 8.4 %copy-start.4 = (f32[768]{0:T(1024)S(1)}, f32[768]{0:T(1024)}, u32[]{:S(2)}) copy-start(f32[768]{0:T(1024)} %param.22) | copy-start | bytes 9220
  7.2 9.0 %copy-start.2 = (bf16[12,12]{1,0:T(8,128)(2,1)S(1)}, bf16[12,12]{1,0:T(8,128)(2,1)}, u32[]{:S(2)}) copy-start(bf16[12,12]{1,0:T(8,128)(2,1)} %param.20) | copy-start | bytes 868
  9.6 7.2 %collective-permute-start.2 = (bf16[256,768]{1,0:T(8,128)(2,1)S(1)}, bf16[256,768]{1,0:T(8,128)(2,1)}, u32[]{:S(2)}, u32[]{:S(2)}) collective-permute-start(bf16[256,768]{1,0:T(8,128)(2,1)S(1)} %get-tuple-element.192), channel_id=1, source_target_pairs={{0,1},{1,0},{2,3},{3,2},{4,5},{5,4},{6,7},{7,6},{8,9},{9,8},{10,11... | collective-permute-start | bytes 1179656 | tf_op jit(solution)/shard_map/ppermute | solution.py:882
  10.1 17.9 %collective-permute-start = (bf16[256,768]{1,0:T(8,128)(2,1)}, bf16[256,768]{1,0:T(8,128)(2,1)}, u32[]{:S(2)}, u32[]{:S(2)}) collective-permute-start(bf16[256,768]{1,0:T(8,128)(2,1)} %get-tuple-element.194), channel_id=1, source_target_pairs={{0,2},{1,3},{2,0},{3,1},{4,6},{5,7},{6,4},{7,5},{8,10},{9,11},{10,... | collective-permute-start | bytes 1179656 | tf_op jit(solution)/shard_map/ppermute | solution.py:882
  12.6 18.3 %collective-permute-start.1 = (bf16[256,768]{1,0:T(8,128)(2,1)}, bf16[256,768]{1,0:T(8,128)(2,1)}, u32[]{:S(2)}, u32[]{:S(2)}) collective-permute-start(bf16[256,768]{1,0:T(8,128)(2,1)} %get-tuple-element.193), channel_id=1, source_target_pairs={{0,3},{1,2},{2,1},{3,0},{4,7},{5,6},{6,5},{7,4},{8,11},{9,10},{10,... | collective-permute-start | bytes 1179656 | tf_op jit(solution)/shard_map/ppermute | solution.py:882
  24.6 53.4 %collective-permute-start.3 = (bf16[256,768]{1,0:T(8,128)(2,1)}, bf16[256,768]{1,0:T(8,128)(2,1)}, u32[]{:S(2)}, u32[]{:S(2)}) collective-permute-start(bf16[256,768]{1,0:T(8,128)(2,1)} %get-tuple-element.116), channel_id=1, source_target_pairs={{0,1},{1,0},{2,3},{3,2},{4,5},{5,4},{6,7},{7,6},{8,9},{9,8},{10,11... | collective-permute-start | bytes 1179656 | tf_op jit(solution)/shard_map/ppermute | solution.py:882
  24.8 53.3 %collective-permute-start.4 = (bf16[256,768]{1,0:T(8,128)(2,1)}, bf16[256,768]{1,0:T(8,128)(2,1)}, u32[]{:S(2)}, u32[]{:S(2)}) collective-permute-start(bf16[256,768]{1,0:T(8,128)(2,1)} %get-tuple-element.117), channel_id=1, source_target_pairs={{0,2},{1,3},{2,0},{3,1},{4,6},{5,7},{6,4},{7,5},{8,10},{9,11},{10,... | collective-permute-start | bytes 1179656 | tf_op jit(solution)/shard_map/ppermute | solution.py:882
  26.7 51.4 %collective-permute-start.5 = (bf16[256,768]{1,0:T(8,128)(2,1)}, bf16[256,768]{1,0:T(8,128)(2,1)}, u32[]{:S(2)}, u32[]{:S(2)}) collective-permute-start(bf16[256,768]{1,0:T(8,128)(2,1)} %get-tuple-element.118), channel_id=1, source_target_pairs={{0,3},{1,2},{2,1},{3,0},{4,7},{5,6},{6,5},{7,4},{8,11},{9,10},{10,... | collective-permute-start | bytes 1179656 | tf_op jit(solution)/shard_map/ppermute | solution.py:882
  128.2 12.5 %collective-permute-start.7 = (bf16[6,384,768]{2,1,0:T(8,128)(2,1)}, bf16[6,384,768]{2,1,0:T(8,128)(2,1)}, u32[]{:S(2)}, u32[]{:S(2)}) collective-permute-start(bf16[6,384,768]{2,1,0:T(8,128)(2,1)} %get-tuple-element.126), channel_id=1, source_target_pairs={{0,1},{1,0},{2,3},{3,2},{4,5},{5,4},{6,7},{7,6},{8,9},{9,8},{10,11... | collective-permute-start | bytes 10616840 | tf_op jit(solution)/shard_map/ppermute | solution.py:882
  136.7 4.0 %collective-permute-start.8 = (bf16[3,384,768]{2,1,0:T(8,128)(2,1)}, bf16[3,384,768]{2,1,0:T(8,128)(2,1)}, u32[]{:S(2)}, u32[]{:S(2)}) collective-permute-start(bf16[3,384,768]{2,1,0:T(8,128)(2,1)} %get-tuple-element.129), channel_id=1, source_target_pairs={{0,1},{1,0},{2,3},{3,2},{4,5},{5,4},{6,7},{7,6},{8,9},{9,8},{10,11... | collective-permute-start | bytes 5308424 | tf_op jit(solution)/shard_map/ppermute | solution.py:882
  149.0 49.6 %all-to-all-start = ((bf16[4,6,96,768]{3,2,1,0:T(8,128)(2,1)}), bf16[4,6,96,768]{3,2,1,0:T(8,128)(2,1)}, u32[]{:S(2)}, u32[]{:S(2)}) async-start(bf16[4,6,96,768]{3,2,1,0:T(8,128)(2,1)} %get-tuple-element.130.rest_0_), calls=%async_computation | async-start | bytes 7077888 | tf_op jit(solution)/shard_map/all_to_all | solution.py:937
  153.7 44.8 %collective-permute-start.10 = (bf16[3,96,768]{2,1,0:T(8,128)(2,1)}, bf16[3,96,768]{2,1,0:T(8,128)(2,1)}, u32[]{:S(2)}, u32[]{:S(2)}) collective-permute-start(bf16[3,96,768]{2,1,0:T(8,128)(2,1)} %get-tuple-element.133), channel_id=1, source_target_pairs={{0,16},{1,17},{2,18},{3,19},{4,20},{5,21},{6,22},{7,23},{8,24},{9,... | collective-permute-start | bytes 1327112 | tf_op jit(solution)/shard_map/ppermute | solution.py:882
  156.8 41.7 %collective-permute-start.11 = (bf16[3,96,768]{2,1,0:T(8,128)(2,1)}, bf16[3,96,768]{2,1,0:T(8,128)(2,1)}, u32[]{:S(2)}, u32[]{:S(2)}) collective-permute-start(bf16[3,96,768]{2,1,0:T(8,128)(2,1)} %get-tuple-element.134), channel_id=1, source_target_pairs={{0,24},{1,25},{2,26},{3,27},{4,28},{5,29},{6,30},{7,31},{8,16},{9,... | collective-permute-start | bytes 1327112 | tf_op jit(solution)/shard_map/ppermute | solution.py:882
  158.2 40.4 %collective-permute-start.9 = (bf16[3,96,768]{2,1,0:T(8,128)(2,1)}, bf16[3,96,768]{2,1,0:T(8,128)(2,1)}, u32[]{:S(2)}, u32[]{:S(2)}) collective-permute-start(bf16[3,96,768]{2,1,0:T(8,128)(2,1)} %get-tuple-element.132), channel_id=1, source_target_pairs={{0,8},{1,9},{2,10},{3,11},{4,12},{5,13},{6,14},{7,15},{8,0},{9,1},... | collective-permute-start | bytes 1327112 | tf_op jit(solution)/shard_map/ppermute | solution.py:882
  203.0 28.4 %collective-permute-start.15 = (bf16[2,256,768]{2,1,0:T(8,128)(2,1)}, bf16[2,256,768]{2,1,0:T(8,128)(2,1)}, u32[]{:S(2)}, u32[]{:S(2)}) collective-permute-start(bf16[2,256,768]{2,1,0:T(8,128)(2,1)} %get-tuple-element.148), channel_id=1, source_target_pairs={{0,2},{1,3},{2,0},{3,1},{4,6},{5,7},{6,4},{7,5},{8,10},{9,11},{10,... | collective-permute-start | bytes 2359304 | tf_op jit(solution)/shard_map/ppermute | solution.py:882
  204.9 26.4 %all-to-all-start.1 = ((bf16[4,3,24,768]{3,2,1,0:T(8,128)(2,1)}), bf16[4,3,24,768]{3,2,1,0:T(8,128)(2,1)}, u32[]{:S(2)}, u32[]{:S(2)}) async-start(bf16[4,3,24,768]{3,2,1,0:T(8,128)(2,1)} %get-tuple-element.141), calls=%async_computation.1 | async-start | bytes 884736 | tf_op jit(solution)/shard_map/all_to_all | solution.py:937
  209.1 139.2 %all-gather.3.cloned.1.call-start = ((), (), s32[]{:S(2)}) async-start(), calls=%async_computation.2 | async-start | bytes 10948608 | tf_op jit(solution)/shard_map/all_gather | solution.py:1002
  209.1 22.2 %collective-permute-start.12 = (bf16[6,24,768]{2,1,0:T(8,128)(2,1)}, bf16[6,24,768]{2,1,0:T(8,128)(2,1)}, u32[]{:S(2)}, u32[]{:S(2)}) collective-permute-start(bf16[6,24,768]{2,1,0:T(8,128)(2,1)} %get-tuple-element.143), channel_id=1, source_target_pairs={{0,8},{1,9},{2,10},{3,11},{4,12},{5,13},{6,14},{7,15},{8,0},{9,1},... | collective-permute-start | bytes 663560 | tf_op jit(solution)/shard_map/ppermute | solution.py:882
  211.0 20.4 %collective-permute-start.13 = (bf16[6,24,768]{2,1,0:T(8,128)(2,1)}, bf16[6,24,768]{2,1,0:T(8,128)(2,1)}, u32[]{:S(2)}, u32[]{:S(2)}) collective-permute-start(bf16[6,24,768]{2,1,0:T(8,128)(2,1)} %get-tuple-element.144), channel_id=1, source_target_pairs={{0,16},{1,17},{2,18},{3,19},{4,20},{5,21},{6,22},{7,23},{8,24},{9,... | collective-permute-start | bytes 663560 | tf_op jit(solution)/shard_map/ppermute | solution.py:882
  212.7 18.7 %collective-permute-start.14 = (bf16[6,24,768]{2,1,0:T(8,128)(2,1)}, bf16[6,24,768]{2,1,0:T(8,128)(2,1)}, u32[]{:S(2)}, u32[]{:S(2)}) collective-permute-start(bf16[6,24,768]{2,1,0:T(8,128)(2,1)} %get-tuple-element.145), channel_id=1, source_target_pairs={{0,24},{1,25},{2,26},{3,27},{4,28},{5,29},{6,30},{7,31},{8,16},{9,... | collective-permute-start | bytes 663560 | tf_op jit(solution)/shard_map/ppermute | solution.py:882
  239.9 3.2 collective-permute-start.17
  239.9 28.8 %collective-permute-start.6 = (bf16[256,768]{1,0:T(8,128)(2,1)}, bf16[256,768]{1,0:T(8,128)(2,1)}, u32[]{:S(2)}, u32[]{:S(2)}) collective-permute-start(bf16[256,768]{1,0:T(8,128)(2,1)} %get-tuple-element.120), channel_id=1, source_target_pairs={{0,1},{1,0},{2,3},{3,2},{4,5},{5,4},{6,7},{7,6},{8,9},{9,8},{10,11... | collective-permute-start | bytes 1179656 | tf_op jit(solution)/shard_map/ppermute | solution.py:882
  242.2 26.6 %collective-permute-start.16 = (bf16[256,768]{1,0:T(8,128)(2,1)}, bf16[256,768]{1,0:T(8,128)(2,1)}, u32[]{:S(2)}, u32[]{:S(2)}) collective-permute-start(bf16[256,768]{1,0:T(8,128)(2,1)} %slice_bitcast_fusion.1), channel_id=1, source_target_pairs={{0,1},{1,0},{2,3},{3,2},{4,5},{5,4},{6,7},{7,6},{8,9},{9,8},{10,11... | collective-permute-start | bytes 1179656 | tf_op jit(solution)/shard_map/ppermute | solution.py:882
  245.8 23.0 %collective-permute-start.18 = (bf16[2,96,768]{2,1,0:T(8,128)(2,1)}, bf16[2,96,768]{2,1,0:T(8,128)(2,1)}, u32[]{:S(2)}, u32[]{:S(2)}) collective-permute-start(bf16[2,96,768]{2,1,0:T(8,128)(2,1)} %get-tuple-element.155), channel_id=1, source_target_pairs={{0,2},{1,3},{2,0},{3,1},{4,6},{5,7},{6,4},{7,5},{8,10},{9,11},{10,... | collective-permute-start | bytes 884744 | tf_op jit(solution)/shard_map/ppermute | solution.py:882
  247.7 21.1 %collective-permute-start.19 = (bf16[2,96,768]{2,1,0:T(8,128)(2,1)}, bf16[2,96,768]{2,1,0:T(8,128)(2,1)}, u32[]{:S(2)}, u32[]{:S(2)}) collective-permute-start(bf16[2,96,768]{2,1,0:T(8,128)(2,1)} %get-tuple-element.156), channel_id=1, source_target_pairs={{0,4},{1,5},{2,6},{3,7},{4,0},{5,1},{6,2},{7,3},{8,12},{9,13},{10,... | collective-permute-start | bytes 884744 | tf_op jit(solution)/shard_map/ppermute | solution.py:882
  249.1 19.6 %collective-permute-start.20 = (bf16[2,96,768]{2,1,0:T(8,128)(2,1)}, bf16[2,96,768]{2,1,0:T(8,128)(2,1)}, u32[]{:S(2)}, u32[]{:S(2)}) collective-permute-start(bf16[2,96,768]{2,1,0:T(8,128)(2,1)} %get-tuple-element.157), channel_id=1, source_target_pairs={{0,6},{1,7},{2,4},{3,5},{4,2},{5,3},{6,0},{7,1},{8,14},{9,15},{10,... | collective-permute-start | bytes 884744 | tf_op jit(solution)/shard_map/ppermute | solution.py:882
  273.3 2.4 collective-permute-start.21
  278.0 14.1 %collective-permute-start.22 = (bf16[104,768]{1,0:T(8,128)(2,1)}, bf16[104,768]{1,0:T(8,128)(2,1)}, u32[]{:S(2)}, u32[]{:S(2)}) collective-permute-start(bf16[104,768]{1,0:T(8,128)(2,1)} %get-tuple-element.165), channel_id=1, source_target_pairs={{0,2},{1,3},{2,0},{3,1},{4,6},{5,7},{6,4},{7,5},{8,10},{9,11},{10,... | collective-permute-start | bytes 479240 | tf_op jit(solution)/shard_map/ppermute | solution.py:882
  279.9 12.2 %collective-permute-start.23 = (bf16[104,768]{1,0:T(8,128)(2,1)}, bf16[104,768]{1,0:T(8,128)(2,1)}, u32[]{:S(2)}, u32[]{:S(2)}) collective-permute-start(bf16[104,768]{1,0:T(8,128)(2,1)} %get-tuple-element.166), channel_id=1, source_target_pairs={{0,4},{1,5},{2,6},{3,7},{4,0},{5,1},{6,2},{7,3},{8,12},{9,13},{10,... | collective-permute-start | bytes 479240 | tf_op jit(solution)/shard_map/ppermute | solution.py:882
  281.3 10.8 %collective-permute-start.24 = (bf16[104,768]{1,0:T(8,128)(2,1)}, bf16[104,768]{1,0:T(8,128)(2,1)}, u32[]{:S(2)}, u32[]{:S(2)}) collective-permute-start(bf16[104,768]{1,0:T(8,128)(2,1)} %get-tuple-element.167), channel_id=1, source_target_pairs={{0,6},{1,7},{2,4},{3,5},{4,2},{5,3},{6,0},{7,1},{8,14},{9,15},{10,... | collective-permute-start | bytes 479240 | tf_op jit(solution)/shard_map/ppermute | solution.py:882
  294.7 29.1 %collective-permute-start.28 = (bf16[2,256,768]{2,1,0:T(8,128)(2,1)}, bf16[2,256,768]{2,1,0:T(8,128)(2,1)}, u32[]{:S(2)}, u32[]{:S(2)}) collective-permute-start(bf16[2,256,768]{2,1,0:T(8,128)(2,1)} %get-tuple-element.177), channel_id=1, source_target_pairs={{0,2},{1,3},{2,0},{3,1},{4,6},{5,7},{6,4},{7,5},{8,10},{9,11},{10,... | collective-permute-start | bytes 2359304 | tf_op jit(solution)/shard_map/ppermute | solution.py:882
  296.6 12.8 %collective-permute-start.25 = (bf16[80,768]{1,0:T(8,128)(2,1)}, bf16[80,768]{1,0:T(8,128)(2,1)}, u32[]{:S(2)}, u32[]{:S(2)}) collective-permute-start(bf16[80,768]{1,0:T(8,128)(2,1)} %get-tuple-element.173), channel_id=1, source_target_pairs={{0,8},{1,9},{2,10},{3,11},{4,12},{5,13},{6,14},{7,15},{8,0},{9,1},... | collective-permute-start | bytes 368648 | tf_op jit(solution)/shard_map/ppermute | solution.py:882
  297.8 14.5 %collective-permute-start.26 = (bf16[80,768]{1,0:T(8,128)(2,1)}, bf16[80,768]{1,0:T(8,128)(2,1)}, u32[]{:S(2)}, u32[]{:S(2)}) collective-permute-start(bf16[80,768]{1,0:T(8,128)(2,1)} %get-tuple-element.174), channel_id=1, source_target_pairs={{0,16},{1,17},{2,18},{3,19},{4,20},{5,21},{6,22},{7,23},{8,24},{9,... | collective-permute-start | bytes 368648 | tf_op jit(solution)/shard_map/ppermute | solution.py:882
  300.1 16.5 %collective-permute-start.27 = (bf16[80,768]{1,0:T(8,128)(2,1)}, bf16[80,768]{1,0:T(8,128)(2,1)}, u32[]{:S(2)}, u32[]{:S(2)}) collective-permute-start(bf16[80,768]{1,0:T(8,128)(2,1)} %get-tuple-element.175), channel_id=1, source_target_pairs={{0,24},{1,25},{2,26},{3,27},{4,28},{5,29},{6,30},{7,31},{8,16},{9,... | collective-permute-start | bytes 368648 | tf_op jit(solution)/shard_map/ppermute | solution.py:882
  300.9 31.5 %collective-permute-start.29 = (bf16[256,768]{1,0:T(8,128)(2,1)}, bf16[256,768]{1,0:T(8,128)(2,1)}, u32[]{:S(2)}, u32[]{:S(2)}) collective-permute-start(bf16[256,768]{1,0:T(8,128)(2,1)} %get-tuple-element.180), channel_id=1, source_target_pairs={{0,1},{1,0},{2,3},{3,2},{4,5},{5,4},{6,7},{7,6},{8,9},{9,8},{10,11... | collective-permute-start | bytes 1179656 | tf_op jit(solution)/shard_map/ppermute | solution.py:882
  327.9 4.5 %collective-permute-start.30 = (bf16[256,768]{1,0:T(8,128)(2,1)S(1)}, bf16[256,768]{1,0:T(8,128)(2,1)S(1)}, u32[]{:S(2)}, u32[]{:S(2)}) collective-permute-start(bf16[256,768]{1,0:T(8,128)(2,1)S(1)} %slice_bitcast_fusion), channel_id=1, source_target_pairs={{0,1},{1,0},{2,3},{3,2},{4,5},{5,4},{6,7},{7,6},{8,9},{9,8},{10,11... | collective-permute-start | bytes 1179656 | tf_op jit(solution)/shard_map/ppermute | solution.py:882
  328.0 7.9 %collective-permute-start.31 = (bf16[1,3,24,768]{3,2,1,0:T(8,128)(2,1)}, bf16[1,3,24,768]{3,2,1,0:T(8,128)(2,1)}, u32[]{:S(2)}, u32[]{:S(2)}) collective-permute-start(bf16[1,3,24,768]{3,2,1,0:T(8,128)(2,1)} %bitcast.21), channel_id=1, source_target_pairs={{0,2},{1,3},{2,0},{3,1},{4,6},{5,7},{6,4},{7,5},{8,10},{9,11},{10,... | collective-permute-start | bytes 331784 | tf_op jit(solution)/shard_map/ppermute | solution.py:882
  329.5 11.7 %collective-permute-start.32 = (bf16[1,3,24,768]{3,2,1,0:T(8,128)(2,1)}, bf16[1,3,24,768]{3,2,1,0:T(8,128)(2,1)}, u32[]{:S(2)}, u32[]{:S(2)}) collective-permute-start(bf16[1,3,24,768]{3,2,1,0:T(8,128)(2,1)} %bitcast.22), channel_id=1, source_target_pairs={{0,16},{1,17},{2,18},{3,19},{4,20},{5,21},{6,22},{7,23},{8,24},{9,... | collective-permute-start | bytes 331784 | tf_op jit(solution)/shard_map/ppermute | solution.py:882
  331.6 11.3 %collective-permute-start.33 = (bf16[1,3,24,768]{3,2,1,0:T(8,128)(2,1)}, bf16[1,3,24,768]{3,2,1,0:T(8,128)(2,1)}, u32[]{:S(2)}, u32[]{:S(2)}) collective-permute-start(bf16[1,3,24,768]{3,2,1,0:T(8,128)(2,1)} %bitcast.23), channel_id=1, source_target_pairs={{0,18},{1,19},{2,16},{3,17},{4,22},{5,23},{6,20},{7,21},{8,26},{9,... | collective-permute-start | bytes 331784 | tf_op jit(solution)/shard_map/ppermute | solution.py:882
  332.4 0.7 copy-start
  344.8 20.2 %collective-permute-start.34 = (bf16[4,3,24,768]{3,2,1,0:T(8,128)(2,1)}, bf16[4,3,24,768]{3,2,1,0:T(8,128)(2,1)}, u32[]{:S(2)}, u32[]{:S(2)}) collective-permute-start(bf16[4,3,24,768]{3,2,1,0:T(8,128)(2,1)} %stack_line.1.refs_0_), channel_id=1, source_target_pairs={{0,4},{1,5},{2,6},{3,7},{4,0},{5,1},{6,2},{7,3},{8,12},{9,13},{10,... | collective-permute-start | bytes 1327112 | tf_op jit(solution)/shard_map/ppermute | solution.py:882
  346.3 18.7 %collective-permute-start.35 = (bf16[4,3,24,768]{3,2,1,0:T(8,128)(2,1)}, bf16[4,3,24,768]{3,2,1,0:T(8,128)(2,1)}, u32[]{:S(2)}, u32[]{:S(2)}) collective-permute-start(bf16[4,3,24,768]{3,2,1,0:T(8,128)(2,1)} %stack_line.1.refs_0_), channel_id=1, source_target_pairs={{0,8},{1,9},{2,10},{3,11},{4,12},{5,13},{6,14},{7,15},{8,0},{9,1},... | collective-permute-start | bytes 1327112 | tf_op jit(solution)/shard_map/ppermute | solution.py:882
  346.5 20.9 %collective-permute-start.36 = (bf16[4,3,24,768]{3,2,1,0:T(8,128)(2,1)}, bf16[4,3,24,768]{3,2,1,0:T(8,128)(2,1)}, u32[]{:S(2)}, u32[]{:S(2)}) collective-permute-start(bf16[4,3,24,768]{3,2,1,0:T(8,128)(2,1)} %stack_line.1.refs_0_), channel_id=1, source_target_pairs={{0,12},{1,13},{2,14},{3,15},{4,8},{5,9},{6,10},{7,11},{8,4},{9,5},... | collective-permute-start | bytes 1327112 | tf_op jit(solution)/shard_map/ppermute | solution.py:882
  370.1 4.0 %collective-permute-start.37 = (bf16[16,3,24,768]{3,2,1,0:T(8,128)(2,1)}, bf16[16,3,24,768]{3,2,1,0:T(8,128)(2,1)}, u32[]{:S(2)}, u32[]{:S(2)}) collective-permute-start(bf16[16,3,24,768]{3,2,1,0:T(8,128)(2,1)} %stack_plane.1.own), channel_id=1, source_target_pairs={{0,1},{1,0},{2,3},{3,2},{4,5},{5,4},{6,7},{7,6},{8,9},{9,8},{10,11... | collective-permute-start | bytes 5308424 | tf_op jit(solution)/shard_map/ppermute | solution.py:882
Sparse Core Ops, SparseCore 0:
  233.8 97.2 all-gather.2

commit v4 on v3

--- a/solution.py
+++ b/solution.py
@@ -746,12 +746,12 @@
         at += ref.shape[0]
 
 
-def stack(mine, parts, name, first=()):
+def stack(mine, parts, name, first=(), through=()):
     rows = sum(p.shape[0] for p in parts)
-    (out,), _ = plain_call(
-        partial(stack_kernel, len(parts), len(first)), list(parts), mine, [shape((rows,) + parts[0].shape[1:])], name,
-        (), first)
-    return out
+    (out,), through = plain_call(
+        partial(stack_kernel, len(parts), len(first) + len(through)), list(parts), mine,
+        [shape((rows,) + parts[0].shape[1:])], name, (), first, through)
+    return (out, *through) if through else out
 
 
 def tokens_kernel(waits, at, *refs):
@@ -831,6 +831,7 @@
 
 
 def fill_kernel(counts, wide_count, starts, pieces, w_hidden, gain, *refs):
+    refs = refs[-5:]
     outs, by_gain, weighed = refs[:3], refs[3], refs[4]
     matrix, begin, rows = pl.program_id(0), 0, pieces.shape[2]
 
@@ -856,7 +857,7 @@
         by_gain[...] = (as_row(weighed) / gain[...])[0]
 
 
-def fill(pieces, starts, w_hidden, gain):
+def fill(pieces, starts, w_hidden, gain, first):
     blocks = w_hidden.shape[1] // D
     down, over = (blocks, 1, 1), (1, blocks, 1)
     out_specs, out_shape, count, places = matrix_outs(down, over)
@@ -865,13 +866,14 @@
     return pl.pallas_call(
         partial(fill_kernel, tuple(d * o for d, o in zip(down, over)), wide_and_thin(blocks)[0], starts),
         grid=(count,),
-        in_specs=[pl.BlockSpec((devices, 1, rows, D), lambda m: (0, m, 0, 0)), pl.BlockSpec((D, D), places[1]), line],
+        in_specs=[pl.BlockSpec((devices, 1, rows, D), lambda m: (0, m, 0, 0)), pl.BlockSpec((D, D), places[1]), line]
+        + [ANY] * len(first),
         out_specs=out_specs + [whole((D,))],
         out_shape=out_shape + [shape((D,), F32)],
         scratch_shapes=[pltpu.VMEM((D, 128), F32)],
         compiler_params=params(),
         name="fill",
-    )(pieces, w_hidden, gain)
+    )(pieces, w_hidden, gain, *first)
 
 
 BOTH = ("rows", "seq")
@@ -937,8 +939,8 @@
     return lax.all_to_all(values, BOTH, split_axis=0, concat_axis=0, tiled=True, axis_index_groups=groups)
 
 
-def widen(mine, values, dims, name, first=()):
-    return stack(mine, exchange([values] * (1 << len(dims)), dims), name, first)
+def widen(mine, values, dims, name, first=(), through=()):
+    return stack(mine, exchange([values] * (1 << len(dims)), dims), name, first, through)
 
 
 def send_far(parts):
@@ -994,31 +996,30 @@
     wide, thin = shares_of(
         spots[1:], wide_kept, swap(wide_sent, 1), thin_kept, swap(thin_sent, 1), sizes[0], sizes[1], [thin_kept])
     grad_q, grad_logits, by_logits = query_grads(mix_w, mix_l, soft, v, g_t, k_t, q_t, [wide, thin[0]])
-    wide, thin, far = reshare(spots, trade(wide, plane), exchange(thin, line), [grad_q], out[2:])
-    out = send_far((*out[:2], *far))
+    wide, thin, _ = reshare(spots, trade(wide, plane), exchange(thin, line), [grad_q], [])
     grad_k = key_grads(mix_l, grad_logits, q, [wide[0]])
-    piece, far = piece_of(spots, exchange(wide, line), trade(thin, plane), [grad_k], out[2:])
-    out = hand_on((*out[:2], *far))
+    piece, _ = piece_of(spots, exchange(wide, line), trade(thin, plane), [grad_k], [])
     pieces = lax.all_gather(finish_sum(piece, others), BOTH, axis=0)
     pair_kept, pair_sent = project_weight_grads(core, normed_t, [grad_q, grad_k], (), [piece])
     pair = split(spots[:1], pair_kept, swap(pair_sent, 1), sizes[0], "split_pair")
     grad_v, by_weights = value_grads(mix_w, soft, v, g, [piece, pair[0]])
     pair = exchange(pair, plane)
-    one_kept, one_sent = project_weight_grads(core, normed_t, [grad_v], [by_logits, by_weights], [*pair[1:], out[1], out[3]])
+    one_kept, one_sent = project_weight_grads(core, normed_t, [grad_v], [by_logits, by_weights], pair[1:])
     one = split_small(spots[:1], one_kept, swap(one_sent, 1), sizes[0], "split_one")
     grad_in = input_grads(
         at, parts, grad_q, grad_k, grad_v, x, grad_middle, w_query, w_key, w_value, gain_one, one[0])
-    shares, grad_in = project_reshare(spots, pair, exchange(one, plane), sizes[1], grad_in)
+    shares, (*grad_in, far) = project_reshare(spots, pair, exchange(one, plane), sizes[1], [*grad_in, out[2]])
+    out = hand_on(send_far((*out[:2], far)))
     own, by_logits, by_weights = [finish_sum(a, others) for a in project_piece(spots, exchange(shares, line))]
+    block_out = tokens_of(at, out, "block_out", [own])
+    own, *grad_in = widen(spots, own[None], early_line, "stack_line", [block_out], grad_in)
     grad_in = send_far(grad_in)
-    block_out, far = tokens_of(at, out, "block_out", [own], grad_in[2:])
-    grad_inputs = tokens_of(at, hand_on((*grad_in[:2], far)), "grad_inputs")
-    own = widen(spots, own[None], early_line, "stack_line", [grad_inputs])
     grad_w_back, grad_w_hidden, grad_w_out, grad_gain_two = fill(
-        pieces, (row_starts(plane, line), row_starts(line, plane)), w_hidden, gain_two)
-    own = widen(spots, own, late_plane, "stack_plane", [grad_w_out])
+        pieces, (row_starts(plane, line), row_starts(line, plane)), w_hidden, gain_two, [own])
+    own = widen(spots, own, late_plane, "stack_plane", [grad_w_out, grad_in[2]])
+    grad_inputs = tokens_of(at, hand_on(grad_in), "grad_inputs", [own])
     grad_w_query, grad_w_key, grad_w_value, grad_gain_one = spread(
-        where, sizes, own, swap(own, 1), w_query, w_key, w_value, gain_one, [grad_w_out])
+        where, sizes, own, swap(own, 1), w_query, w_key, w_value, gain_one, [grad_inputs])
     return (
         block_out,
         grad_inputs,

time: 394 us -> 411 us (1.043)
  waiting for transfers between devices: 43.9 us -> 60.9 us
    ppermute x38, waiting for transfers between devices: 43.8 us -> 60.9 us  [swap(): return lax.ppermute(values, BOTH, [(s, s ^ mask) for s in range(n)])]
  transfers between devices with their start and end apart: 41 -> 41, of which waited for: 12 -> 12; matrix products, arithmetic and copies ran while one was open for 2% -> 2% of each run, Pallas kernels for 50% -> 48%
where the time goes in v4:
time: 411 us; the launch traced here: 407 us
  Pallas kernels  271 us (66%)
  waiting for transfers between devices  60.9 us (15%)
  starting transfers between devices  47.1 us (11%)
  between operations  14.5 us (4%)
  local copies, waits for them, and re-layouts  10.7 us (3%)
    pallas_call x11, Pallas kernels, step_call(): pl.pallas_call(kernel, grid_spec=pltpu.PrefetchScalarGridSpec(num_scalar_...  113 us
    pallas_call x3, Pallas kernels, run(): pl.pallas_call(kernel, grid=(heads // BACKWARD_HEADS,), in_specs=in_specs...  76.7 us
    ppermute x38, waiting for transfers between devices, swap(): return lax.ppermute(values, BOTH, [(s, s ^ mask) for s in range(n)])  60.9 us
    pallas_call x1, Pallas kernels, attend(): pl.pallas_call(attend_kernel, grid=(H // heads,), in_specs=[SMEM, SMEM, w...  40.9 us
    ppermute x38, starting transfers between devices, swap(): return lax.ppermute(values, BOTH, [(s, s ^ mask) for s in range(n)])  38.2 us
    pallas_call x9, Pallas kernels, plain_call(): pl.pallas_call(kernel, in_specs=[SMEM] + [VMEM] * len(operands) + [ANY] *...  23.6 us
    pallas_call x1, Pallas kernels, fill(): pl.pallas_call(partial(fill_kernel, tuple((d * o for d, o in zip(down, ov...  16.7 us
    all_to_all x2, starting transfers between devices, trade(): lax.all_to_all(values, BOTH, split_axis=0, concat_axis=0, tiled=True, axi...  8.86 us
  transfers between devices with their start and end apart: 41, of which 12 were waited for; matrix products, arithmetic and copies ran while one was open for 2% of the time, Pallas kernels for 48%

profile of v4, /device:TPU:0, one launch (start us, length us, event | category | flops | bytes accessed | tf_op | source)
XLA Modules:
  0.0 406.9 jit_solution(1320941083295318679)
XLA Ops:
  7.2 2.4 dynamic-slice_bitcast_fusion
  10.1 2.5 collective-permute-start
  12.7 0.7 fusion
  14.6 1.0 copy.41.id_col
  16.9 7.8 %project.2 = (bf16[1024,768]{1,0:T(8,128)(2,1)}, bf16[768,1024]{1,0:T(8,128)(2,1)}, bf16[1024,768]{1,0:T(8,128)(2,1)}, bf16[768,1024]{1,0:T(8,128)(2,1)}, bf16[1...) custom-call(s32[1]{0:T(128)} %bitcast.at, ...), custom_call_target="tpu_custom_call" | custom-call | flops 226492416 | bytes 786432 | tf_op jit(solution)/shard_map/project/pallas_call | solution.py:298
  24.8 1.9 collective-permute-start.4
  26.7 1.3 constant_dynamic-slice_fusion.id_row
  28.0 2.9 collective-permute-done.1.refs_1_
  30.9 6.3 %project.3 = (bf16[1024,768]{1,0:T(8,128)(2,1)}, bf16[768,1024]{1,0:T(8,128)(2,1)}, bf16[1024,768]{1,0:T(8,128)(2,1)}, bf16[768,1024]{1,0:T(8,128)(2,1)}, bf16[1...) custom-call(s32[1]{0:T(128)} %bitcast.at, ...), custom_call_target="tpu_custom_call", output_to_operand_aliasing={{0}: (7, {}), {1}: (8, {}), {2}: (9, {}), {3}: (10, {}), {4... | custom-call | flops 226492416 | bytes 786432 | tf_op jit(solution)/shard_map/project/pallas_call | solution.py:298
  37.2 40.9 %attend.1 = (bf16[12,1024,1024]{2,1,0:T(8,128)(2,1)}, bf16[1024,768]{1,0:T(8,128)(2,1)}) custom-call(f32[12,12]{1,0:T(8,128)} %convert_multiply_fusion.mix_l, f32[12,12]{1,0:T(8,128)} %convert_element_type.7.mix_w, s32[1,1024]{1,0:T(1,128)} %constant_dynamic-slice_fusion.id_row, s32[1024,1]{1,0:T(8,128)} %copy.41.id_col, ...), custom_call_target="tpu_custom_call" | custom-call | flops 3019898880 | bytes 1048576 | tf_op jit(solution)/shard_map/attend/pallas_call | solution.py:88
  78.1 36.2 %feed.1 = (bf16[256,768]{1,0:T(8,128)(2,1)}, bf16[256,768]{1,0:T(8,128)(2,1)}, bf16[2,256,768]{2,1,0:T(8,128)(2,1)}, bf16[1024,768]{1,0:T(8,128)(2,1)}, bf16[102...) custom-call(s32[1]{0:T(128)} %bitcast.at, ...), custom_call_target="tpu_custom_call" | custom-call | flops 2717908992 | bytes 786432 | tf_op jit(solution)/shard_map/feed/pallas_call | solution.py:298
  114.2 14.0 %wide_weight_grads.1 = (bf16[6,384,768]{2,1,0:T(8,128)(2,1)}, bf16[6,384,768]{2,1,0:T(8,128)(2,1)}) custom-call(s32[1]{0:T(128)} %bitcast.8.core, bf16[1024,3072]{1,0:T(8,128)(2,1)} %get-tuple-element.126.act_kept.act_sent, bf16[1024,3072]{1,0:T(8,128)(2,1)} %get-tuple-element.126.act_kept.act_sent, bf16[1024,768]{1,0:T(8,128)(2,1)} %get-tuple-element.127.cot, ...), custom_call_target="tpu_custom_call" | custom-call | flops 905969664 | bytes 786432 | tf_op jit(solution)/shard_map/wide_weight_grads/pallas_call | solution.py:298
  128.5 8.2 %thin_weight_grads.1 = (bf16[3,384,768]{2,1,0:T(8,128)(2,1)}, bf16[3,384,768]{2,1,0:T(8,128)(2,1)}) custom-call(s32[1]{0:T(128)} %bitcast.8.core, bf16[1024,768]{1,0:T(8,128)(2,1)} %get-tuple-element.128.n2_kept.n2_sent, bf16[1024,768]{1,0:T(8,128)(2,1)} %get-tuple-element.128.n2_kept.n2_sent, bf16[1024,3072]{1,0:T(8,128)(2,1)} %get-tuple-element.129.grad_hidden, ...), custom_call_target="tpu_custom_call" | custom-call | flops 452984832 | bytes 786432 | tf_op jit(solution)/shard_map/thin_weight_grads/pallas_call | solution.py:298
  137.0 3.7 collective-permute-done.8.d
  140.7 8.3 %shares.1 = (bf16[4,6,96,768]{3,2,1,0:T(8,128)(2,1)}, bf16[3,96,768]{2,1,0:T(8,128)(2,1)}, bf16[3,96,768]{2,1,0:T(8,128)(2,1)}, bf16[3,96,768]{2,1,0:T(8,128)(2,1)}, bf16[3,96,768]{2,1,0:T(8,128)(2,1)}) custom-call(s32[1]{0:T(128)} %bitcast.7.mine, bf16[6,384,768]{2,1,0:T(8,128)(2,1)} %get-tuple-element.130.refs_0_.a, ...), custom_call_target="tpu_custom_call" | custom-call | bytes 786432 | tf_op jit(solution)/shard_map/shares/pallas_call | solution.py:298
  149.0 4.7 %all-to-all-start = ((bf16[4,6,96,768]{3,2,1,0:T(8,128)(2,1)}), bf16[4,6,96,768]{3,2,1,0:T(8,128)(2,1)}, u32[]{:S(2)}, u32[]{:S(2)}) async-start(bf16[4,6,96,768]{3,2,1,0:T(8,128)(2,1)} %get-tuple-element.135.rest_0_), calls=%async_computation | async-start | bytes 7077888 | tf_op jit(solution)/shard_map/all_to_all | solution.py:939
  153.7 2.1 collective-permute-start.9
  155.8 2.6 collective-permute-start.10
  159.0 39.4 %query_grads.1 = (bf16[1024,768]{1,0:T(8,128)(2,1)}, bf16[12,1024,1024]{2,1,0:T(8,128)(2,1)}, f32[12,1,768]{2,1,0:T(1,128)}) custom-call(f32[12,12]{1,0:T(8,128)} %convert_element_type.7.mix_w, f32[12,12]{1,0:T(8,128)} %convert_multiply_fusion.mix_l, bf16[12,1024,1024]{2,1,0:T(8,128)(2,1)} %get-tuple-element.122.soft, ...), custom_call_target="tpu_custom_call" | custom-call | flops 3019898880 | bytes 1048576 | tf_op jit(solution)/shard_map/query_grads/pallas_call | solution.py:200
  198.5 4.5 %reshare.1 = (bf16[6,24,768]{2,1,0:T(8,128)(2,1)}, bf16[6,24,768]{2,1,0:T(8,128)(2,1)}, bf16[6,24,768]{2,1,0:T(8,128)(2,1)}, bf16[6,24,768]{2,1,0:T(8,128)(2,1)}, bf16[4,3,24,768]{3,2,1,0:T(8,128)(2,1)}) custom-call(s32[2]{0:T(128)} %pad_add_fusion.mine, bf16[4,6,96,768]{3,2,1,0:T(8,128)(2,1)} %all-to-all-done.wide, ...), custom_call_target="tpu_custom_call" | custom-call | tf_op jit(solution)/shard_map/reshare/pallas_call | solution.py:618
  203.0 4.1 %all-to-all-start.1 = ((bf16[4,3,24,768]{3,2,1,0:T(8,128)(2,1)}), bf16[4,3,24,768]{3,2,1,0:T(8,128)(2,1)}, u32[]{:S(2)}, u32[]{:S(2)}) async-start(bf16[4,3,24,768]{3,2,1,0:T(8,128)(2,1)} %get-tuple-element.144), calls=%async_computation.1 | async-start | bytes 884736 | tf_op jit(solution)/shard_map/all_to_all | solution.py:939
  207.2 1.0 collective-permute-start.12
  208.1 3.5 collective-permute-start.13
  211.6 17.8 %key_grads.1.refs_4_.refs_1_.grad_k = bf16[1024,768]{1,0:T(8,128)(2,1)} custom-call(f32[12,12]{1,0:T(8,128)} %convert_multiply_fusion.mix_l, bf16[12,1024,1024]{2,1,0:T(8,128)(2,1)} %get-tuple-element.138.grad_logits, bf16[1024,768]{1,0:T(8,128)(2,1)} %get-tuple-element.139.q, bf16[6,24,768]{2,1,0:T(8,128)(2,1)} %get-tuple-element.143.rest_0_.refs_0_), custom_call_target="tpu_custom_call" | custom-call | flops 1509949440 | bytes 1048576 | tf_op jit(solution)/shard_map/key_grads/pallas_call | solution.py:200
  229.4 2.3 piece.1.refs_2_.rest_0_
  231.7 6.2 %project_weight_grads.2 = (bf16[2,384,768]{2,1,0:T(8,128)(2,1)}, bf16[2,384,768]{2,1,0:T(8,128)(2,1)}) custom-call(s32[1]{0:T(128)} %bitcast.8.core, bf16[768,1024]{1,0:T(8,128)(2,1)} %get-tuple-element.121.nt_kept.nt_sent, bf16[768,1024]{1,0:T(8,128)(2,1)} %get-tuple-element.121.nt_kept.nt_sent, ...), custom_call_target="tpu_custom_call" | custom-call | flops 301989888 | bytes 786432 | tf_op jit(solution)/shard_map/project_weight_grads/pallas_call | solution.py:298
  237.9 3.2 collective-permute-done.15.came
  241.1 2.7 split_pair.1
  243.9 1.9 collective-permute-start.16
  245.8 1.5 collective-permute-start.17
  247.3 19.5 %value_grads.1 = (bf16[1024,768]{1,0:T(8,128)(2,1)}, f32[12,1,768]{2,1,0:T(1,128)}) custom-call(f32[12,12]{1,0:T(8,128)} %convert_element_type.7.mix_w, bf16[12,1024,1024]{2,1,0:T(8,128)(2,1)} %get-tuple-element.122.soft, bf16[1024,768]{1,0:T(8,128)(2,1)} %get-tuple-element.123.v, bf16[1024,768]{1,0:T(8,128)(2,1)} %get-tuple-element.154.g, ...), custom_call_target="tpu_custom_call" | custom-call | flops 1509949440 | bytes 1048576 | tf_op jit(solution)/shard_map/value_grads/pallas_call | solution.py:200
  266.8 4.5 %project_weight_grads.3 = (bf16[1,400,768]{2,1,0:T(8,128)(2,1)}, bf16[1,400,768]{2,1,0:T(8,128)(2,1)}) custom-call(s32[1]{0:T(128)} %bitcast.8.core, bf16[768,1024]{1,0:T(8,128)(2,1)} %get-tuple-element.121.nt_kept.nt_sent, bf16[768,1024]{1,0:T(8,128)(2,1)} %get-tuple-element.121.nt_kept.nt_sent, bf16[1024,768]{1,0:T(8,128)(2,1)} %get-tuple-element.155.refs_0_.grad_v, ...), custom_call_target="tpu_custom_call" | custom-call | flops 150994944 | bytes 786432 | tf_op jit(solution)/shard_map/project_weight_grads/pallas_call | solution.py:298
  271.3 2.4 collective-permute-done.19.came
  273.7 2.3 split_one.1
  276.0 1.9 collective-permute-start.20
  277.9 1.5 collective-permute-start.21
  279.5 10.8 %input_grads.1 = (bf16[256,768]{1,0:T(8,128)(2,1)}, bf16[256,768]{1,0:T(8,128)(2,1)}, bf16[2,256,768]{2,1,0:T(8,128)(2,1)}) custom-call(s32[1]{0:T(128)} %bitcast.at, bf16[1024,768]{1,0:T(8,128)(2,1)} %get-tuple-element.137.refs_4_.refs_0_.grad_q, bf16[1024,768]{1,0:T(8,128)(2,1)} %key_grads.1.refs_4_.refs_1_.grad_k, ...), custom_call_target="tpu_custom_call" | custom-call | flops 452984832 | bytes 786432 | tf_op jit(solution)/shard_map/input_grads/pallas_call | solution.py:298
  290.4 2.6 project_reshare.1
  293.0 1.9 collective-permute-start.23
  294.9 27.7 %collective-permute-done.23.refs_2_ = bf16[2,256,768]{2,1,0:T(8,128)(2,1)S(1)} collective-permute-done((bf16[2,256,768]{2,1,0:T(8,128)(2,1)}, bf16[2,256,768]{2,1,0:T(8,128)(2,1)S(1)}, u32[]{:S(2)}, u32[]{:S(2)}) %collective-permute-start.23) | collective-permute-done | bytes 786464 | tf_op jit(solution)/shard_map/ppermute | solution.py:884
  322.6 0.9 copy-done
  323.5 0.8 slice_bitcast_fusion.1
  324.3 1.5 collective-permute-start.25
  325.8 2.4 collective-permute-start.26
  328.7 4.1 %collective-permute-done.25.refs_1_ = bf16[80,768]{1,0:T(8,128)(2,1)} collective-permute-done((bf16[80,768]{1,0:T(8,128)(2,1)}, bf16[80,768]{1,0:T(8,128)(2,1)}, u32[]{:S(2)}, u32[]{:S(2)}) %collective-permute-start.25) | collective-permute-done | bytes 122912 | tf_op jit(solution)/shard_map/ppermute | solution.py:884
  332.8 5.6 %collective-permute-done.26.refs_2_ = bf16[80,768]{1,0:T(8,128)(2,1)} collective-permute-done((bf16[80,768]{1,0:T(8,128)(2,1)}, bf16[80,768]{1,0:T(8,128)(2,1)}, u32[]{:S(2)}, u32[]{:S(2)}) %collective-permute-start.26) | collective-permute-done | bytes 122912 | tf_op jit(solution)/shard_map/ppermute | solution.py:884
  338.4 1.9 project_piece.1
  340.3 1.1 collective-permute-start.28
  341.4 3.5 collective-permute-start.29
  345.2 2.7 block_out.1.refs_4_
  347.9 5.5 %collective-permute-done.29.refs_2_ = bf16[1,3,24,768]{3,2,1,0:T(8,128)(2,1)} collective-permute-done((bf16[1,3,24,768]{3,2,1,0:T(8,128)(2,1)}, bf16[1,3,24,768]{3,2,1,0:T(8,128)(2,1)}, u32[]{:S(2)}, u32[]{:S(2)}) %collective-permute-start.29) | collective-permute-done | bytes 110624 | tf_op jit(solution)/shard_map/ppermute | solution.py:884
  353.5 1.6 collective-permute-done.30.refs_3_
  355.0 1.9 stack_line.1
  356.9 1.1 collective-permute-start.32
  358.0 1.4 collective-permute-start.34
  359.5 2.0 collective-permute-start.36
  361.5 16.7 %fill.1 = (f32[3072,768]{1,0:T(8,128)}, f32[768,3072]{1,0:T(8,128)}, f32[768,768]{1,0:T(8,128)}, f32[768]{0:T(1024)}) custom-call(bf16[32,9,24,768]{3,2,1,0:T(8,128)(2,1)} %bitcast.20, bf16[768,3072]{1,0:T(8,128)(2,1)} %w_hidden.1, f32[1,768]{1,0:T(1,128)} %reshape.39.refs_7_.gain, bf16[4,3,24,768]{3,2,1,0:T(8,128)(2,1)} %get-tuple-element.181.refs_0_), custom_call_target="tpu_custom_call" | custom-call | tf_op jit(solution)/shard_map/fill/pallas_call | solution.py:866
  378.2 1.5 collective-permute-done.36.refs_3_
  379.8 2.8 stack_plane.1.refs_4_.own
  383.1 1.0 slice_bitcast_fusion
  384.8 2.4 collective-permute-done.31.refs_1_
  388.0 0.7 copy-done.2
  388.7 2.7 grad_inputs.1.refs_0_
  391.4 8.4 %spread.1 = (f32[768,768]{1,0:T(8,128)}, f32[768,768]{1,0:T(8,128)}, f32[768,768]{1,0:T(8,128)}, f32[768]{0:T(1024)}) custom-call(s32[3]{0:T(128)} %pad_add_fusion.1.place, bf16[16,3,24,768]{3,2,1,0:T(8,128)(2,1)} %stack_plane.1.refs_4_.own, bf16[16,3,24,768]{3,2,1,0:T(8,128)(2,1)} %collective-permute-done.37.other, bf16[768,768]{1,0:T(8,128)(2,1)} %w_query.3, ...), custom_call_target="tpu_custom_call" | custom-call | bytes 786432 | tf_op jit(solution)/shard_map/spread/pallas_call | solution.py:298
  (70 shorter events, 7.4 us)
Async XLA Ops:
  7.2 6.3 %copy-start.5 = (f32[768]{0:T(1024)S(1)}, f32[768]{0:T(1024)}, u32[]{:S(2)}) copy-start(f32[768]{0:T(1024)} %param.15) | copy-start | bytes 9220
  7.2 6.8 %copy-start.3 = (bf16[12,12]{1,0:T(8,128)(2,1)S(1)}, bf16[12,12]{1,0:T(8,128)(2,1)}, u32[]{:S(2)}) copy-start(bf16[12,12]{1,0:T(8,128)(2,1)} %param.21) | copy-start | bytes 868
  7.2 8.4 %copy-start.6 = (f32[768]{0:T(1024)S(1)}, f32[768]{0:T(1024)}, u32[]{:S(2)}) copy-start(f32[768]{0:T(1024)} %param.22) | copy-start | bytes 9220
  7.2 9.0 %copy-start.4 = (bf16[12,12]{1,0:T(8,128)(2,1)S(1)}, bf16[12,12]{1,0:T(8,128)(2,1)}, u32[]{:S(2)}) copy-start(bf16[12,12]{1,0:T(8,128)(2,1)} %param.20) | copy-start | bytes 868
  9.6 7.2 %collective-permute-start.2 = (bf16[256,768]{1,0:T(8,128)(2,1)S(1)}, bf16[256,768]{1,0:T(8,128)(2,1)}, u32[]{:S(2)}, u32[]{:S(2)}) collective-permute-start(bf16[256,768]{1,0:T(8,128)(2,1)S(1)} %get-tuple-element.192), channel_id=1, source_target_pairs={{0,1},{1,0},{2,3},{3,2},{4,5},{5,4},{6,7},{7,6},{8,9},{9,8},{10,11... | collective-permute-start | bytes 1179656 | tf_op jit(solution)/shard_map/ppermute | solution.py:884
  10.1 17.9 %collective-permute-start = (bf16[256,768]{1,0:T(8,128)(2,1)}, bf16[256,768]{1,0:T(8,128)(2,1)}, u32[]{:S(2)}, u32[]{:S(2)}) collective-permute-start(bf16[256,768]{1,0:T(8,128)(2,1)} %get-tuple-element.194), channel_id=1, source_target_pairs={{0,2},{1,3},{2,0},{3,1},{4,6},{5,7},{6,4},{7,5},{8,10},{9,11},{10,... | collective-permute-start | bytes 1179656 | tf_op jit(solution)/shard_map/ppermute | solution.py:884
  12.6 18.3 %collective-permute-start.1 = (bf16[256,768]{1,0:T(8,128)(2,1)}, bf16[256,768]{1,0:T(8,128)(2,1)}, u32[]{:S(2)}, u32[]{:S(2)}) collective-permute-start(bf16[256,768]{1,0:T(8,128)(2,1)} %get-tuple-element.193), channel_id=1, source_target_pairs={{0,3},{1,2},{2,1},{3,0},{4,7},{5,6},{6,5},{7,4},{8,11},{9,10},{10,... | collective-permute-start | bytes 1179656 | tf_op jit(solution)/shard_map/ppermute | solution.py:884
  24.6 53.4 %collective-permute-start.3 = (bf16[256,768]{1,0:T(8,128)(2,1)}, bf16[256,768]{1,0:T(8,128)(2,1)}, u32[]{:S(2)}, u32[]{:S(2)}) collective-permute-start(bf16[256,768]{1,0:T(8,128)(2,1)} %get-tuple-element.116), channel_id=1, source_target_pairs={{0,1},{1,0},{2,3},{3,2},{4,5},{5,4},{6,7},{7,6},{8,9},{9,8},{10,11... | collective-permute-start | bytes 1179656 | tf_op jit(solution)/shard_map/ppermute | solution.py:884
  24.8 53.3 %collective-permute-start.4 = (bf16[256,768]{1,0:T(8,128)(2,1)}, bf16[256,768]{1,0:T(8,128)(2,1)}, u32[]{:S(2)}, u32[]{:S(2)}) collective-permute-start(bf16[256,768]{1,0:T(8,128)(2,1)} %get-tuple-element.117), channel_id=1, source_target_pairs={{0,2},{1,3},{2,0},{3,1},{4,6},{5,7},{6,4},{7,5},{8,10},{9,11},{10,... | collective-permute-start | bytes 1179656 | tf_op jit(solution)/shard_map/ppermute | solution.py:884
  26.7 51.4 %collective-permute-start.5 = (bf16[256,768]{1,0:T(8,128)(2,1)}, bf16[256,768]{1,0:T(8,128)(2,1)}, u32[]{:S(2)}, u32[]{:S(2)}) collective-permute-start(bf16[256,768]{1,0:T(8,128)(2,1)} %get-tuple-element.118), channel_id=1, source_target_pairs={{0,3},{1,2},{2,1},{3,0},{4,7},{5,6},{6,5},{7,4},{8,11},{9,10},{10,... | collective-permute-start | bytes 1179656 | tf_op jit(solution)/shard_map/ppermute | solution.py:884
  128.2 12.5 %collective-permute-start.7 = (bf16[6,384,768]{2,1,0:T(8,128)(2,1)}, bf16[6,384,768]{2,1,0:T(8,128)(2,1)}, u32[]{:S(2)}, u32[]{:S(2)}) collective-permute-start(bf16[6,384,768]{2,1,0:T(8,128)(2,1)} %get-tuple-element.131), channel_id=1, source_target_pairs={{0,1},{1,0},{2,3},{3,2},{4,5},{5,4},{6,7},{7,6},{8,9},{9,8},{10,11... | collective-permute-start | bytes 10616840 | tf_op jit(solution)/shard_map/ppermute | solution.py:884
  136.7 4.0 collective-permute-start.8
  149.0 49.5 %all-to-all-start = ((bf16[4,6,96,768]{3,2,1,0:T(8,128)(2,1)}), bf16[4,6,96,768]{3,2,1,0:T(8,128)(2,1)}, u32[]{:S(2)}, u32[]{:S(2)}) async-start(bf16[4,6,96,768]{3,2,1,0:T(8,128)(2,1)} %get-tuple-element.135.rest_0_), calls=%async_computation | async-start | bytes 7077888 | tf_op jit(solution)/shard_map/all_to_all | solution.py:939
  153.7 44.7 %collective-permute-start.9 = (bf16[3,96,768]{2,1,0:T(8,128)(2,1)}, bf16[3,96,768]{2,1,0:T(8,128)(2,1)}, u32[]{:S(2)}, u32[]{:S(2)}) collective-permute-start(bf16[3,96,768]{2,1,0:T(8,128)(2,1)} %get-tuple-element.140), channel_id=1, source_target_pairs={{0,8},{1,9},{2,10},{3,11},{4,12},{5,13},{6,14},{7,15},{8,0},{9,1},... | collective-permute-start | bytes 1327112 | tf_op jit(solution)/shard_map/ppermute | solution.py:884
  155.8 42.6 %collective-permute-start.10 = (bf16[3,96,768]{2,1,0:T(8,128)(2,1)}, bf16[3,96,768]{2,1,0:T(8,128)(2,1)}, u32[]{:S(2)}, u32[]{:S(2)}) collective-permute-start(bf16[3,96,768]{2,1,0:T(8,128)(2,1)} %get-tuple-element.141), channel_id=1, source_target_pairs={{0,16},{1,17},{2,18},{3,19},{4,20},{5,21},{6,22},{7,23},{8,24},{9,... | collective-permute-start | bytes 1327112 | tf_op jit(solution)/shard_map/ppermute | solution.py:884
  158.4 40.1 %collective-permute-start.11 = (bf16[3,96,768]{2,1,0:T(8,128)(2,1)}, bf16[3,96,768]{2,1,0:T(8,128)(2,1)}, u32[]{:S(2)}, u32[]{:S(2)}) collective-permute-start(bf16[3,96,768]{2,1,0:T(8,128)(2,1)} %get-tuple-element.142), channel_id=1, source_target_pairs={{0,24},{1,25},{2,26},{3,27},{4,28},{5,29},{6,30},{7,31},{8,16},{9,... | collective-permute-start | bytes 1327112 | tf_op jit(solution)/shard_map/ppermute | solution.py:884
  203.0 26.4 %all-to-all-start.1 = ((bf16[4,3,24,768]{3,2,1,0:T(8,128)(2,1)}), bf16[4,3,24,768]{3,2,1,0:T(8,128)(2,1)}, u32[]{:S(2)}, u32[]{:S(2)}) async-start(bf16[4,3,24,768]{3,2,1,0:T(8,128)(2,1)} %get-tuple-element.144), calls=%async_computation.1 | async-start | bytes 884736 | tf_op jit(solution)/shard_map/all_to_all | solution.py:939
  207.1 154.4 %all-gather.3.cloned.1.call-start = ((), (), s32[]{:S(2)}) async-start(), calls=%async_computation.2 | async-start | bytes 10948608 | tf_op jit(solution)/shard_map/all_gather | solution.py:1002
  207.2 22.2 %collective-permute-start.12 = (bf16[6,24,768]{2,1,0:T(8,128)(2,1)}, bf16[6,24,768]{2,1,0:T(8,128)(2,1)}, u32[]{:S(2)}, u32[]{:S(2)}) collective-permute-start(bf16[6,24,768]{2,1,0:T(8,128)(2,1)} %get-tuple-element.145), channel_id=1, source_target_pairs={{0,8},{1,9},{2,10},{3,11},{4,12},{5,13},{6,14},{7,15},{8,0},{9,1},... | collective-permute-start | bytes 663560 | tf_op jit(solution)/shard_map/ppermute | solution.py:884
  208.1 21.3 %collective-permute-start.13 = (bf16[6,24,768]{2,1,0:T(8,128)(2,1)}, bf16[6,24,768]{2,1,0:T(8,128)(2,1)}, u32[]{:S(2)}, u32[]{:S(2)}) collective-permute-start(bf16[6,24,768]{2,1,0:T(8,128)(2,1)} %get-tuple-element.146), channel_id=1, source_target_pairs={{0,16},{1,17},{2,18},{3,19},{4,20},{5,21},{6,22},{7,23},{8,24},{9,... | collective-permute-start | bytes 663560 | tf_op jit(solution)/shard_map/ppermute | solution.py:884
  211.6 17.8 %collective-permute-start.14 = (bf16[6,24,768]{2,1,0:T(8,128)(2,1)}, bf16[6,24,768]{2,1,0:T(8,128)(2,1)}, u32[]{:S(2)}, u32[]{:S(2)}) collective-permute-start(bf16[6,24,768]{2,1,0:T(8,128)(2,1)} %get-tuple-element.147), channel_id=1, source_target_pairs={{0,24},{1,25},{2,26},{3,27},{4,28},{5,29},{6,30},{7,31},{8,16},{9,... | collective-permute-start | bytes 663560 | tf_op jit(solution)/shard_map/ppermute | solution.py:884
  237.9 3.2 collective-permute-start.15
  243.9 23.0 %collective-permute-start.16 = (bf16[2,96,768]{2,1,0:T(8,128)(2,1)}, bf16[2,96,768]{2,1,0:T(8,128)(2,1)}, u32[]{:S(2)}, u32[]{:S(2)}) collective-permute-start(bf16[2,96,768]{2,1,0:T(8,128)(2,1)} %get-tuple-element.151), channel_id=1, source_target_pairs={{0,2},{1,3},{2,0},{3,1},{4,6},{5,7},{6,4},{7,5},{8,10},{9,11},{10,... | collective-permute-start | bytes 884744 | tf_op jit(solution)/shard_map/ppermute | solution.py:884
  245.8 21.1 %collective-permute-start.17 = (bf16[2,96,768]{2,1,0:T(8,128)(2,1)}, bf16[2,96,768]{2,1,0:T(8,128)(2,1)}, u32[]{:S(2)}, u32[]{:S(2)}) collective-permute-start(bf16[2,96,768]{2,1,0:T(8,128)(2,1)} %get-tuple-element.152), channel_id=1, source_target_pairs={{0,4},{1,5},{2,6},{3,7},{4,0},{5,1},{6,2},{7,3},{8,12},{9,13},{10,... | collective-permute-start | bytes 884744 | tf_op jit(solution)/shard_map/ppermute | solution.py:884
  247.2 19.6 %collective-permute-start.18 = (bf16[2,96,768]{2,1,0:T(8,128)(2,1)}, bf16[2,96,768]{2,1,0:T(8,128)(2,1)}, u32[]{:S(2)}, u32[]{:S(2)}) collective-permute-start(bf16[2,96,768]{2,1,0:T(8,128)(2,1)} %get-tuple-element.153), channel_id=1, source_target_pairs={{0,6},{1,7},{2,4},{3,5},{4,2},{5,3},{6,0},{7,1},{8,14},{9,15},{10,... | collective-permute-start | bytes 884744 | tf_op jit(solution)/shard_map/ppermute | solution.py:884
  271.3 2.4 collective-permute-start.19
  276.0 14.3 %collective-permute-start.20 = (bf16[104,768]{1,0:T(8,128)(2,1)}, bf16[104,768]{1,0:T(8,128)(2,1)}, u32[]{:S(2)}, u32[]{:S(2)}) collective-permute-start(bf16[104,768]{1,0:T(8,128)(2,1)} %get-tuple-element.161), channel_id=1, source_target_pairs={{0,2},{1,3},{2,0},{3,1},{4,6},{5,7},{6,4},{7,5},{8,10},{9,11},{10,... | collective-permute-start | bytes 479240 | tf_op jit(solution)/shard_map/ppermute | solution.py:884
  277.9 12.5 %collective-permute-start.21 = (bf16[104,768]{1,0:T(8,128)(2,1)}, bf16[104,768]{1,0:T(8,128)(2,1)}, u32[]{:S(2)}, u32[]{:S(2)}) collective-permute-start(bf16[104,768]{1,0:T(8,128)(2,1)} %get-tuple-element.162), channel_id=1, source_target_pairs={{0,4},{1,5},{2,6},{3,7},{4,0},{5,1},{6,2},{7,3},{8,12},{9,13},{10,... | collective-permute-start | bytes 479240 | tf_op jit(solution)/shard_map/ppermute | solution.py:884
  279.4 11.0 %collective-permute-start.22 = (bf16[104,768]{1,0:T(8,128)(2,1)}, bf16[104,768]{1,0:T(8,128)(2,1)}, u32[]{:S(2)}, u32[]{:S(2)}) collective-permute-start(bf16[104,768]{1,0:T(8,128)(2,1)} %get-tuple-element.163), channel_id=1, source_target_pairs={{0,6},{1,7},{2,4},{3,5},{4,2},{5,3},{6,0},{7,1},{8,14},{9,15},{10,... | collective-permute-start | bytes 479240 | tf_op jit(solution)/shard_map/ppermute | solution.py:884
  293.0 29.6 %collective-permute-start.23 = (bf16[2,256,768]{2,1,0:T(8,128)(2,1)}, bf16[2,256,768]{2,1,0:T(8,128)(2,1)S(1)}, u32[]{:S(2)}, u32[]{:S(2)}) collective-permute-start(bf16[2,256,768]{2,1,0:T(8,128)(2,1)} %get-tuple-element.169), channel_id=1, source_target_pairs={{0,2},{1,3},{2,0},{3,1},{4,6},{5,7},{6,4},{7,5},{8,10},{9,11},{10,... | collective-permute-start | bytes 2359304 | tf_op jit(solution)/shard_map/ppermute | solution.py:884
  294.9 50.3 %collective-permute-start.6 = (bf16[256,768]{1,0:T(8,128)(2,1)}, bf16[256,768]{1,0:T(8,128)(2,1)}, u32[]{:S(2)}, u32[]{:S(2)}) collective-permute-start(bf16[256,768]{1,0:T(8,128)(2,1)} %get-tuple-element.120), channel_id=1, source_target_pairs={{0,1},{1,0},{2,3},{3,2},{4,5},{5,4},{6,7},{7,6},{8,9},{9,8},{10,11... | collective-permute-start | bytes 1179656 | tf_op jit(solution)/shard_map/ppermute | solution.py:884
  322.6 0.9 copy-start
  324.3 21.0 %collective-permute-start.24 = (bf16[256,768]{1,0:T(8,128)(2,1)}, bf16[256,768]{1,0:T(8,128)(2,1)}, u32[]{:S(2)}, u32[]{:S(2)}) collective-permute-start(bf16[256,768]{1,0:T(8,128)(2,1)} %slice_bitcast_fusion.1), channel_id=1, source_target_pairs={{0,1},{1,0},{2,3},{3,2},{4,5},{5,4},{6,7},{7,6},{8,9},{9,8},{10,11... | collective-permute-start | bytes 1179656 | tf_op jit(solution)/shard_map/ppermute | solution.py:884
  324.3 8.5 %collective-permute-start.25 = (bf16[80,768]{1,0:T(8,128)(2,1)}, bf16[80,768]{1,0:T(8,128)(2,1)}, u32[]{:S(2)}, u32[]{:S(2)}) collective-permute-start(bf16[80,768]{1,0:T(8,128)(2,1)} %get-tuple-element.171), channel_id=1, source_target_pairs={{0,8},{1,9},{2,10},{3,11},{4,12},{5,13},{6,14},{7,15},{8,0},{9,1},... | collective-permute-start | bytes 368648 | tf_op jit(solution)/shard_map/ppermute | solution.py:884
  325.8 12.7 %collective-permute-start.26 = (bf16[80,768]{1,0:T(8,128)(2,1)}, bf16[80,768]{1,0:T(8,128)(2,1)}, u32[]{:S(2)}, u32[]{:S(2)}) collective-permute-start(bf16[80,768]{1,0:T(8,128)(2,1)} %get-tuple-element.172), channel_id=1, source_target_pairs={{0,16},{1,17},{2,18},{3,19},{4,20},{5,21},{6,22},{7,23},{8,24},{9,... | collective-permute-start | bytes 368648 | tf_op jit(solution)/shard_map/ppermute | solution.py:884
  328.2 10.3 %collective-permute-start.27 = (bf16[80,768]{1,0:T(8,128)(2,1)}, bf16[80,768]{1,0:T(8,128)(2,1)}, u32[]{:S(2)}, u32[]{:S(2)}) collective-permute-start(bf16[80,768]{1,0:T(8,128)(2,1)} %get-tuple-element.173), channel_id=1, source_target_pairs={{0,24},{1,25},{2,26},{3,27},{4,28},{5,29},{6,30},{7,31},{8,16},{9,... | collective-permute-start | bytes 368648 | tf_op jit(solution)/shard_map/ppermute | solution.py:884
  340.3 7.6 %collective-permute-start.28 = (bf16[1,3,24,768]{3,2,1,0:T(8,128)(2,1)}, bf16[1,3,24,768]{3,2,1,0:T(8,128)(2,1)}, u32[]{:S(2)}, u32[]{:S(2)}) collective-permute-start(bf16[1,3,24,768]{3,2,1,0:T(8,128)(2,1)} %bitcast.21), channel_id=1, source_target_pairs={{0,2},{1,3},{2,0},{3,1},{4,6},{5,7},{6,4},{7,5},{8,10},{9,11},{10,... | collective-permute-start | bytes 331784 | tf_op jit(solution)/shard_map/ppermute | solution.py:884
  341.4 12.0 %collective-permute-start.29 = (bf16[1,3,24,768]{3,2,1,0:T(8,128)(2,1)}, bf16[1,3,24,768]{3,2,1,0:T(8,128)(2,1)}, u32[]{:S(2)}, u32[]{:S(2)}) collective-permute-start(bf16[1,3,24,768]{3,2,1,0:T(8,128)(2,1)} %bitcast.22), channel_id=1, source_target_pairs={{0,16},{1,17},{2,18},{3,19},{4,20},{5,21},{6,22},{7,23},{8,24},{9,... | collective-permute-start | bytes 331784 | tf_op jit(solution)/shard_map/ppermute | solution.py:884
  344.9 10.1 %collective-permute-start.30 = (bf16[1,3,24,768]{3,2,1,0:T(8,128)(2,1)}, bf16[1,3,24,768]{3,2,1,0:T(8,128)(2,1)}, u32[]{:S(2)}, u32[]{:S(2)}) collective-permute-start(bf16[1,3,24,768]{3,2,1,0:T(8,128)(2,1)} %bitcast.23), channel_id=1, source_target_pairs={{0,18},{1,19},{2,16},{3,17},{4,22},{5,23},{6,20},{7,21},{8,26},{9,... | collective-permute-start | bytes 331784 | tf_op jit(solution)/shard_map/ppermute | solution.py:884
  356.9 22.9 %collective-permute-start.32 = (bf16[2,256,768]{2,1,0:T(8,128)(2,1)}, bf16[2,256,768]{2,1,0:T(8,128)(2,1)}, u32[]{:S(2)}, u32[]{:S(2)}) collective-permute-start(bf16[2,256,768]{2,1,0:T(8,128)(2,1)} %get-tuple-element.180), channel_id=1, source_target_pairs={{0,2},{1,3},{2,0},{3,1},{4,6},{5,7},{6,4},{7,5},{8,10},{9,11},{10,... | collective-permute-start | bytes 2359304 | tf_op jit(solution)/shard_map/ppermute | solution.py:884
  358.0 20.2 %collective-permute-start.34 = (bf16[4,3,24,768]{3,2,1,0:T(8,128)(2,1)}, bf16[4,3,24,768]{3,2,1,0:T(8,128)(2,1)}, u32[]{:S(2)}, u32[]{:S(2)}) collective-permute-start(bf16[4,3,24,768]{3,2,1,0:T(8,128)(2,1)} %get-tuple-element.181.refs_0_), channel_id=1, source_target_pairs={{0,4},{1,5},{2,6},{3,7},{4,0},{5,1},{6,2},{7,3},{8,12},{9,13},{10,... | collective-permute-start | bytes 1327112 | tf_op jit(solution)/shard_map/ppermute | solution.py:884
  359.5 18.8 %collective-permute-start.35 = (bf16[4,3,24,768]{3,2,1,0:T(8,128)(2,1)}, bf16[4,3,24,768]{3,2,1,0:T(8,128)(2,1)}, u32[]{:S(2)}, u32[]{:S(2)}) collective-permute-start(bf16[4,3,24,768]{3,2,1,0:T(8,128)(2,1)} %get-tuple-element.181.refs_0_), channel_id=1, source_target_pairs={{0,8},{1,9},{2,10},{3,11},{4,12},{5,13},{6,14},{7,15},{8,0},{9,1},... | collective-permute-start | bytes 1327112 | tf_op jit(solution)/shard_map/ppermute | solution.py:884
  359.5 20.3 %collective-permute-start.36 = (bf16[4,3,24,768]{3,2,1,0:T(8,128)(2,1)}, bf16[4,3,24,768]{3,2,1,0:T(8,128)(2,1)}, u32[]{:S(2)}, u32[]{:S(2)}) collective-permute-start(bf16[4,3,24,768]{3,2,1,0:T(8,128)(2,1)} %get-tuple-element.181.refs_0_), channel_id=1, source_target_pairs={{0,12},{1,13},{2,14},{3,15},{4,8},{5,9},{6,10},{7,11},{8,4},{9,5},... | collective-permute-start | bytes 1327112 | tf_op jit(solution)/shard_map/ppermute | solution.py:884
  382.6 8.9 %collective-permute-start.37 = (bf16[16,3,24,768]{3,2,1,0:T(8,128)(2,1)}, bf16[16,3,24,768]{3,2,1,0:T(8,128)(2,1)}, u32[]{:S(2)}, u32[]{:S(2)}) collective-permute-start(bf16[16,3,24,768]{3,2,1,0:T(8,128)(2,1)} %stack_plane.1.refs_4_.own), channel_id=1, source_target_pairs={{0,1},{1,0},{2,3},{3,2},{4,5},{5,4},{6,7},{7,6},{8,9},{9,8},{10,11... | collective-permute-start | bytes 5308424 | tf_op jit(solution)/shard_map/ppermute | solution.py:884
  382.6 4.7 %collective-permute-start.31 = (bf16[256,768]{1,0:T(8,128)(2,1)}, bf16[256,768]{1,0:T(8,128)(2,1)S(1)}, u32[]{:S(2)}, u32[]{:S(2)}) collective-permute-start(bf16[256,768]{1,0:T(8,128)(2,1)} %get-tuple-element.179), channel_id=1, source_target_pairs={{0,1},{1,0},{2,3},{3,2},{4,5},{5,4},{6,7},{7,6},{8,9},{9,8},{10,11... | collective-permute-start | bytes 1179656 | tf_op jit(solution)/shard_map/ppermute | solution.py:884
  384.1 3.3 collective-permute-start.33
  387.2 0.7 copy-start.1
  388.0 0.7 copy-start.2
Sparse Core Ops, SparseCore 0:
  231.8 98.4 all-gather.2
